TPU v7x, 512 devices: a whole 4x4x16 slice. The times are simulated.
512 devices in a mesh: station: 512 (over z, y, x, core).
Axes of the slice: x: 4, y: 4, z: 16, core: 2. Of those that a mesh axis runs over, the one named last changes fastest.
Arguments:
- right_side: float32 [512, 512, 128], P('station'), may hold values from -6 to 6
- diag_blocks: float32 [512, 512, 512], P('station'), may hold values from -1 to 7
- lower_blocks: float32 [512, 512, 512], P('station'), may hold values from -0.15625 to 0.15625
- upper_blocks: float32 [512, 512, 512], P('station'), may hold values from -0.15625 to 0.15625
- approx_inverse: float32 [512, 512, 512], P('station'), may hold values from -1 to 1
Outputs:
- solution: float32 [512, 512, 128], P('station')
- residual: float32 [512, 512, 128], P('station')
All inputs are finite; a program needn't handle non-finite values.
Results may differ from a plain program's by a relative error of at most 0.0003.
Values sent between devices are 32-bit elements; how exact they have to be, the bound alone decides.
No kernel may reach another device: no remote copies, remote signals or barrier semaphores. Data moves between devices by JAX's collectives and lax.ppermute only.
A program may use at most 64 MiB of HBM per device.

v0:
```python
import jax
import jax.numpy as jnp
from jax import lax
from jax.sharding import PartitionSpec as P

ITERS = 2


def passed_along(value, axis, steps):
    count = lax.axis_size(axis)
    pairs = [(source, (source + steps) % count) for source in range(count)]
    return lax.ppermute(value, axis, pairs)


def padded(x, sides, width):
    for axis, dim in sides:
        size, length = (lax.axis_size(axis), x.shape[dim])
        up = [(i, (i + 1) % size) for i in range(size)]
        down = [(j, i) for i, j in up]
        last = lax.slice_in_dim(x, length - width, length, axis=dim)
        leading = lax.slice_in_dim(x, 0, width, axis=dim)
        before = lax.ppermute(last, axis, up)
        after = lax.ppermute(leading, axis, down)
        x = jnp.concatenate([before, x, after], axis=dim)
    return x


def product(matrix, vector):
    return jnp.einsum("sij,sjk->sik", matrix, vector, precision=lax.Precision.HIGHEST)


def local(right_side, diag_blocks, lower_blocks, upper_blocks, approx_inverse):
    solution = jnp.zeros_like(right_side)
    residual = right_side
    left_inverse, left_lower = passed_along((approx_inverse, lower_blocks), "station", 1)
    right_inverse, right_upper = passed_along((approx_inverse, upper_blocks), "station", -1)
    for iteration in range(ITERS):
        first_pass = product(approx_inverse, residual)
        nearby = padded(first_pass, (("station", 0),), 1)
        reduced = residual - product(lower_blocks, nearby[0:1]) - product(upper_blocks, nearby[2:3])
        second_pass = product(approx_inverse, reduced)
        far_left = passed_along(second_pass, "station", 2)
        far_right = passed_along(second_pass, "station", -2)
        left_before = product(left_inverse, product(left_lower, far_left))
        right_after = product(right_inverse, product(right_upper, far_right))
        twice_reduced = (
            reduced + product(lower_blocks, left_before) + product(upper_blocks, right_after)
        )
        solution = solution + product(approx_inverse, twice_reduced)
        neighbours = padded(solution, (("station", 0),), 1)
        residual = (
            right_side
            - product(lower_blocks, neighbours[0:1])
            - product(diag_blocks, solution)
            - product(upper_blocks, neighbours[2:3])
        )
    return (solution, residual)


def solution(mesh):
    in_specs = (
        P("station", None, None),
        P("station", None, None),
        P("station", None, None),
        P("station", None, None),
        P("station", None, None),
    )
    out_specs = (P("station", None, None), P("station", None, None))
    return jax.shard_map(local, mesh=mesh, in_specs=in_specs, out_specs=out_specs, check_vma=False)
```

profile of v0, /device:TPU:0, one launch (start us, length us, event | category | flops | bytes accessed | tf_op | source)
XLA Modules:
  0.0 151.5 jit_solution(3750793110571762520)
XLA Ops:
  0.7 3.1 %convolution_bitcast_fusion.18 = f32[1,512,128]{2,1,0:T(8,128)} fusion(f32[1,512,512]{2,1,0:T(8,128)} %param.9, f32[1,512,128]{2,1,0:T(8,128)} %param.5), kind=kOutput, calls=%fused_computation.18 | convolution fusion | flops 402653184 | bytes 1572864 | tf_op jit(solution)/shard_map/sij,sjk->sik/dot_general | solution.py:29
  3.8 10.1 %collective-permute-start.1 = (f32[1,512,128]{2,1,0:T(8,128)}, f32[1,512,128]{2,1,0:T(8,128)}, u32[]{:S(2)}, u32[]{:S(2)}) collective-permute-start(f32[1,512,128]{2,1,0:T(8,128)} %convolution_bitcast_fusion.18), channel_id=1, source_target_pairs={{1,0},{2,1},{3,2},{4,3},{5,4},{6,5},{7,6},{8,7},{9,8},{10,9},{11,1... | collective-permute-start | bytes 786440 | tf_op jit(solution)/shard_map/ppermute | solution.py:23
  13.9 2.6 %collective-permute-start.6 = (f32[1,512,512]{2,1,0:T(8,128)}, f32[1,512,512]{2,1,0:T(8,128)}, u32[]{:S(2)}, u32[]{:S(2)}) collective-permute-start(f32[1,512,512]{2,1,0:T(8,128)} %param.8), channel_id=1, source_target_pairs={{0,511},{1,0},{2,1},{3,2},{4,3},{5,4},{6,5},{7,6},{8,7},{9,8},{10,... | collective-permute-start | bytes 3145736 | tf_op jit(solution)/shard_map/ppermute | solution.py:12
  16.5 1.9 %collective-permute-start = (f32[1,512,128]{2,1,0:T(8,128)}, f32[1,512,128]{2,1,0:T(8,128)}, u32[]{:S(2)}, u32[]{:S(2)}) collective-permute-start(f32[1,512,128]{2,1,0:T(8,128)} %convolution_bitcast_fusion.18), channel_id=1, source_target_pairs={{0,1},{1,2},{2,3},{3,4},{4,5},{5,6},{6,7},{7,8},{8,9},{9,10},{10,1... | collective-permute-start | bytes 786440 | tf_op jit(solution)/shard_map/ppermute | solution.py:22
  18.4 9.1 %collective-permute-start.7 = (f32[1,512,512]{2,1,0:T(8,128)S(1)}, f32[1,512,512]{2,1,0:T(8,128)}, u32[]{:S(2)}, u32[]{:S(2)}) collective-permute-start(f32[1,512,512]{2,1,0:T(8,128)S(1)} %copy-done.1), channel_id=1, source_target_pairs={{0,511},{1,0},{2,1},{3,2},{4,3},{5,4},{6,5},{7,6},{8,7},{9,8},{10,... | collective-permute-start | bytes 3145736 | tf_op jit(solution)/shard_map/ppermute | solution.py:12
  27.5 1.9 %collective-permute-start.3 = (f32[1,512,512]{2,1,0:T(8,128)}, f32[1,512,512]{2,1,0:T(8,128)}, u32[]{:S(2)}, u32[]{:S(2)}) collective-permute-start(f32[1,512,512]{2,1,0:T(8,128)} %param.7), channel_id=1, source_target_pairs={{0,1},{1,2},{2,3},{3,4},{4,5},{5,6},{6,7},{7,8},{8,9},{9,10},{10,1... | collective-permute-start | bytes 3145736 | tf_op jit(solution)/shard_map/ppermute | solution.py:12
  30.6 2.3 %convolution_bitcast_fusion.16 = f32[1,512,128]{1,2,0:T(8,128)S(1)} fusion(f32[1,512,512]{2,1,0:T(8,128)S(1)} %copy-done.2, f32[1,512,128]{2,1,0:T(8,128)} %collective-permute-done.1), kind=kOutput, calls=%fused_computation.16 | convolution fusion | flops 402653184 | bytes 1572864 | tf_op jit(solution)/shard_map/sij,sjk->sik/dot_general | solution.py:29
  32.9 2.2 %fusion.2 = f32[1,512,128]{1,2,0:T(8,128)S(1)} fusion(f32[1,512,128]{1,2,0:T(8,128)S(1)} %convolution_bitcast_fusion.16, f32[1,512,128]{1,2,0:T(8,128)S(1)} %copy.7, f32[1,512,512]{2,1,0:T(8,128)S(1)} %copy-done.3, f32[1,512,128]{2,1,0:T(8,128)} %collective-permute-done), kind=kOutput, calls=%fused_computation.21 | convolution fusion | flops 402784256 | bytes 2097152 | tf_op jit(solution)/shard_map/sij,sjk->sik/dot_general | solution.py:29
  35.1 1.2 convolution_bitcast_fusion.15
  36.3 2.3 %collective-permute-start.5 = (f32[1,512,128]{1,2,0:T(8,128)S(1)}, f32[1,512,128]{1,2,0:T(8,128)S(1)}, u32[]{:S(2)}, u32[]{:S(2)}) collective-permute-start(f32[1,512,128]{1,2,0:T(8,128)S(1)} %convolution_bitcast_fusion.15), channel_id=1, source_target_pairs={{0,510},{1,511},{2,0},{3,1},{4,2},{5,3},{6,4},{7,5},{8,6},{9,7},{1... | collective-permute-start | bytes 786440 | tf_op jit(solution)/shard_map/ppermute | solution.py:12
  38.6 8.8 %collective-permute-start.4 = (f32[1,512,512]{2,1,0:T(8,128)S(1)}, f32[1,512,512]{2,1,0:T(8,128)S(1)}, u32[]{:S(2)}, u32[]{:S(2)}) collective-permute-start(f32[1,512,512]{2,1,0:T(8,128)S(1)} %copy-done.1), channel_id=1, source_target_pairs={{0,1},{1,2},{2,3},{3,4},{4,5},{5,6},{6,7},{7,8},{8,9},{9,10},{10,1... | collective-permute-start | bytes 3145736 | tf_op jit(solution)/shard_map/ppermute | solution.py:12
  47.4 1.9 %collective-permute-start.2 = (f32[1,512,128]{1,2,0:T(8,128)S(1)}, f32[1,512,128]{1,2,0:T(8,128)S(1)}, u32[]{:S(2)}, u32[]{:S(2)}) collective-permute-start(f32[1,512,128]{1,2,0:T(8,128)S(1)} %convolution_bitcast_fusion.15), channel_id=1, source_target_pairs={{0,2},{1,3},{2,4},{3,5},{4,6},{5,7},{6,8},{7,9},{8,10},{9,11},{10,... | collective-permute-start | bytes 786440 | tf_op jit(solution)/shard_map/ppermute | solution.py:12
  49.3 2.4 %fusion.25 = f32[128,512]{1,0:T(8,128)S(1)} fusion(f32[1,512,512]{2,1,0:T(8,128)} %collective-permute-done.6, f32[1,512,128]{1,2,0:T(8,128)S(1)} %collective-permute-done.5), kind=kOutput, calls=%fused_computation.44 | convolution fusion | flops 402653184 | bytes 1572864 | tf_op jit(solution)/shard_map/sij,sjk->sik/dot_general | solution.py:29
  51.7 2.4 %fusion.21 = f32[128,512]{1,0:T(8,128)S(1)} fusion(f32[128,512]{1,0:T(8,128)S(1)} %fusion.25, f32[1,512,512]{2,1,0:T(8,128)} %collective-permute-done.7), kind=kOutput, calls=%fused_computation.40 | convolution fusion | flops 402653184 | bytes 1572864 | tf_op jit(solution)/shard_map/sij,sjk->sik/dot_general | solution.py:29
  54.1 1.2 convolution_bitcast_fusion.13
  55.3 8.6 %collective-permute-done.2 = f32[1,512,128]{1,2,0:T(8,128)S(1)} collective-permute-done((f32[1,512,128]{1,2,0:T(8,128)S(1)}, f32[1,512,128]{1,2,0:T(8,128)S(1)}, u32[]{:S(2)}, u32[]{:S(2)}) %collective-permute-start.2) | collective-permute-done | bytes 262176 | tf_op jit(solution)/shard_map/ppermute | solution.py:12
  63.9 2.4 %fusion.33 = f32[128,512]{1,0:T(8,128)S(1)} fusion(f32[1,512,512]{2,1,0:T(8,128)} %collective-permute-done.3, f32[1,512,128]{1,2,0:T(8,128)S(1)} %collective-permute-done.2), kind=kOutput, calls=%fused_computation.52 | convolution fusion | flops 402653184 | bytes 1572864 | tf_op jit(solution)/shard_map/sij,sjk->sik/dot_general | solution.py:29
  66.4 1.2 fusion.29
  67.5 1.2 fusion.5
  68.7 1.2 fusion.50
  69.9 3.3 %collective-permute-start.9 = (f32[1,512,128]{1,2,0:T(8,128)S(1)}, f32[1,512,128]{1,2,0:T(8,128)S(1)}, u32[]{:S(2)}, u32[]{:S(2)}) collective-permute-start(f32[1,512,128]{1,2,0:T(8,128)S(1)} %bitcast.239), channel_id=1, source_target_pairs={{1,0},{2,1},{3,2},{4,3},{5,4},{6,5},{7,6},{8,7},{9,8},{10,9},{11,1... | collective-permute-start | bytes 786440 | tf_op jit(solution)/shard_map/ppermute | solution.py:23
  73.3 2.7 %collective-permute-start.8 = (f32[1,512,128]{1,2,0:T(8,128)S(1)}, f32[1,512,128]{1,2,0:T(8,128)S(1)}, u32[]{:S(2)}, u32[]{:S(2)}) collective-permute-start(f32[1,512,128]{1,2,0:T(8,128)S(1)} %bitcast.240), channel_id=1, source_target_pairs={{0,1},{1,2},{2,3},{3,4},{4,5},{5,6},{6,7},{7,8},{8,9},{9,10},{10,1... | collective-permute-start | bytes 786440 | tf_op jit(solution)/shard_map/ppermute | solution.py:22
  78.3 8.1 %collective-permute-done.8 = f32[1,512,128]{1,2,0:T(8,128)S(1)} collective-permute-done((f32[1,512,128]{1,2,0:T(8,128)S(1)}, f32[1,512,128]{1,2,0:T(8,128)S(1)}, u32[]{:S(2)}, u32[]{:S(2)}) %collective-permute-start.8) | collective-permute-done | bytes 262176 | tf_op jit(solution)/shard_map/ppermute | solution.py:22
  86.4 1.2 fusion.8
  88.8 1.9 %collective-permute-start.11 = (f32[1,512,128]{1,2,0:T(8,128)S(1)}, f32[1,512,128]{1,2,0:T(8,128)S(1)}, u32[]{:S(2)}, u32[]{:S(2)}) collective-permute-start(f32[1,512,128]{1,2,0:T(8,128)S(1)} %convolution_bitcast_fusion.9), channel_id=1, source_target_pairs={{1,0},{2,1},{3,2},{4,3},{5,4},{6,5},{7,6},{8,7},{9,8},{10,9},{11,1... | collective-permute-start | bytes 786440 | tf_op jit(solution)/shard_map/ppermute | solution.py:23
  90.7 2.4 %collective-permute-start.10 = (f32[1,512,128]{1,2,0:T(8,128)S(1)}, f32[1,512,128]{1,2,0:T(8,128)S(1)}, u32[]{:S(2)}, u32[]{:S(2)}) collective-permute-start(f32[1,512,128]{1,2,0:T(8,128)S(1)} %convolution_bitcast_fusion.9), channel_id=1, source_target_pairs={{0,1},{1,2},{2,3},{3,4},{4,5},{5,6},{6,7},{7,8},{8,9},{9,10},{10,1... | collective-permute-start | bytes 786440 | tf_op jit(solution)/shard_map/ppermute | solution.py:22
  93.1 1.5 collective-permute-done.11
  95.7 8.1 %collective-permute-done.10 = f32[1,512,128]{1,2,0:T(8,128)S(1)} collective-permute-done((f32[1,512,128]{1,2,0:T(8,128)S(1)}, f32[1,512,128]{1,2,0:T(8,128)S(1)}, u32[]{:S(2)}, u32[]{:S(2)}) %collective-permute-start.10) | collective-permute-done | bytes 262176 | tf_op jit(solution)/shard_map/ppermute | solution.py:22
  103.8 1.2 fusion.10
  105.0 1.2 convolution_bitcast_fusion.6
  106.2 1.9 %collective-permute-start.13 = (f32[1,512,128]{1,2,0:T(8,128)S(1)}, f32[1,512,128]{1,2,0:T(8,128)S(1)}, u32[]{:S(2)}, u32[]{:S(2)}) collective-permute-start(f32[1,512,128]{1,2,0:T(8,128)S(1)} %convolution_bitcast_fusion.6), channel_id=1, source_target_pairs={{0,510},{1,511},{2,0},{3,1},{4,2},{5,3},{6,4},{7,5},{8,6},{9,7},{1... | collective-permute-start | bytes 786440 | tf_op jit(solution)/shard_map/ppermute | solution.py:12
  108.1 4.1 %collective-permute-start.12 = (f32[1,512,128]{1,2,0:T(8,128)S(1)}, f32[1,512,128]{1,2,0:T(8,128)S(1)}, u32[]{:S(2)}, u32[]{:S(2)}) collective-permute-start(f32[1,512,128]{1,2,0:T(8,128)S(1)} %convolution_bitcast_fusion.6), channel_id=1, source_target_pairs={{0,2},{1,3},{2,4},{3,5},{4,6},{5,7},{6,8},{7,9},{8,10},{9,11},{10,... | collective-permute-start | bytes 786440 | tf_op jit(solution)/shard_map/ppermute | solution.py:12
  112.3 2.2 %collective-permute-done.13 = f32[1,512,128]{1,2,0:T(8,128)S(1)} collective-permute-done((f32[1,512,128]{1,2,0:T(8,128)S(1)}, f32[1,512,128]{1,2,0:T(8,128)S(1)}, u32[]{:S(2)}, u32[]{:S(2)}) %collective-permute-start.13) | collective-permute-done | bytes 262176 | tf_op jit(solution)/shard_map/ppermute | solution.py:12
  114.4 2.4 %fusion.23 = f32[128,512]{1,0:T(8,128)S(1)} fusion(f32[1,512,512]{2,1,0:T(8,128)} %collective-permute-done.6, f32[1,512,128]{1,2,0:T(8,128)S(1)} %collective-permute-done.13), kind=kOutput, calls=%fused_computation.42 | convolution fusion | flops 402653184 | bytes 1572864 | tf_op jit(solution)/shard_map/sij,sjk->sik/dot_general | solution.py:29
  116.8 2.4 %fusion.19 = f32[128,512]{1,0:T(8,128)S(1)} fusion(f32[128,512]{1,0:T(8,128)S(1)} %fusion.23, f32[1,512,512]{2,1,0:T(8,128)} %collective-permute-done.7), kind=kOutput, calls=%fused_computation.38 | convolution fusion | flops 402653184 | bytes 1572864 | tf_op jit(solution)/shard_map/sij,sjk->sik/dot_general | solution.py:29
  119.2 1.2 convolution_bitcast_fusion.4
  120.4 2.6 %collective-permute-done.12 = f32[1,512,128]{1,2,0:T(8,128)S(1)} collective-permute-done((f32[1,512,128]{1,2,0:T(8,128)S(1)}, f32[1,512,128]{1,2,0:T(8,128)S(1)}, u32[]{:S(2)}, u32[]{:S(2)}) %collective-permute-start.12) | collective-permute-done | bytes 262176 | tf_op jit(solution)/shard_map/ppermute | solution.py:12
  123.0 2.4 %fusion.31 = f32[128,512]{1,0:T(8,128)S(1)} fusion(f32[1,512,512]{2,1,0:T(8,128)} %collective-permute-done.3, f32[1,512,128]{1,2,0:T(8,128)S(1)} %collective-permute-done.12), kind=kOutput, calls=%fused_computation.50 | convolution fusion | flops 402653184 | bytes 1572864 | tf_op jit(solution)/shard_map/sij,sjk->sik/dot_general | solution.py:29
  125.4 1.2 fusion.27
  126.6 1.2 fusion.13
  127.8 1.9 %fusion = f32[512,128]{0,1:T(8,128)} fusion(f32[512,128]{0,1:T(8,128)S(1)} %fusion.13, f32[1,512,512]{2,1,0:T(8,128)S(1)} %copy-done.1, f32[128,512]{1,0:T(8,128)S(1)} %fusion.50), kind=kOutput, calls=%fused_computation.19 | convolution fusion | flops 402718720 | bytes 1835008 | tf_op jit(solution)/shard_map/sij,sjk->sik/dot_general | solution.py:29
  129.7 4.6 %collective-permute-start.15 = (f32[1,512,128]{1,2,0:T(8,128)}, f32[1,512,128]{1,2,0:T(8,128)}, u32[]{:S(2)}, u32[]{:S(2)}) collective-permute-start(f32[1,512,128]{1,2,0:T(8,128)} %bitcast.60), channel_id=1, source_target_pairs={{1,0},{2,1},{3,2},{4,3},{5,4},{6,5},{7,6},{8,7},{9,8},{10,9},{11,1... | collective-permute-start | bytes 786440 | tf_op jit(solution)/shard_map/ppermute | solution.py:23
  134.3 1.8 %copy.10 = f32[1,512,128]{2,1,0:T(8,128)} copy(f32[1,512,128]{1,2,0:T(8,128)} %bitcast.60) | data formatting | bytes 524288
  136.1 1.9 %collective-permute-start.14 = (f32[1,512,128]{1,2,0:T(8,128)}, f32[1,512,128]{1,2,0:T(8,128)S(1)}, u32[]{:S(2)}, u32[]{:S(2)}) collective-permute-start(f32[1,512,128]{1,2,0:T(8,128)} %bitcast.60), channel_id=1, source_target_pairs={{0,1},{1,2},{2,3},{3,4},{4,5},{5,6},{6,7},{7,8},{8,9},{9,10},{10,1... | collective-permute-start | bytes 786440 | tf_op jit(solution)/shard_map/ppermute | solution.py:22
  138.0 2.1 %convolution_bitcast_fusion.1 = f32[1,512,128]{1,2,0:T(8,128)S(1)} fusion(f32[512,128]{0,1:T(8,128)} %fusion, f32[1,512,512]{2,1,0:T(8,128)S(1)} %copy-done), kind=kOutput, calls=%fused_computation.1 | convolution fusion | flops 402653184 | bytes 1572864 | tf_op jit(solution)/shard_map/sij,sjk->sik/dot_general | solution.py:29
  140.2 2.2 %convolution_bitcast_fusion = f32[1,512,128]{1,2,0:T(8,128)S(1)} fusion(f32[1,512,512]{2,1,0:T(8,128)S(1)} %copy-done.2, f32[1,512,128]{1,2,0:T(8,128)} %collective-permute-done.15), kind=kOutput, calls=%fused_computation | convolution fusion | flops 402653184 | bytes 1572864 | tf_op jit(solution)/shard_map/sij,sjk->sik/dot_general | solution.py:29
  142.4 7.0 %collective-permute-done.14 = f32[1,512,128]{1,2,0:T(8,128)S(1)} collective-permute-done((f32[1,512,128]{1,2,0:T(8,128)}, f32[1,512,128]{1,2,0:T(8,128)S(1)}, u32[]{:S(2)}, u32[]{:S(2)}) %collective-permute-start.14) | collective-permute-done | bytes 262176 | tf_op jit(solution)/shard_map/ppermute | solution.py:22
  149.4 1.2 fusion.16
  (25 shorter events, 6.7 us)
Async XLA Ops:
  0.6 75.3 %copy-start = (f32[1,512,512]{2,1,0:T(8,128)S(1)}, f32[1,512,512]{2,1,0:T(8,128)}, u32[]{:S(2)}) copy-start(f32[1,512,512]{2,1,0:T(8,128)} %param.6) | copy-start | bytes 3145732
  0.6 17.8 %copy-start.1 = (f32[1,512,512]{2,1,0:T(8,128)S(1)}, f32[1,512,512]{2,1,0:T(8,128)}, u32[]{:S(2)}) copy-start(f32[1,512,512]{2,1,0:T(8,128)} %param.9) | copy-start | bytes 3145732
  0.7 29.9 %copy-start.2 = (f32[1,512,512]{2,1,0:T(8,128)S(1)}, f32[1,512,512]{2,1,0:T(8,128)}, u32[]{:S(2)}) copy-start(f32[1,512,512]{2,1,0:T(8,128)} %param.8) | copy-start | bytes 3145732
  3.8 26.8 %collective-permute-start.1 = (f32[1,512,128]{2,1,0:T(8,128)}, f32[1,512,128]{2,1,0:T(8,128)}, u32[]{:S(2)}, u32[]{:S(2)}) collective-permute-start(f32[1,512,128]{2,1,0:T(8,128)} %convolution_bitcast_fusion.18), channel_id=1, source_target_pairs={{1,0},{2,1},{3,2},{4,3},{5,4},{6,5},{7,6},{8,7},{9,8},{10,9},{11,1... | collective-permute-start | bytes 786440 | tf_op jit(solution)/shard_map/ppermute | solution.py:23
  13.9 35.4 %collective-permute-start.6 = (f32[1,512,512]{2,1,0:T(8,128)}, f32[1,512,512]{2,1,0:T(8,128)}, u32[]{:S(2)}, u32[]{:S(2)}) collective-permute-start(f32[1,512,512]{2,1,0:T(8,128)} %param.8), channel_id=1, source_target_pairs={{0,511},{1,0},{2,1},{3,2},{4,3},{5,4},{6,5},{7,6},{8,7},{9,8},{10,... | collective-permute-start | bytes 3145736 | tf_op jit(solution)/shard_map/ppermute | solution.py:12
  16.5 16.4 %collective-permute-start = (f32[1,512,128]{2,1,0:T(8,128)}, f32[1,512,128]{2,1,0:T(8,128)}, u32[]{:S(2)}, u32[]{:S(2)}) collective-permute-start(f32[1,512,128]{2,1,0:T(8,128)} %convolution_bitcast_fusion.18), channel_id=1, source_target_pairs={{0,1},{1,2},{2,3},{3,4},{4,5},{5,6},{6,7},{7,8},{8,9},{9,10},{10,1... | collective-permute-start | bytes 786440 | tf_op jit(solution)/shard_map/ppermute | solution.py:22
  18.4 33.3 %collective-permute-start.7 = (f32[1,512,512]{2,1,0:T(8,128)S(1)}, f32[1,512,512]{2,1,0:T(8,128)}, u32[]{:S(2)}, u32[]{:S(2)}) collective-permute-start(f32[1,512,512]{2,1,0:T(8,128)S(1)} %copy-done.1), channel_id=1, source_target_pairs={{0,511},{1,0},{2,1},{3,2},{4,3},{5,4},{6,5},{7,6},{8,7},{9,8},{10,... | collective-permute-start | bytes 3145736 | tf_op jit(solution)/shard_map/ppermute | solution.py:12
  27.5 36.5 %collective-permute-start.3 = (f32[1,512,512]{2,1,0:T(8,128)}, f32[1,512,512]{2,1,0:T(8,128)}, u32[]{:S(2)}, u32[]{:S(2)}) collective-permute-start(f32[1,512,512]{2,1,0:T(8,128)} %param.7), channel_id=1, source_target_pairs={{0,1},{1,2},{2,3},{3,4},{4,5},{5,6},{6,7},{7,8},{8,9},{9,10},{10,1... | collective-permute-start | bytes 3145736 | tf_op jit(solution)/shard_map/ppermute | solution.py:12
  30.5 2.3 %copy-start.3 = (f32[1,512,512]{2,1,0:T(8,128)S(1)}, f32[1,512,512]{2,1,0:T(8,128)}, u32[]{:S(2)}) copy-start(f32[1,512,512]{2,1,0:T(8,128)} %param.7) | copy-start | bytes 3145732
  36.3 11.1 %collective-permute-start.5 = (f32[1,512,128]{1,2,0:T(8,128)S(1)}, f32[1,512,128]{1,2,0:T(8,128)S(1)}, u32[]{:S(2)}, u32[]{:S(2)}) collective-permute-start(f32[1,512,128]{1,2,0:T(8,128)S(1)} %convolution_bitcast_fusion.15), channel_id=1, source_target_pairs={{0,510},{1,511},{2,0},{3,1},{4,2},{5,3},{6,4},{7,5},{8,6},{9,7},{1... | collective-permute-start | bytes 786440 | tf_op jit(solution)/shard_map/ppermute | solution.py:12
  38.6 27.8 %collective-permute-start.4 = (f32[1,512,512]{2,1,0:T(8,128)S(1)}, f32[1,512,512]{2,1,0:T(8,128)S(1)}, u32[]{:S(2)}, u32[]{:S(2)}) collective-permute-start(f32[1,512,512]{2,1,0:T(8,128)S(1)} %copy-done.1), channel_id=1, source_target_pairs={{0,1},{1,2},{2,3},{3,4},{4,5},{5,6},{6,7},{7,8},{8,9},{9,10},{10,1... | collective-permute-start | bytes 3145736 | tf_op jit(solution)/shard_map/ppermute | solution.py:12
  47.4 16.6 %collective-permute-start.2 = (f32[1,512,128]{1,2,0:T(8,128)S(1)}, f32[1,512,128]{1,2,0:T(8,128)S(1)}, u32[]{:S(2)}, u32[]{:S(2)}) collective-permute-start(f32[1,512,128]{1,2,0:T(8,128)S(1)} %convolution_bitcast_fusion.15), channel_id=1, source_target_pairs={{0,2},{1,3},{2,4},{3,5},{4,6},{5,7},{6,8},{7,9},{8,10},{9,11},{10,... | collective-permute-start | bytes 786440 | tf_op jit(solution)/shard_map/ppermute | solution.py:12
  69.9 7.2 %collective-permute-start.9 = (f32[1,512,128]{1,2,0:T(8,128)S(1)}, f32[1,512,128]{1,2,0:T(8,128)S(1)}, u32[]{:S(2)}, u32[]{:S(2)}) collective-permute-start(f32[1,512,128]{1,2,0:T(8,128)S(1)} %bitcast.239), channel_id=1, source_target_pairs={{1,0},{2,1},{3,2},{4,3},{5,4},{6,5},{7,6},{8,7},{9,8},{10,9},{11,1... | collective-permute-start | bytes 786440 | tf_op jit(solution)/shard_map/ppermute | solution.py:23
  73.3 13.1 %collective-permute-start.8 = (f32[1,512,128]{1,2,0:T(8,128)S(1)}, f32[1,512,128]{1,2,0:T(8,128)S(1)}, u32[]{:S(2)}, u32[]{:S(2)}) collective-permute-start(f32[1,512,128]{1,2,0:T(8,128)S(1)} %bitcast.240), channel_id=1, source_target_pairs={{0,1},{1,2},{2,3},{3,4},{4,5},{5,6},{6,7},{7,8},{8,9},{9,10},{10,1... | collective-permute-start | bytes 786440 | tf_op jit(solution)/shard_map/ppermute | solution.py:22
  88.8 5.8 %collective-permute-start.11 = (f32[1,512,128]{1,2,0:T(8,128)S(1)}, f32[1,512,128]{1,2,0:T(8,128)S(1)}, u32[]{:S(2)}, u32[]{:S(2)}) collective-permute-start(f32[1,512,128]{1,2,0:T(8,128)S(1)} %convolution_bitcast_fusion.9), channel_id=1, source_target_pairs={{1,0},{2,1},{3,2},{4,3},{5,4},{6,5},{7,6},{8,7},{9,8},{10,9},{11,1... | collective-permute-start | bytes 786440 | tf_op jit(solution)/shard_map/ppermute | solution.py:23
  90.7 13.1 %collective-permute-start.10 = (f32[1,512,128]{1,2,0:T(8,128)S(1)}, f32[1,512,128]{1,2,0:T(8,128)S(1)}, u32[]{:S(2)}, u32[]{:S(2)}) collective-permute-start(f32[1,512,128]{1,2,0:T(8,128)S(1)} %convolution_bitcast_fusion.9), channel_id=1, source_target_pairs={{0,1},{1,2},{2,3},{3,4},{4,5},{5,6},{6,7},{7,8},{8,9},{9,10},{10,1... | collective-permute-start | bytes 786440 | tf_op jit(solution)/shard_map/ppermute | solution.py:22
  106.2 8.3 %collective-permute-start.13 = (f32[1,512,128]{1,2,0:T(8,128)S(1)}, f32[1,512,128]{1,2,0:T(8,128)S(1)}, u32[]{:S(2)}, u32[]{:S(2)}) collective-permute-start(f32[1,512,128]{1,2,0:T(8,128)S(1)} %convolution_bitcast_fusion.6), channel_id=1, source_target_pairs={{0,510},{1,511},{2,0},{3,1},{4,2},{5,3},{6,4},{7,5},{8,6},{9,7},{1... | collective-permute-start | bytes 786440 | tf_op jit(solution)/shard_map/ppermute | solution.py:12
  108.1 14.9 %collective-permute-start.12 = (f32[1,512,128]{1,2,0:T(8,128)S(1)}, f32[1,512,128]{1,2,0:T(8,128)S(1)}, u32[]{:S(2)}, u32[]{:S(2)}) collective-permute-start(f32[1,512,128]{1,2,0:T(8,128)S(1)} %convolution_bitcast_fusion.6), channel_id=1, source_target_pairs={{0,2},{1,3},{2,4},{3,5},{4,6},{5,7},{6,8},{7,9},{8,10},{9,11},{10,... | collective-permute-start | bytes 786440 | tf_op jit(solution)/shard_map/ppermute | solution.py:12
  129.7 10.5 %collective-permute-start.15 = (f32[1,512,128]{1,2,0:T(8,128)}, f32[1,512,128]{1,2,0:T(8,128)}, u32[]{:S(2)}, u32[]{:S(2)}) collective-permute-start(f32[1,512,128]{1,2,0:T(8,128)} %bitcast.60), channel_id=1, source_target_pairs={{1,0},{2,1},{3,2},{4,3},{5,4},{6,5},{7,6},{8,7},{9,8},{10,9},{11,1... | collective-permute-start | bytes 786440 | tf_op jit(solution)/shard_map/ppermute | solution.py:23
  136.1 13.3 %collective-permute-start.14 = (f32[1,512,128]{1,2,0:T(8,128)}, f32[1,512,128]{1,2,0:T(8,128)S(1)}, u32[]{:S(2)}, u32[]{:S(2)}) collective-permute-start(f32[1,512,128]{1,2,0:T(8,128)} %bitcast.60), channel_id=1, source_target_pairs={{0,1},{1,2},{2,3},{3,4},{4,5},{5,6},{6,7},{7,8},{8,9},{9,10},{10,1... | collective-permute-start | bytes 786440 | tf_op jit(solution)/shard_map/ppermute | solution.py:22
  140.2 9.3 %copy-start.4 = (f32[1,512,512]{2,1,0:T(8,128)S(1)}, f32[1,512,512]{2,1,0:T(8,128)}, u32[]{:S(2)}) copy-start(f32[1,512,512]{2,1,0:T(8,128)} %param.7) | copy-start | bytes 3145732
where the time goes:
time: 152 us; the launch traced here: 151 us
  starting transfers between devices  61.5 us (40%)
  matrix products  47 us (31%)
  waiting for transfers between devices  38.1 us (25%)
  local copies, waits for them, and re-layouts  3.74 us (2%)
    dot_general x28, matrix products, product(): jnp.einsum('sij,sjk->sik', matrix, vector, precision=lax.Precision.HIGHEST)  47 us
    ppermute x8, starting transfers between devices, passed_along(): return lax.ppermute(value, axis, pairs)  32.7 us
    ppermute x4, waiting for transfers between devices, padded(): before = lax.ppermute(last, axis, up)  23.2 us
    ppermute x4, starting transfers between devices, padded(): after = lax.ppermute(leading, axis, down)  20 us
    ppermute x8, waiting for transfers between devices, passed_along(): return lax.ppermute(value, axis, pairs)  13.4 us
    ppermute x4, starting transfers between devices, padded(): before = lax.ppermute(last, axis, up)  8.89 us
    unnamed x13, local copies, waits for them, and re-layouts  3.74 us
  transfers between devices with their start and end apart: 16, of which 7 were waited for; matrix products, arithmetic and copies ran while one was open for 20% of the time, Pallas kernels for 0%

commit v1 on v0

v1 whole, which is shorter than its diff:
```python
import jax
import jax.numpy as jnp
from jax import lax
from jax.experimental import pallas as pl
from jax.experimental.pallas import tpu as pltpu
from jax.sharding import PartitionSpec as P

F32 = jnp.float32
BF16 = jnp.bfloat16
VMEM = pl.BlockSpec(memory_space=pltpu.VMEM)
SMEM = pl.BlockSpec(memory_space=pltpu.SMEM)
AXIS = "station"


def split(v):
    high = v.astype(BF16)
    return high, (v - high.astype(F32)).astype(BF16)


def times(matrix, v):
    both = jnp.concatenate(split(v), axis=1)
    out = jnp.dot(matrix[0][...], both, preferred_element_type=F32)
    out += jnp.dot(matrix[1][...], both, preferred_element_type=F32)
    n = v.shape[1]
    return out[:, :n] + out[:, n:]


def put_split(pair, value, at=None):
    high, low = split(value)
    if at is None:
        pair[0][...], pair[1][...] = high, low
    else:
        pair[0][:, at], pair[1][:, at] = high, low


def setup_kernel(odd, rhs, lower, upper, diag, inverse, w, h, e0, e1, n0, n1, f0, f1, d0, d1, j0, j1, h0, h1):
    e, n, f = (e0, e1), (n0, n1), (f0, f1)
    put_split(e, inverse[...])
    w[...] = times(e, rhs[...])
    is_odd = odd[0] == 1
    cols = rhs.shape[1]
    for k in range(inverse.shape[1] // cols):
        at = pl.ds(k * cols, cols)
        low, up = lower[:, at], upper[:, at]
        near = jnp.where(is_odd, low, up)
        far = jnp.where(is_odd, up, low)
        put_split(n, near, at)
        put_split(f, far, at)
        put_split((d0, d1), diag[:, at], at)
        put_split((j0, j1), times(e, near), at)
        product = times(e, far)
        put_split((h0, h1), product, at)
        h[k] = product


def first_pair_kernel(odd, w, near, j0, j1, h, out):
    blocks = h.shape[0]
    out[:blocks] = h[...]
    out[blocks] = w[...]
    out[blocks + 1] = w[...] - times((j0, j1), near[1 - odd[0]])


def pair_kernel(odd, w, near, j0, j1, out):
    out[0] = w[...]
    out[1] = w[...] - times((j0, j1), near[1 - odd[0]])


def second_pass(odd, sent, got, at, h, k, pair, s_far):
    w, ps = sent[at], sent[at + 1]
    w_far, ps_far = got[odd[0], at], got[odd[0], at + 1]
    pair[0] = ps - times(h, w_far)
    sf = ps_far - times(k, w)
    s_far[...] = sf
    pair[1] = times(h, sf)


def first_second_kernel(odd, sent, got, h0, h1, pair, s_far, k0, k1):
    blocks = sent.shape[0] - 2
    cols = sent.shape[2]
    for i in range(blocks):
        put_split((k0, k1), got[odd[0], i], pl.ds(i * cols, cols))
    second_pass(odd, sent, got, blocks, (h0, h1), (k0, k1), pair, s_far)


def second_kernel(odd, sent, got, h0, h1, k0, k1, pair, s_far):
    second_pass(odd, sent, got, 0, (h0, h1), (k0, k1), pair, s_far)


def parts_kernel(odd, near, j0, j1, out):
    n = near.shape[3]
    v = jnp.concatenate([near[1 - odd[0], 0], near[1 - odd[0], 1]], axis=1)
    both = times((j0, j1), v)
    out[0], out[1] = both[:, :n], both[:, n:]


def step_kernel(odd, pair, s_far, sent, got, r, h0, h1, k0, k1, d0, d1, f0, f1, d, rest):
    m, u = sent[0], sent[1]
    m_far, u_far = got[odd[0], 0], got[odd[0], 1]
    step = pair[0] + u + times((h0, h1), m_far)
    step_far = s_far[...] + u_far + times((k0, k1), m)
    d[...] = step
    rest[...] = r[...] - times((d0, d1), step) - times((f0, f1), step_far)


def residual_kernel(odd, near, rest, n0, n1, e0, e1, r, w):
    value = rest[...] - times((n0, n1), near[1 - odd[0]])
    r[...] = value
    w[...] = times((e0, e1), value)


def last_kernel(odd, near, rest, n0, n1, first, d, x, r):
    r[0] = rest[...] - times((n0, n1), near[1 - odd[0]])
    x[0] = first[...] + d[...]


def call(kernel, outs, *args):
    return pl.pallas_call(
        kernel,
        out_shape=[jax.ShapeDtypeStruct(shape, dtype) for shape, dtype in outs],
        in_specs=[SMEM] + [VMEM] * (len(args) - 1),
        out_specs=[VMEM] * len(outs),
        compiler_params=pltpu.CompilerParams(vmem_limit_bytes=24 * 1024 * 1024),
    )(*args)


def local(right_side, diag_blocks, lower_blocks, upper_blocks, approx_inverse):
    count = lax.axis_size(AXIS)
    near_groups = [[i, i + 1] for i in range(0, count, 2)]
    far_groups = [[i + 1, (i + 2) % count] for i in range(0, count, 2)]

    def near(v):
        return lax.all_gather(v, AXIS, axis_index_groups=near_groups)

    def far(v):
        return lax.all_gather(v, AXIS, axis_index_groups=far_groups)

    odd = (lax.axis_index(AXIS) % 2).astype(jnp.int32).reshape(1)
    b = right_side[0]
    size, cols = b.shape
    blocks = size // cols
    vec = ((size, cols), F32)
    two = ((2, size, cols), F32)
    half = [((size, size), BF16)] * 2

    w, h, *mats = call(
        setup_kernel, [vec, ((blocks, size, cols), F32)] + half * 6,
        odd, b, lower_blocks[0], upper_blocks[0], diag_blocks[0], approx_inverse[0],
    )
    E, N, F, D, J, H = (mats[i:i + 2] for i in range(0, 12, 2))
    (sent,) = call(first_pair_kernel, [((blocks + 2, size, cols), F32)], odd, w, near(w), *J, h)
    pair, s_far, *K = call(first_second_kernel, [two, vec] + half, odd, sent, far(sent), *H)
    (parts,) = call(parts_kernel, [two], odd, near(pair), *J)
    d1, rest = call(step_kernel, [vec, vec], odd, pair, s_far, parts, far(parts), b, *H, *K, *D, *F)
    r, w = call(residual_kernel, [vec, vec], odd, near(d1), rest, *N, *E)
    (sent,) = call(pair_kernel, [two], odd, w, near(w), *J)
    pair, s_far = call(second_kernel, [two, vec], odd, sent, far(sent), *H, *K)
    (parts,) = call(parts_kernel, [two], odd, near(pair), *J)
    d2, rest = call(step_kernel, [vec, vec], odd, pair, s_far, parts, far(parts), r, *H, *K, *D, *F)
    one = ((1, size, cols), F32)
    return tuple(call(last_kernel, [one, one], odd, near(d2), rest, *N, d1, d2))


def solution(mesh):
    spec = P(AXIS, None, None)
    return jax.shard_map(local, mesh=mesh, in_specs=(spec,) * 5, out_specs=(spec, spec), check_vma=False)
```

time: 152 us -> 256 us (1.68)
  the two profiles are of different devices: /device:TPU:0 before, /device:TPU:1 now
where the time goes in v1:
time: 256 us; the launch traced here: 254 us
  waiting for transfers between devices  154 us (60%)
  local copies, waits for them, and re-layouts  35.6 us (14%)
  blocking collectives  28.1 us (11%)
  Pallas kernels  21.9 us (9%)
  between operations  14.3 us (6%)
    all_gather x4, waiting for transfers between devices, far(): return lax.all_gather(v, AXIS, axis_index_groups=far_groups)  111 us
    all_gather x2, waiting for transfers between devices, near(): return lax.all_gather(v, AXIS, axis_index_groups=near_groups)  42.6 us
    unnamed x88, local copies, waits for them, and re-layouts  35.6 us
    all_gather x4, blocking collectives, near(): return lax.all_gather(v, AXIS, axis_index_groups=near_groups)  28.1 us
    pallas_call x11, Pallas kernels, call(): pl.pallas_call(kernel, out_shape=[jax.ShapeDtypeStruct(shape, dtype) for...  21.9 us
  transfers between devices with their start and end apart: 6, of which 6 were waited for; matrix products, arithmetic and copies ran while one was open for 0% of the time, Pallas kernels for 0%

profile of v1, /device:TPU:1, one launch (start us, length us, event | category | flops | bytes accessed | tf_op | source)
XLA Modules:
  0.0 254.3 jit_solution(13970107069049208456)
XLA Ops:
  7.2 1.2 copy-done.23
  8.4 1.2 copy-done.24
  9.7 1.2 copy-done.25
  10.9 1.2 copy-done.26
  12.1 0.9 copy-done.27
  13.1 2.8 %shard_map.68 = (f32[512,128]{1,0:T(8,128)S(1)}, f32[4,512,128]{2,1,0:T(8,128)S(1)}, bf16[512,512]{1,0:T(8,128)(2,1)S(1)}, bf16[512,512]{1,0:T(8,128)(2,1)S(1)},...) custom-call(s32[1]{0:T(128)} %bitcast.odd, ...), custom_call_target="tpu_custom_call" | custom-call | tf_op jit(solution)/shard_map/pallas_call | solution.py:117
  17.5 0.8 copy-done.11
  18.3 0.8 copy-done.14
  19.2 0.8 copy-done.17
  20.7 0.8 copy-done.36
  22.4 8.7 %all-gather = f32[1024,128]{1,0:T(8,128)S(1)} all-gather(f32[512,128]{1,0:T(8,128)S(1)} %get-tuple-element.28.w), channel_id=2, replica_groups={{0,1},{2,3},{4,5},{6,7},{8,9},{10,11},{12,13},{14,15},{16,17},{18,19},{..., dimensions={0}, use_global_device_ids=true | all-gather | bytes 786432 | tf_op jit(solution)/shard_map/all_gather | solution.py:132
  31.1 1.7 shard_map.69.sent
  32.8 37.9 %all-gather.17.cloned.1.call-done = f32[12,512,128]{2,1,0:T(8,128)} async-done(((f32[6,512,128]{2,1,0:T(8,128)}), f32[12,512,128]{2,1,0:T(8,128)}) %all-gather.17.cloned.1.call-update) | async-done | bytes 3145744 | tf_op jit(solution)/shard_map/all_gather | solution.py:135
  70.6 1.9 copy-done
  72.5 3.0 %shard_map.70 = (f32[2,512,128]{2,1,0:T(8,128)S(1)}, f32[512,128]{1,0:T(8,128)S(1)}, bf16[512,512]{1,0:T(8,128)(2,1)S(1)}, bf16[512,512]{1,0:T(8,128)(2,1)S(1)}) custom-call(s32[1]{0:T(128)} %bitcast.odd, f32[6,512,128]{2,1,0:T(8,128)} %shard_map.69.sent, f32[2,6,512,128]{3,2,1,0:T(8,128)S(1)} %bitcast.16, bf16[512,512]{1,0:T(8,128)(2,1)S(1)} %get-tuple-element.32.h0, ...), custom_call_target="tpu_custom_call" | custom-call | tf_op jit(solution)/shard_map/pallas_call | solution.py:117
  77.1 21.3 %all-gather.19.cloned.1.call-done = f32[4,512,128]{2,1,0:T(8,128)} async-done(((f32[2,512,128]{2,1,0:T(8,128)}), f32[4,512,128]{2,1,0:T(8,128)}) %all-gather.19.cloned.1.call-update) | async-done | bytes 1048592 | tf_op jit(solution)/shard_map/all_gather | solution.py:132
  98.4 1.2 copy-done.32
  99.6 1.5 shard_map.71.sent
  101.2 26.6 %all-gather.21.cloned.1.call-done = f32[4,512,128]{2,1,0:T(8,128)} async-done(((f32[2,512,128]{2,1,0:T(8,128)}), f32[4,512,128]{2,1,0:T(8,128)}) %all-gather.21.cloned.1.call-update) | async-done | bytes 1048592 | tf_op jit(solution)/shard_map/all_gather | solution.py:135
  127.8 1.0 copy-done.10
  128.8 1.0 copy-done.12
  129.9 1.0 copy-done.15
  130.9 1.0 copy-done.18
  132.0 1.0 copy-done.21
  133.0 1.2 copy-done.34
  134.2 0.9 copy-done.43
  135.2 2.5 shard_map.72
  137.7 8.6 %all-gather.4 = f32[1024,128]{1,0:T(8,128)S(1)} all-gather(f32[512,128]{1,0:T(8,128)S(1)} %get-tuple-element.42.first), channel_id=6, replica_groups={{0,1},{2,3},{4,5},{6,7},{8,9},{10,11},{12,13},{14,15},{16,17},{18,19},{..., dimensions={0}, use_global_device_ids=true | all-gather | bytes 786432 | tf_op jit(solution)/shard_map/all_gather | solution.py:132
  146.4 1.3 shard_map.73
  147.7 2.2 all-gather.5
  149.9 1.2 shard_map.74.sent
  151.2 20.5 %all-gather.23.cloned.1.call-done = f32[4,512,128]{2,1,0:T(8,128)} async-done(((f32[2,512,128]{2,1,0:T(8,128)}), f32[4,512,128]{2,1,0:T(8,128)}) %all-gather.23.cloned.1.call-update) | async-done | bytes 1048592 | tf_op jit(solution)/shard_map/all_gather | solution.py:135
  171.7 1.2 copy-done.35
  172.9 2.6 %shard_map.75 = (f32[2,512,128]{2,1,0:T(8,128)S(1)}, f32[512,128]{1,0:T(8,128)S(1)}) custom-call(s32[1]{0:T(128)} %bitcast.odd, f32[2,512,128]{2,1,0:T(8,128)} %shard_map.74.sent, f32[2,2,512,128]{3,2,1,0:T(8,128)S(1)} %bitcast.31, bf16[512,512]{1,0:T(8,128)(2,1)S(1)} %get-tuple-element.32.h0, bf16[512,512]{1,0:T(8,128)(2,1)S(1)} %get-tuple-element.33.h1, ...), custom_call_target="tpu_custom_call" | custom-call | tf_op jit(solution)/shard_map/pallas_call | solution.py:117
  177.1 21.3 %all-gather.25.cloned.1.call-done = f32[4,512,128]{2,1,0:T(8,128)} async-done(((f32[2,512,128]{2,1,0:T(8,128)}), f32[4,512,128]{2,1,0:T(8,128)}) %all-gather.25.cloned.1.call-update) | async-done | bytes 1048592 | tf_op jit(solution)/shard_map/all_gather | solution.py:132
  198.4 1.2 copy-done.31
  199.6 1.5 shard_map.76.sent
  201.2 26.6 %all-gather.27.cloned.1.call-done = f32[4,512,128]{2,1,0:T(8,128)} async-done(((f32[2,512,128]{2,1,0:T(8,128)}), f32[4,512,128]{2,1,0:T(8,128)}) %all-gather.27.cloned.1.call-update) | async-done | bytes 1048592 | tf_op jit(solution)/shard_map/all_gather | solution.py:135
  227.8 1.0 copy-done.8
  228.8 1.0 copy-done.13
  229.8 1.0 copy-done.16
  230.9 1.0 copy-done.19
  231.9 1.0 copy-done.22
  233.0 1.2 copy-done.33
  234.2 0.9 copy-done.41
  235.2 2.5 shard_map.77
  237.6 8.6 %all-gather.9 = f32[1024,128]{1,0:T(8,128)S(1)} all-gather(f32[512,128]{1,0:T(8,128)S(1)} %get-tuple-element.52.d), channel_id=11, replica_groups={{0,1},{2,3},{4,5},{6,7},{8,9},{10,11},{12,13},{14,15},{16,17},{18,19},{..., dimensions={0}, use_global_device_ids=true | all-gather | bytes 786432 | tf_op jit(solution)/shard_map/all_gather | solution.py:132
  246.3 1.2 shard_map.78
  (73 shorter events, 6.6 us)
Async XLA Ops:
  7.2 63.5 %all-gather.17.cloned.1.call-start = ((), (), s32[]{:S(2)}) async-start(), calls=%async_computation | async-start | bytes 4718592 | tf_op jit(solution)/shard_map/all_gather | solution.py:135
  7.2 1.2 copy-start.23
  8.4 1.2 copy-start.24
  9.7 1.2 copy-start.25
  10.9 1.2 copy-start.26
  12.1 0.9 copy-start.27
  15.9 0.8 copy-start.1
  16.7 0.8 copy-start.4
  17.5 0.8 copy-start.11
  18.3 0.8 copy-start.14
  19.2 0.8 copy-start.17
  20.0 0.8 copy-start.20
  20.7 0.8 copy-start.36
  21.6 0.8 copy-start.38
  32.7 65.7 %all-gather.19.cloned.1.call-start = ((), (), s32[]{:S(2)}) async-start(), calls=%async_computation.1 | async-start | bytes 1572864 | tf_op jit(solution)/shard_map/all_gather | solution.py:132
  70.6 1.9 copy-start
  75.6 0.8 copy-start.9
  77.1 50.7 %copy-start.28 = (f32[1,512,128]{2,1,0:T(8,128)S(1)}, f32[1,512,128]{2,1,0:T(8,128)}, u32[]{:S(2)}) copy-start(f32[1,512,128]{2,1,0:T(8,128)} %param.5) | copy-start | bytes 786436
  77.1 50.7 %all-gather.21.cloned.1.call-start = ((), (), s32[]{:S(2)}) async-start(), calls=%async_computation.2 | async-start | bytes 1572864 | tf_op jit(solution)/shard_map/all_gather | solution.py:135
  98.4 1.2 copy-start.32
  101.2 70.5 %all-gather.23.cloned.1.call-start = ((), (), s32[]{:S(2)}) async-start(), calls=%async_computation.3 | async-start | bytes 1572864 | tf_op jit(solution)/shard_map/all_gather | solution.py:135
  127.8 1.0 copy-start.10
  128.8 1.0 copy-start.12
  129.9 1.0 copy-start.15
  130.9 1.0 copy-start.18
  132.0 1.0 copy-start.21
  133.0 1.2 copy-start.34
  134.2 0.9 copy-start.43
  135.2 11.2 %copy-start.2 = (bf16[512,512]{1,0:T(8,128)(2,1)S(1)}, bf16[512,512]{1,0:T(8,128)(2,1)}, u32[]{:S(2)}) copy-start(bf16[512,512]{1,0:T(8,128)(2,1)} %copy-done.1) | copy-start | bytes 1572868
  135.2 11.2 %copy-start.5 = (bf16[512,512]{1,0:T(8,128)(2,1)S(1)}, bf16[512,512]{1,0:T(8,128)(2,1)}, u32[]{:S(2)}) copy-start(bf16[512,512]{1,0:T(8,128)(2,1)} %copy-done.4) | copy-start | bytes 1572868
  135.2 11.2 %copy-start.37 = (bf16[512,512]{1,0:T(8,128)(2,1)S(1)}, bf16[512,512]{1,0:T(8,128)(2,1)}, u32[]{:S(2)}) copy-start(bf16[512,512]{1,0:T(8,128)(2,1)} %copy-done.36) | copy-start | bytes 1572868
  135.2 11.2 %copy-start.39 = (bf16[512,512]{1,0:T(8,128)(2,1)S(1)}, bf16[512,512]{1,0:T(8,128)(2,1)}, u32[]{:S(2)}) copy-start(bf16[512,512]{1,0:T(8,128)(2,1)} %copy-done.38) | copy-start | bytes 1572868
  137.7 10.0 %copy-start.29 = (f32[512,128]{1,0:T(8,128)}, f32[512,128]{1,0:T(8,128)S(1)}, u32[]{:S(2)}) copy-start(f32[512,128]{1,0:T(8,128)S(1)} %get-tuple-element.42.first) | copy-start | bytes 786436
  151.1 47.3 %all-gather.25.cloned.1.call-start = ((), (), s32[]{:S(2)}) async-start(), calls=%async_computation.4 | async-start | bytes 1572864 | tf_op jit(solution)/shard_map/all_gather | solution.py:132
  171.7 1.2 copy-start.35
  175.5 0.8 copy-start.7
  177.1 50.7 %all-gather.27.cloned.1.call-start = ((), (), s32[]{:S(2)}) async-start(), calls=%async_computation.5 | async-start | bytes 1572864 | tf_op jit(solution)/shard_map/all_gather | solution.py:135
  198.4 1.2 copy-start.31
  227.8 1.0 copy-start.8
  228.8 1.0 copy-start.13
  229.8 1.0 copy-start.16
  230.9 1.0 copy-start.19
  231.9 1.0 copy-start.22
  233.0 1.2 copy-start.33
  234.2 0.9 copy-start.41
  235.1 11.1 %copy-start.3 = (bf16[512,512]{1,0:T(8,128)(2,1)S(1)}, bf16[512,512]{1,0:T(8,128)(2,1)}, u32[]{:S(2)}) copy-start(bf16[512,512]{1,0:T(8,128)(2,1)} %copy-done.1) | copy-start | bytes 1572868
  235.1 11.1 %copy-start.6 = (bf16[512,512]{1,0:T(8,128)(2,1)S(1)}, bf16[512,512]{1,0:T(8,128)(2,1)}, u32[]{:S(2)}) copy-start(bf16[512,512]{1,0:T(8,128)(2,1)} %copy-done.4) | copy-start | bytes 1572868
  235.1 11.1 %copy-start.30 = (f32[512,128]{1,0:T(8,128)S(1)}, f32[512,128]{1,0:T(8,128)}, u32[]{:S(2)}) copy-start(f32[512,128]{1,0:T(8,128)} %copy-done.29) | copy-start | bytes 786436
  (2 other events, 1.4 us)
Sparse Core Ops, SparseCore 0:
  32.8 37.7 all-gather.16
  77.2 21.1 all-gather.18
  101.3 26.4 all-gather.20
  151.3 20.3 all-gather.22
  177.2 21.1 all-gather.24
  201.3 26.4 all-gather.26

commit v2 on v1

v2 whole, which is shorter than its diff:
```python
import jax
import jax.numpy as jnp
from jax import lax
from jax.experimental import pallas as pl
from jax.experimental.pallas import tpu as pltpu
from jax.sharding import PartitionSpec as P

F32 = jnp.float32
BF16 = jnp.bfloat16
VMEM = pl.BlockSpec(memory_space=pltpu.VMEM)
SMEM = pl.BlockSpec(memory_space=pltpu.SMEM)
HBM = pl.BlockSpec(memory_space=pltpu.HBM)
ANY = pl.BlockSpec(memory_space=pl.ANY)
AXIS = "station"
ROWS = 128
COST = 8 * 512 * 512 * 128


def split(v):
    high = v.astype(BF16)
    return high, (v - high.astype(F32)).astype(BF16)


def stack(v):
    return jnp.concatenate(split(v), axis=1)


def rows_times(matrix, rows, both):
    out = jnp.dot(matrix[0][rows, :], both, preferred_element_type=F32)
    out += jnp.dot(matrix[1][rows, :], both, preferred_element_type=F32)
    n = both.shape[1] // 2
    return out[:, :n] + out[:, n:]


def blocks_of(size):
    return [pl.ds(k, ROWS) for k in range(0, size, ROWS)]


def times(matrix, v):
    both = stack(v)
    return jnp.concatenate([rows_times(matrix, rows, both) for rows in blocks_of(v.shape[0])], axis=0)


def put_split(pair, value, *at):
    index = at if at else (...,)
    pair[0][index], pair[1][index] = split(value)


def first_kernel(odd, rhs, lower, upper, inverse, w, e0, e1, n0, n1, b_in, e_in, n_in, b_sem, e_sem, n_sem):
    cuts = blocks_of(inverse.shape[0])
    is_odd = odd[0] == 1
    b_copy = pltpu.make_async_copy(rhs, b_in, b_sem)
    b_copy.start()
    e_copies, n_copies = [], []
    for k, rows in enumerate(cuts):
        copy = pltpu.make_async_copy(inverse.at[rows], e_in.at[rows], e_sem.at[k])
        copy.start()
        e_copies.append(copy)
    for k, rows in enumerate(cuts):
        low = pltpu.make_async_copy(lower.at[rows], n_in.at[rows], n_sem.at[k])
        up = pltpu.make_async_copy(upper.at[rows], n_in.at[rows], n_sem.at[k])
        pl.when(is_odd)(low.start)
        pl.when(jnp.logical_not(is_odd))(up.start)
        n_copies.append(low)
    b_copy.wait()
    both = stack(b_in[...])
    for k, rows in enumerate(cuts):
        e_copies[k].wait()
        put_split((e0, e1), e_in[rows], rows)
        w[rows] = rows_times((e0, e1), rows, both)
    for k, rows in enumerate(cuts):
        n_copies[k].wait()
        put_split((n0, n1), n_in[rows], rows)


def first_pair_kernel(odd, w, near, n0, n1, e0, e1, out):
    out[0] = w[...]
    out[1] = w[...] - times((e0, e1), times((n0, n1), near[1 - odd[0]]))


def far_block_kernel(odd, _, lower, upper, e0, e1, h, f0, f1, h0, h1):
    cols = h.shape[2]
    for k in range(h.shape[0]):
        at = pl.ds(k * cols, cols)
        far = jnp.where(odd[0] == 1, upper[:, at], lower[:, at])
        put_split((f0, f1), far, slice(None), at)
        product = times((e0, e1), far)
        h[k] = product
        put_split((h0, h1), product, slice(None), at)


def near_block_kernel(_, diag, e0, e1, n0, n1, d0, d1, j0, j1):
    cols = ROWS
    for k in range(0, diag.shape[1], cols):
        at = pl.ds(k, cols)
        put_split((d0, d1), diag[:, at], slice(None), at)
        both = jnp.concatenate([n0[:, at], n1[:, at]], axis=1)
        for rows in blocks_of(diag.shape[0]):
            put_split((j0, j1), rows_times((e0, e1), rows, both), rows, at)


def second_kernel(sent, got, h0, h1, s):
    s[...] = sent[1] - times((h0, h1), got[0])


def k_kernel(sent, got, k_in, h0, h1, f, s_far, k0, k1):
    cols = k_in.shape[2]
    for i in range(k_in.shape[0]):
        put_split((k0, k1), k_in[i], slice(None), pl.ds(i * cols, cols))
    value = got[1] - times((k0, k1), sent[0])
    s_far[...] = value
    f[...] = times((h0, h1), value)


def part_kernel(odd, near, j0, j1, out):
    out[...] = times((j0, j1), near[1 - odd[0]])


def parts_kernel(odd, m, near, j0, j1, out):
    out[0] = m[...]
    out[1] = times((j0, j1), near[1 - odd[0]])


def pair_kernel(odd, w, near, j0, j1, out):
    out[0] = w[...]
    out[1] = w[...] - times((j0, j1), near[1 - odd[0]])


def seconds_kernel(sent, got, h0, h1, k0, k1, pair, s_far):
    value = got[1] - times((k0, k1), sent[0])
    s_far[...] = value
    pair[0] = sent[1] - times((h0, h1), got[0])
    pair[1] = times((h0, h1), value)


def both_parts_kernel(near, j0, j1, out):
    out[0] = times((j0, j1), near[0])
    out[1] = times((j0, j1), near[1])


def step(s, s_far, sent, got, r, H, K, D, F, d, rest):
    change = s[...] + sent[1] + times(H, got[0])
    far = s_far[...] + got[1] + times(K, sent[0])
    d[...] = change
    rest[...] = r[...] - times(D, change) - times(F, far)


def step_kernel(s, s_far, sent, got, r, h0, h1, k0, k1, d0, d1, f0, f1, d, rest):
    step(s, s_far, sent, got, r, (h0, h1), (k0, k1), (d0, d1), (f0, f1), d, rest)


def pair_step_kernel(pair, s_far, sent, got, r, h0, h1, k0, k1, d0, d1, f0, f1, d, rest):
    step(pair.at[0], s_far, sent, got, r, (h0, h1), (k0, k1), (d0, d1), (f0, f1), d, rest)


def residual_kernel(odd, near, rest, n0, n1, e0, e1, r, w):
    value = rest[...] - times((n0, n1), near[1 - odd[0]])
    r[...] = value
    w[...] = times((e0, e1), value)


def last_kernel(odd, near, rest, n0, n1, first, d, x, r):
    r[0] = rest[...] - times((n0, n1), near[1 - odd[0]])
    x[0] = first[...] + d[...]


def call(kernel, outs, *args, specs=None, scratch=(), limit=16, products=1):
    return pl.pallas_call(
        kernel,
        out_shape=[jax.ShapeDtypeStruct(shape, dtype) for shape, dtype in outs],
        in_specs=specs or [SMEM if a.ndim == 1 else VMEM for a in args],
        out_specs=[VMEM] * len(outs),
        scratch_shapes=list(scratch),
        compiler_params=pltpu.CompilerParams(vmem_limit_bytes=limit * 1024 * 1024),
        cost_estimate=pl.CostEstimate(flops=products * COST, bytes_accessed=2**20, transcendentals=0),
    )(*args)


def local(right_side, diag_blocks, lower_blocks, upper_blocks, approx_inverse):
    count = lax.axis_size(AXIS)
    near_groups = [[i, i + 1] for i in range(0, count, 2)]
    near_pairs = [(i, i ^ 1) for i in range(count)]
    far_pairs = [(i, ((i + 1) ^ 1) - 1) for i in range(count)]
    far_pairs = [(i, j % count) for i, j in far_pairs]

    def near(v):
        return lax.all_gather(v, AXIS, axis_index_groups=near_groups)

    def swap_near(v):
        return lax.ppermute(v, AXIS, near_pairs)

    def far(v):
        return lax.ppermute(v, AXIS, far_pairs)

    odd = (lax.axis_index(AXIS) % 2).astype(jnp.int32).reshape(1)
    b, lower, upper, diag, inverse = (a[0] for a in (right_side, lower_blocks, upper_blocks, diag_blocks, approx_inverse))
    size, cols = b.shape
    cuts = size // ROWS
    vec = ((size, cols), F32)
    two = ((2, size, cols), F32)
    half = [((size, size), BF16)] * 2
    square = pltpu.VMEM((size, size), F32)
    dma = pltpu.SemaphoreType.DMA

    w, *mats = call(
        first_kernel, [vec] + half * 2, odd, *(pltpu.with_memory_space_constraint(a, pltpu.HBM) for a in (b, lower, upper, inverse)), specs=[SMEM] + [HBM] * 4,
        scratch=[pltpu.VMEM((size, cols), F32), square, square, dma(()), dma((cuts,)), dma((cuts,))], limit=16,
    )
    E, N = mats[:2], mats[2:]
    (sent,) = call(first_pair_kernel, [two], odd, w, near(w), *N, *E)
    got = far(sent)
    h, *mats = call(
        far_block_kernel, [((size // cols, size, cols), F32)] + half * 2, odd, sent, lower, upper, *E,
        specs=[SMEM, ANY] + [VMEM] * 4, products=5,
    )
    F, H = mats[:2], mats[2:]
    k_in = far(h)
    mats = call(near_block_kernel, half * 2, h, diag, *E, *N, specs=[ANY] + [VMEM] * 5, products=5)
    D, J = mats[:2], mats[2:]

    (s,) = call(second_kernel, [vec], sent, got, *H)
    (m,) = call(part_kernel, [vec], odd, near(s), *J)
    f, s_far, *K = call(k_kernel, [vec, vec] + half, sent, got, k_in, *H)
    (parts,) = call(parts_kernel, [two], odd, m, near(f), *J)
    d1, rest = call(step_kernel, [vec, vec], s, s_far, parts, far(parts), b, *H, *K, *D, *F)

    r, w = call(residual_kernel, [vec, vec], odd, near(d1), rest, *N, *E)
    (sent,) = call(pair_kernel, [two], odd, w, near(w), *J)
    pair, s_far = call(seconds_kernel, [two, vec], sent, far(sent), *H, *K)
    (parts,) = call(both_parts_kernel, [two], swap_near(pair), *J)
    d2, rest = call(pair_step_kernel, [vec, vec], pair, s_far, parts, far(parts), r, *H, *K, *D, *F)
    one = ((1, size, cols), F32)
    return tuple(call(last_kernel, [one, one], odd, near(d2), rest, *N, d1, d2))


def solution(mesh):
    spec = P(AXIS, None, None)
    return jax.shard_map(local, mesh=mesh, in_specs=(spec,) * 5, out_specs=(spec, spec), check_vma=False)
```

time: 256 us -> 116 us (0.45)
  waiting for transfers between devices: 154 us -> 43.1 us
  local copies, waits for them, and re-layouts: 35.6 us -> 0.67 us
  starting transfers between devices: 0.25 us -> 18.7 us
  between operations: 14.3 us -> 0.82 us
  blocking collectives: 28.1 us -> 36.3 us
  Pallas kernels: 21.9 us -> 15.8 us
    all_gather x6 -> x0, waiting for transfers between devices: 154 us -> none  [the longest x4 111 us: far(): return lax.all_gather(v, AXIS, axis_index_groups=far_groups)]
    ppermute x0 -> x6, waiting for transfers between devices: none -> 43.1 us  [the longest x5 41.6 us: far(): return lax.ppermute(v, AXIS, far_pairs)]
    unnamed x88 -> x8, local copies, waits for them, and re-layouts: 35.6 us -> 0.67 us
    ppermute x0 -> x6, starting transfers between devices: none -> 18.7 us  [the longest x5 11.3 us: far(): return lax.ppermute(v, AXIS, far_pairs)]
    all_gather x4 -> x6, blocking collectives: 28.1 us -> 36.3 us  [near(): return lax.all_gather(v, AXIS, axis_index_groups=near_groups)]
    pallas_call x11 -> x15, Pallas kernels: 21.9 us -> 15.8 us  [call(): pl.pallas_call(kernel, out_shape=[jax.ShapeDtypeStruct(shape, dtype) for...]
  transfers between devices with their start and end apart: 6 -> 6, of which waited for: 6 -> 5; matrix products, arithmetic and copies ran while one was open for 0% -> 0% of each run, Pallas kernels for 0% -> 2%
where the time goes in v2:
time: 116 us; the launch traced here: 115 us
  waiting for transfers between devices  43.1 us (37%)
  blocking collectives  36.3 us (31%)
  starting transfers between devices  18.7 us (16%)
  Pallas kernels  15.8 us (14%)
    ppermute x5, waiting for transfers between devices, far(): return lax.ppermute(v, AXIS, far_pairs)  41.6 us
    all_gather x6, blocking collectives, near(): return lax.all_gather(v, AXIS, axis_index_groups=near_groups)  36.3 us
    pallas_call x15, Pallas kernels, call(): pl.pallas_call(kernel, out_shape=[jax.ShapeDtypeStruct(shape, dtype) for...  15.8 us
    ppermute x5, starting transfers between devices, far(): return lax.ppermute(v, AXIS, far_pairs)  11.3 us
    ppermute x1, starting transfers between devices, swap_near(): return lax.ppermute(v, AXIS, near_pairs)  7.41 us
  transfers between devices with their start and end apart: 6, of which 5 were waited for; matrix products, arithmetic and copies ran while one was open for 0% of the time, Pallas kernels for 2%

profile of v2, /device:TPU:1, one launch (start us, length us, event | category | flops | bytes accessed | tf_op | source)
XLA Modules:
  0.0 115.4 jit_solution(17914076903906948360)
XLA Ops:
  0.6 3.0 %shard_map.68 = (f32[512,128]{1,0:T(8,128)S(1)}, bf16[512,512]{1,0:T(8,128)(2,1)S(1)}, bf16[512,512]{1,0:T(8,128)(2,1)S(1)}, bf16[512,512]{1,0:T(8,128)(2,1)S(1)}, bf16[512,512]{1,0:T(8,128)(2,1)S(1)}) custom-call(s32[1]{0:T(128)} %bitcast.odd, f32[512,128]{1,0:T(8,128)} %bitcast.18, f32[512,512]{1,0:T(8,128)} %bitcast.20, f32[512,512]{1,0:T(8,128)} %bitcast.22, ...), custom_call_target="tpu_custom_call" | custom-call | flops 268435456 | bytes 1048576 | tf_op jit(solution)/shard_map/pallas_call | solution.py:168
  3.6 8.6 %all-gather = f32[1024,128]{1,0:T(8,128)S(1)} all-gather(f32[512,128]{1,0:T(8,128)S(1)} %get-tuple-element.28.w), channel_id=2, replica_groups={{0,1},{2,3},{4,5},{6,7},{8,9},{10,11},{12,13},{14,15},{16,17},{18,19},{..., dimensions={0}, use_global_device_ids=true | all-gather | bytes 786432 | tf_op jit(solution)/shard_map/all_gather | solution.py:187
  12.2 0.0 copy-start.1
  12.2 0.0 copy-start.2
  12.2 0.9 shard_map.69._.sent
  13.1 0.3 copy-done.1
  13.4 0.3 copy-done.2
  13.8 0.0 copy-start.3
  13.8 1.3 %shard_map.70 = (f32[4,512,128]{2,1,0:T(8,128)S(1)}, bf16[512,512]{1,0:T(8,128)(2,1)S(1)}, bf16[512,512]{1,0:T(8,128)(2,1)S(1)}, bf16[512,512]{1,0:T(8,128)(2,1)S(1)}, bf16[512,512]{1,0:T(8,128)(2,1)S(1)}) custom-call(s32[1]{0:T(128)} %bitcast.odd, f32[2,512,128]{2,1,0:T(8,128)S(1)} %shard_map.69._.sent, f32[512,512]{1,0:T(8,128)S(1)} %bitcast.21, ...), custom_call_target="tpu_custom_call" | custom-call | flops 1342177280 | bytes 1048576 | tf_op jit(solution)/shard_map/pallas_call | solution.py:168
  15.1 1.9 %collective-permute-start.1 = (f32[4,512,128]{2,1,0:T(8,128)S(1)}, f32[4,512,128]{2,1,0:T(8,128)S(1)}, u32[]{:S(2)}, u32[]{:S(2)}) collective-permute-start(f32[4,512,128]{2,1,0:T(8,128)S(1)} %get-tuple-element.35._), channel_id=1, source_target_pairs={{0,511},{1,2},{2,1},{3,4},{4,3},{5,6},{6,5},{7,8},{8,7},{9,10},{10... | collective-permute-start | bytes 3145736 | tf_op jit(solution)/shard_map/ppermute | solution.py:193
  17.0 3.6 %collective-permute-start = (f32[2,512,128]{2,1,0:T(8,128)S(1)}, f32[2,512,128]{2,1,0:T(8,128)S(1)}, u32[]{:S(2)}, u32[]{:S(2)}) collective-permute-start(f32[2,512,128]{2,1,0:T(8,128)S(1)} %shard_map.69._.sent), channel_id=1, source_target_pairs={{0,511},{1,2},{2,1},{3,4},{4,3},{5,6},{6,5},{7,8},{8,7},{9,10},{10... | collective-permute-start | bytes 1572872 | tf_op jit(solution)/shard_map/ppermute | solution.py:193
  20.7 0.0 copy-done.3
  20.7 1.5 %shard_map.73 = (bf16[512,512]{1,0:T(8,128)(2,1)S(1)}, bf16[512,512]{1,0:T(8,128)(2,1)S(1)}, bf16[512,512]{1,0:T(8,128)(2,1)S(1)}, bf16[512,512]{1,0:T(8,128)(2,1)S(1)}) custom-call(f32[4,512,128]{2,1,0:T(8,128)S(1)} %get-tuple-element.35._, f32[512,512]{1,0:T(8,128)S(1)} %bitcast.24, bf16[512,512]{1,0:T(8,128)(2,1)S(1)} %get-tuple-element.31.e0, ...), custom_call_target="tpu_custom_call" | custom-call | flops 1342177280 | bytes 1048576 | tf_op jit(solution)/shard_map/pallas_call | solution.py:168
  22.2 14.9 %collective-permute-done.got = f32[2,512,128]{2,1,0:T(8,128)S(1)} collective-permute-done((f32[2,512,128]{2,1,0:T(8,128)S(1)}, f32[2,512,128]{2,1,0:T(8,128)S(1)}, u32[]{:S(2)}, u32[]{:S(2)}) %collective-permute-start) | collective-permute-done | bytes 524320 | tf_op jit(solution)/shard_map/ppermute | solution.py:193
  37.1 0.5 shard_map.71.s
  37.6 8.7 %all-gather.1 = f32[1024,128]{1,0:T(8,128)S(1)} all-gather(f32[512,128]{1,0:T(8,128)S(1)} %shard_map.71.s), channel_id=3, replica_groups={{0,1},{2,3},{4,5},{6,7},{8,9},{10,11},{12,13},{14,15},{16,17},{18,19},{..., dimensions={0}, use_global_device_ids=true | all-gather | bytes 786432 | tf_op jit(solution)/shard_map/all_gather | solution.py:187
  46.3 0.4 shard_map.74.m
  46.7 0.0 collective-permute-done.1.k_in
  46.7 0.9 shard_map.72
  47.6 2.2 %all-gather.2 = f32[1024,128]{1,0:T(8,128)S(1)} all-gather(f32[512,128]{1,0:T(8,128)S(1)} %get-tuple-element.39), channel_id=4, replica_groups={{0,1},{2,3},{4,5},{6,7},{8,9},{10,11},{12,13},{14,15},{16,17},{18,19},{..., dimensions={0}, use_global_device_ids=true | all-gather | bytes 786432 | tf_op jit(solution)/shard_map/all_gather | solution.py:187
  49.8 0.0 copy-start
  49.8 0.5 shard_map.75.sent
  50.3 1.9 %collective-permute-start.2 = (f32[2,512,128]{2,1,0:T(8,128)S(1)}, f32[2,512,128]{2,1,0:T(8,128)S(1)}, u32[]{:S(2)}, u32[]{:S(2)}) collective-permute-start(f32[2,512,128]{2,1,0:T(8,128)S(1)} %shard_map.75.sent), channel_id=1, source_target_pairs={{0,511},{1,2},{2,1},{3,4},{4,3},{5,6},{6,5},{7,8},{8,7},{9,10},{10... | collective-permute-start | bytes 1572872 | tf_op jit(solution)/shard_map/ppermute | solution.py:193
  52.3 8.9 %collective-permute-done.2.got = f32[2,512,128]{2,1,0:T(8,128)S(1)} collective-permute-done((f32[2,512,128]{2,1,0:T(8,128)S(1)}, f32[2,512,128]{2,1,0:T(8,128)S(1)}, u32[]{:S(2)}, u32[]{:S(2)}) %collective-permute-start.2) | collective-permute-done | bytes 524320 | tf_op jit(solution)/shard_map/ppermute | solution.py:193
  61.1 0.0 copy-done
  61.1 1.3 %shard_map.76 = (f32[512,128]{1,0:T(8,128)S(1)}, f32[512,128]{1,0:T(8,128)S(1)}) custom-call(f32[512,128]{1,0:T(8,128)S(1)} %shard_map.71.s, f32[512,128]{1,0:T(8,128)S(1)} %get-tuple-element.36.s_far, f32[2,512,128]{2,1,0:T(8,128)S(1)} %shard_map.75.sent, f32[2,512,128]{2,1,0:T(8,128)S(1)} %collective-permute-done.2.got, f32[512,128]{1,0:T(8,128)S(1)} %bitcast.19, ...), custom_call_target="tpu_custom_call" | custom-call | flops 268435456 | bytes 1048576 | tf_op jit(solution)/shard_map/pallas_call | solution.py:168
  62.4 7.3 %all-gather.3 = f32[1024,128]{1,0:T(8,128)S(1)} all-gather(f32[512,128]{1,0:T(8,128)S(1)} %get-tuple-element.46.first), channel_id=5, replica_groups={{0,1},{2,3},{4,5},{6,7},{8,9},{10,11},{12,13},{14,15},{16,17},{18,19},{..., dimensions={0}, use_global_device_ids=true | all-gather | bytes 786432 | tf_op jit(solution)/shard_map/all_gather | solution.py:187
  69.8 0.9 shard_map.77
  70.6 2.2 %all-gather.4 = f32[1024,128]{1,0:T(8,128)S(1)} all-gather(f32[512,128]{1,0:T(8,128)S(1)} %get-tuple-element.48.w), channel_id=6, replica_groups={{0,1},{2,3},{4,5},{6,7},{8,9},{10,11},{12,13},{14,15},{16,17},{18,19},{..., dimensions={0}, use_global_device_ids=true | all-gather | bytes 786432 | tf_op jit(solution)/shard_map/all_gather | solution.py:187
  72.8 0.5 shard_map.78.sent
  73.3 1.9 %collective-permute-start.3 = (f32[2,512,128]{2,1,0:T(8,128)S(1)}, f32[2,512,128]{2,1,0:T(8,128)S(1)}, u32[]{:S(2)}, u32[]{:S(2)}) collective-permute-start(f32[2,512,128]{2,1,0:T(8,128)S(1)} %shard_map.78.sent), channel_id=1, source_target_pairs={{0,511},{1,2},{2,1},{3,4},{4,3},{5,6},{6,5},{7,8},{8,7},{9,10},{10... | collective-permute-start | bytes 1572872 | tf_op jit(solution)/shard_map/ppermute | solution.py:193
  75.2 8.9 %collective-permute-done.3.got = f32[2,512,128]{2,1,0:T(8,128)S(1)} collective-permute-done((f32[2,512,128]{2,1,0:T(8,128)S(1)}, f32[2,512,128]{2,1,0:T(8,128)S(1)}, u32[]{:S(2)}, u32[]{:S(2)}) %collective-permute-start.3) | collective-permute-done | bytes 524320 | tf_op jit(solution)/shard_map/ppermute | solution.py:193
  84.1 1.0 shard_map.79
  85.1 7.4 %collective-permute-start.4 = (f32[2,512,128]{2,1,0:T(8,128)S(1)}, f32[2,512,128]{2,1,0:T(8,128)S(1)}, u32[]{:S(2)}, u32[]{:S(2)}) collective-permute-start(f32[2,512,128]{2,1,0:T(8,128)S(1)} %get-tuple-element.49.pair), channel_id=1, source_target_pairs={{0,1},{1,0},{2,3},{3,2},{4,5},{5,4},{6,7},{7,6},{8,9},{9,8},{10,11... | collective-permute-start | bytes 1572872 | tf_op jit(solution)/shard_map/ppermute | solution.py:190
  92.5 1.5 %collective-permute-done.4.near = f32[2,512,128]{2,1,0:T(8,128)S(1)} collective-permute-done((f32[2,512,128]{2,1,0:T(8,128)S(1)}, f32[2,512,128]{2,1,0:T(8,128)S(1)}, u32[]{:S(2)}, u32[]{:S(2)}) %collective-permute-start.4) | collective-permute-done | bytes 524320 | tf_op jit(solution)/shard_map/ppermute | solution.py:190
  94.0 0.7 shard_map.80.sent
  94.8 1.9 %collective-permute-start.5 = (f32[2,512,128]{2,1,0:T(8,128)S(1)}, f32[2,512,128]{2,1,0:T(8,128)S(1)}, u32[]{:S(2)}, u32[]{:S(2)}) collective-permute-start(f32[2,512,128]{2,1,0:T(8,128)S(1)} %shard_map.80.sent), channel_id=1, source_target_pairs={{0,511},{1,2},{2,1},{3,4},{4,3},{5,6},{6,5},{7,8},{8,7},{9,10},{10... | collective-permute-start | bytes 1572872 | tf_op jit(solution)/shard_map/ppermute | solution.py:193
  96.7 8.9 %collective-permute-done.5.got = f32[2,512,128]{2,1,0:T(8,128)S(1)} collective-permute-done((f32[2,512,128]{2,1,0:T(8,128)S(1)}, f32[2,512,128]{2,1,0:T(8,128)S(1)}, u32[]{:S(2)}, u32[]{:S(2)}) %collective-permute-start.5) | collective-permute-done | bytes 524320 | tf_op jit(solution)/shard_map/ppermute | solution.py:193
  105.6 1.3 %shard_map.81 = (f32[512,128]{1,0:T(8,128)S(1)}, f32[512,128]{1,0:T(8,128)S(1)}) custom-call(f32[2,512,128]{2,1,0:T(8,128)S(1)} %get-tuple-element.49.pair, f32[512,128]{1,0:T(8,128)S(1)} %get-tuple-element.50.s_far, f32[2,512,128]{2,1,0:T(8,128)S(1)} %shard_map.80.sent, f32[2,512,128]{2,1,0:T(8,128)S(1)} %collective-permute-done.5.got, ...), custom_call_target="tpu_custom_call" | custom-call | flops 268435456 | bytes 1048576 | tf_op jit(solution)/shard_map/pallas_call | solution.py:168
  106.9 7.3 %all-gather.5 = f32[1024,128]{1,0:T(8,128)S(1)} all-gather(f32[512,128]{1,0:T(8,128)S(1)} %get-tuple-element.52.d), channel_id=7, replica_groups={{0,1},{2,3},{4,5},{6,7},{8,9},{10,11},{12,13},{14,15},{16,17},{18,19},{..., dimensions={0}, use_global_device_ids=true | all-gather | bytes 786432 | tf_op jit(solution)/shard_map/all_gather | solution.py:187
  114.2 1.2 %shard_map.82 = (f32[1,512,128]{2,1,0:T(8,128)}, f32[1,512,128]{2,1,0:T(8,128)}) custom-call(s32[1]{0:T(128)} %bitcast.odd, f32[2,512,128]{2,1,0:T(8,128)S(1)} %bitcast.12, f32[512,128]{1,0:T(8,128)S(1)} %get-tuple-element.53.rest, bf16[512,512]{1,0:T(8,128)(2,1)S(1)} %get-tuple-element.29.n0, bf16[512,512]{1,0:T(8,128)(2,1)S(1)} %get-tuple-element.30.n1, ...), custom_call_target="tpu_custom_call" | custom-call | flops 268435456 | bytes 1048576 | tf_op jit(solution)/shard_map/pallas_call | solution.py:168
Async XLA Ops:
  12.2 1.2 %copy-start.1 = (f32[1,512,512]{2,1,0:T(8,128)S(1)}, f32[1,512,512]{2,1,0:T(8,128)}, u32[]{:S(2)}) copy-start(f32[1,512,512]{2,1,0:T(8,128)} %param.7) | copy-start | bytes 3145732
  12.2 1.5 %copy-start.2 = (f32[1,512,512]{2,1,0:T(8,128)S(1)}, f32[1,512,512]{2,1,0:T(8,128)}, u32[]{:S(2)}) copy-start(f32[1,512,512]{2,1,0:T(8,128)} %param.8) | copy-start | bytes 3145732
  13.8 6.9 %copy-start.3 = (f32[1,512,512]{2,1,0:T(8,128)S(1)}, f32[1,512,512]{2,1,0:T(8,128)}, u32[]{:S(2)}) copy-start(f32[1,512,512]{2,1,0:T(8,128)} %param.6) | copy-start | bytes 3145732
  15.1 31.6 %collective-permute-start.1 = (f32[4,512,128]{2,1,0:T(8,128)S(1)}, f32[4,512,128]{2,1,0:T(8,128)S(1)}, u32[]{:S(2)}, u32[]{:S(2)}) collective-permute-start(f32[4,512,128]{2,1,0:T(8,128)S(1)} %get-tuple-element.35._), channel_id=1, source_target_pairs={{0,511},{1,2},{2,1},{3,4},{4,3},{5,6},{6,5},{7,8},{8,7},{9,10},{10... | collective-permute-start | bytes 3145736 | tf_op jit(solution)/shard_map/ppermute | solution.py:193
  17.0 20.1 %collective-permute-start = (f32[2,512,128]{2,1,0:T(8,128)S(1)}, f32[2,512,128]{2,1,0:T(8,128)S(1)}, u32[]{:S(2)}, u32[]{:S(2)}) collective-permute-start(f32[2,512,128]{2,1,0:T(8,128)S(1)} %shard_map.69._.sent), channel_id=1, source_target_pairs={{0,511},{1,2},{2,1},{3,4},{4,3},{5,6},{6,5},{7,8},{8,7},{9,10},{10... | collective-permute-start | bytes 1572872 | tf_op jit(solution)/shard_map/ppermute | solution.py:193
  49.8 11.3 %copy-start = (f32[1,512,128]{2,1,0:T(8,128)S(1)}, f32[1,512,128]{2,1,0:T(8,128)}, u32[]{:S(2)}) copy-start(f32[1,512,128]{2,1,0:T(8,128)} %param.5) | copy-start | bytes 786436
  50.3 10.8 %collective-permute-start.2 = (f32[2,512,128]{2,1,0:T(8,128)S(1)}, f32[2,512,128]{2,1,0:T(8,128)S(1)}, u32[]{:S(2)}, u32[]{:S(2)}) collective-permute-start(f32[2,512,128]{2,1,0:T(8,128)S(1)} %shard_map.75.sent), channel_id=1, source_target_pairs={{0,511},{1,2},{2,1},{3,4},{4,3},{5,6},{6,5},{7,8},{8,7},{9,10},{10... | collective-permute-start | bytes 1572872 | tf_op jit(solution)/shard_map/ppermute | solution.py:193
  73.3 10.8 %collective-permute-start.3 = (f32[2,512,128]{2,1,0:T(8,128)S(1)}, f32[2,512,128]{2,1,0:T(8,128)S(1)}, u32[]{:S(2)}, u32[]{:S(2)}) collective-permute-start(f32[2,512,128]{2,1,0:T(8,128)S(1)} %shard_map.78.sent), channel_id=1, source_target_pairs={{0,511},{1,2},{2,1},{3,4},{4,3},{5,6},{6,5},{7,8},{8,7},{9,10},{10... | collective-permute-start | bytes 1572872 | tf_op jit(solution)/shard_map/ppermute | solution.py:193
  85.1 8.9 %collective-permute-start.4 = (f32[2,512,128]{2,1,0:T(8,128)S(1)}, f32[2,512,128]{2,1,0:T(8,128)S(1)}, u32[]{:S(2)}, u32[]{:S(2)}) collective-permute-start(f32[2,512,128]{2,1,0:T(8,128)S(1)} %get-tuple-element.49.pair), channel_id=1, source_target_pairs={{0,1},{1,0},{2,3},{3,2},{4,5},{5,4},{6,7},{7,6},{8,9},{9,8},{10,11... | collective-permute-start | bytes 1572872 | tf_op jit(solution)/shard_map/ppermute | solution.py:190
  94.8 10.8 %collective-permute-start.5 = (f32[2,512,128]{2,1,0:T(8,128)S(1)}, f32[2,512,128]{2,1,0:T(8,128)S(1)}, u32[]{:S(2)}, u32[]{:S(2)}) collective-permute-start(f32[2,512,128]{2,1,0:T(8,128)S(1)} %shard_map.80.sent), channel_id=1, source_target_pairs={{0,511},{1,2},{2,1},{3,4},{4,3},{5,6},{6,5},{7,8},{8,7},{9,10},{10... | collective-permute-start | bytes 1572872 | tf_op jit(solution)/shard_map/ppermute | solution.py:193

commit v3 on v2

v3 whole, which is shorter than its diff:
```python
import jax
import jax.numpy as jnp
from jax import lax
from jax.experimental import pallas as pl
from jax.experimental.pallas import tpu as pltpu
from jax.sharding import PartitionSpec as P

F32 = jnp.float32
BF16 = jnp.bfloat16
VMEM = pl.BlockSpec(memory_space=pltpu.VMEM)
SMEM = pl.BlockSpec(memory_space=pltpu.SMEM)
HBM = pl.BlockSpec(memory_space=pltpu.HBM)
ANY = pl.BlockSpec(memory_space=pl.ANY)
AXIS = "station"
ROWS = 128
COST = 8 * 512 * 512 * 128


def split(v):
    high = v.astype(BF16)
    return high, (v - high.astype(F32)).astype(BF16)


def stack(v):
    return jnp.concatenate(split(v), axis=1)


def rows_times(matrix, rows, both):
    out = jnp.dot(matrix[0][rows, :], both, preferred_element_type=F32)
    out += jnp.dot(matrix[1][rows, :], both, preferred_element_type=F32)
    n = both.shape[1] // 2
    return out[:, :n] + out[:, n:]


def blocks_of(size):
    return [pl.ds(k, ROWS) for k in range(0, size, ROWS)]


def times(matrix, v):
    both = stack(v)
    return jnp.concatenate([rows_times(matrix, rows, both) for rows in blocks_of(v.shape[0])], axis=0)


def put_split(pair, value, *at):
    index = at if at else (...,)
    pair[0][index], pair[1][index] = split(value)


def fetch(source, into, sems):
    copies = []
    for k, rows in enumerate(blocks_of(into.shape[0])):
        copy = pltpu.make_async_copy(source.at[rows], into.at[rows], sems.at[k])
        copy.start()
        copies.append(copy)
    return copies


def fetch_either(is_odd, odd_source, even_source, into, sems):
    copies = []
    for k, rows in enumerate(blocks_of(into.shape[0])):
        copy = pltpu.make_async_copy(odd_source.at[rows], into.at[rows], sems.at[k])
        other = pltpu.make_async_copy(even_source.at[rows], into.at[rows], sems.at[k])
        pl.when(is_odd)(copy.start)
        pl.when(jnp.logical_not(is_odd))(other.start)
        copies.append(copy)
    return copies


def first_kernel(rhs, inverse, w, e0, e1, b_in, e_in, b_sem, e_sem):
    b_copies = fetch(rhs, b_in, b_sem)
    e_copies = fetch(inverse, e_in, e_sem)
    for copy in b_copies:
        copy.wait()
    both = stack(b_in[...])
    for copy, rows in zip(e_copies, blocks_of(inverse.shape[0])):
        copy.wait()
        put_split((e0, e1), e_in[rows], rows)
        w[rows] = rows_times((e0, e1), rows, both)


def blocks_kernel(odd, _, lower, upper, diag, e0, e1, h, h0, h1, j0, j1, n0, n1, f0, f1, d0, d1, n_in, f_in, d_in, n_sem, f_sem, d_sem):
    is_odd = odd[0] == 1
    n_copies = fetch_either(is_odd, lower, upper, n_in, n_sem)
    f_copies = fetch_either(is_odd, upper, lower, f_in, f_sem)
    d_copies = fetch(diag, d_in, d_sem)
    cuts = blocks_of(diag.shape[0])
    cols = h.shape[2]

    def product(parts, to, whole=None):
        for k in range(h.shape[0]):
            at = pl.ds(k * cols, cols)
            both = jnp.concatenate([parts[0][:, at], parts[1][:, at]], axis=1)
            for rows in cuts:
                value = rows_times((e0, e1), rows, both)
                put_split(to, value, rows, at)
                if whole is not None:
                    whole[k, rows] = value

    for copies, source, to in ((n_copies, n_in, (n0, n1)), (f_copies, f_in, (f0, f1)), (d_copies, d_in, (d0, d1))):
        for copy, rows in zip(copies, cuts):
            copy.wait()
            put_split(to, source[rows], rows)
    product((n0, n1), (j0, j1))
    product((f0, f1), (h0, h1), h)


def near_part_kernel(odd, w, near, j0, j1, out):
    out[...] = w[...] - times((j0, j1), near[1 - odd[0]])


def second_kernel(part, got, h0, h1, s):
    s[...] = part[...] - times((h0, h1), got[...])


def part_kernel(odd, near, j0, j1, h, out, h_out):
    out[...] = times((j0, j1), near[1 - odd[0]])


def product_kernel(v, h0, h1, out):
    out[...] = times((h0, h1), v[...])


def parts_kernel(odd, m, near, j0, j1, out):
    out[0] = m[...]
    out[1] = times((j0, j1), near[1 - odd[0]])


def pair_kernel(odd, w, near, j0, j1, out):
    out[0] = w[...]
    out[1] = w[...] - times((j0, j1), near[1 - odd[0]])


def split_kernel(k_in, k0, k1):
    cols = k_in.shape[2]
    for i in range(k_in.shape[0]):
        put_split((k0, k1), k_in[i], slice(None), pl.ds(i * cols, cols))


def sent_kernel(sent, k0, k1, out):
    out[...] = times((k0, k1), sent[0])


def seconds_kernel(sent, got, effect, h0, h1, pair, s_far):
    value = got[1] - effect[...]
    s_far[...] = value
    pair[0] = sent[1] - times((h0, h1), got[0])
    pair[1] = times((h0, h1), value)


def both_parts_kernel(near, j0, j1, out):
    out[0] = times((j0, j1), near[0])
    out[1] = times((j0, j1), near[1])


def step_kernel(s, s_far, effect, sent, got, r, h0, h1, d0, d1, f0, f1, d, rest):
    change = s[...] + sent[1] + times((h0, h1), got[0])
    far = s_far[...] + got[1] + effect[...]
    d[...] = change
    rest[...] = r[...] - times((d0, d1), change) - times((f0, f1), far)


def pair_step_kernel(pair, s_far, effect, sent, got, r, h0, h1, d0, d1, f0, f1, d, rest):
    step_kernel(pair.at[0], s_far, effect, sent, got, r, h0, h1, d0, d1, f0, f1, d, rest)


def residual_kernel(odd, near, rest, n0, n1, e0, e1, r, w):
    value = rest[...] - times((n0, n1), near[1 - odd[0]])
    r[...] = value
    w[...] = times((e0, e1), value)


def last_kernel(odd, near, rest, n0, n1, first, d, x, r):
    r[0] = rest[...] - times((n0, n1), near[1 - odd[0]])
    x[0] = first[...] + d[...]


def call(kernel, outs, *args, specs=None, scratch=(), limit=16, products=1, aliases={}, outs_at=None):
    return pl.pallas_call(
        kernel,
        out_shape=[jax.ShapeDtypeStruct(shape, dtype) for shape, dtype in outs],
        in_specs=specs or [SMEM if a.ndim == 1 else VMEM for a in args],
        out_specs=outs_at or [VMEM] * len(outs),
        input_output_aliases=aliases,
        scratch_shapes=list(scratch),
        compiler_params=pltpu.CompilerParams(vmem_limit_bytes=limit * 1024 * 1024),
        cost_estimate=pl.CostEstimate(flops=products * COST, bytes_accessed=2**20, transcendentals=0),
    )(*args)


def local(right_side, diag_blocks, lower_blocks, upper_blocks, approx_inverse):
    count = lax.axis_size(AXIS)
    near_groups = [[i, i + 1] for i in range(0, count, 2)]
    near_pairs = [(i, i ^ 1) for i in range(count)]
    far_pairs = [(i, ((i + 1) ^ 1) - 1) for i in range(count)]
    far_pairs = [(i, j % count) for i, j in far_pairs]

    def near(v):
        return lax.all_gather(v, AXIS, axis_index_groups=near_groups)

    def swap_near(v):
        return lax.ppermute(v, AXIS, near_pairs)

    def far(v):
        return lax.ppermute(v, AXIS, far_pairs)

    odd = (lax.axis_index(AXIS) % 2).astype(jnp.int32).reshape(1)
    b, lower, upper, diag, inverse = (a[0] for a in (right_side, lower_blocks, upper_blocks, diag_blocks, approx_inverse))
    size, cols = b.shape
    cuts = size // ROWS
    vec = ((size, cols), F32)
    two = ((2, size, cols), F32)
    half = [((size, size), BF16)] * 2
    square = pltpu.VMEM((size, size), F32)
    dmas = pltpu.SemaphoreType.DMA((cuts,))
    blocks = ((size // cols, size, cols), F32)

    def in_hbm(*arrays):
        return [pltpu.with_memory_space_constraint(a, pltpu.HBM) for a in arrays]

    w, *E = call(
        first_kernel, [vec] + half, *in_hbm(b, inverse), specs=[HBM] * 2,
        scratch=[pltpu.VMEM((size, cols), F32), square, dmas, dmas],
    )
    w_far = far(w)
    h, *mats = call(
        blocks_kernel, [blocks] + half * 5, odd, w, *in_hbm(lower, upper, diag), *E,
        specs=[SMEM, ANY] + [HBM] * 3 + [VMEM] * 2, scratch=[square] * 3 + [dmas] * 3, products=10,
    )
    H, J, N, F, D = (mats[i:i + 2] for i in range(0, 10, 2))
    (part,) = call(near_part_kernel, [vec], odd, w, near(w), *J)
    (s,) = call(second_kernel, [vec], part, w_far, *H)
    s_far = far(s)
    m, h = call(
        part_kernel, [vec, blocks], odd, near(s), *J, h,
        specs=[SMEM] + [VMEM] * 3 + [ANY], outs_at=[VMEM, ANY], aliases={4: 1},
    )
    k_in = far(h)
    (f,) = call(product_kernel, [vec], s_far, *H, products=20)
    (parts,) = call(parts_kernel, [two], odd, m, near(f), *J)
    got = far(parts)
    K = call(split_kernel, half, k_in)
    (effect,) = call(sent_kernel, [vec], parts, *K)
    d1, rest = call(step_kernel, [vec, vec], s, s_far, effect, parts, got, b, *H, *D, *F)

    r, w = call(residual_kernel, [vec, vec], odd, near(d1), rest, *N, *E)
    (sent,) = call(pair_kernel, [two], odd, w, near(w), *J)
    got = far(sent)
    (effect,) = call(sent_kernel, [vec], sent, *K)
    pair, s_far = call(seconds_kernel, [two, vec], sent, got, effect, *H)
    (parts,) = call(both_parts_kernel, [two], swap_near(pair), *J)
    got = far(parts)
    (effect,) = call(sent_kernel, [vec], parts, *K)
    d2, rest = call(pair_step_kernel, [vec, vec], pair, s_far, effect, parts, got, r, *H, *D, *F)
    one = ((1, size, cols), F32)
    return tuple(call(last_kernel, [one, one], odd, near(d2), rest, *N, d1, d2))


def solution(mesh):
    spec = P(AXIS, None, None)
    return jax.shard_map(local, mesh=mesh, in_specs=(spec,) * 5, out_specs=(spec, spec), check_vma=False)
```

time: 116 us -> 112 us (0.966)
  waiting for transfers between devices: 43.1 us -> 29.5 us
  blocking collectives: 36.3 us -> 42.8 us
  starting transfers between devices: 18.7 us -> 21.5 us
  Pallas kernels: 15.8 us -> 17 us
    ppermute x5 -> x6, waiting for transfers between devices: 41.6 us -> 28 us  [far(): return lax.ppermute(v, AXIS, far_pairs)]
    all_gather x6, blocking collectives: 36.3 us -> 42.8 us  [near(): return lax.all_gather(v, AXIS, axis_index_groups=near_groups)]
    ppermute x5 -> x6, starting transfers between devices: 11.3 us -> 14.1 us  [far(): return lax.ppermute(v, AXIS, far_pairs)]
    pallas_call x15 -> x18, Pallas kernels: 15.8 us -> 17 us  [call(): pl.pallas_call(kernel, out_shape=[jax.ShapeDtypeStruct(shape, dtype) for...]
  transfers between devices with their start and end apart: 6 -> 7, of which waited for: 5 -> 5; matrix products, arithmetic and copies ran while one was open for 0% -> 0% of each run, Pallas kernels for 2% -> 7%
where the time goes in v3:
time: 112 us
  blocking collectives  42.8 us (38%)
  waiting for transfers between devices  29.5 us (26%)
  starting transfers between devices  21.5 us (19%)
  Pallas kernels  17 us (15%)
    all_gather x6, blocking collectives, near(): return lax.all_gather(v, AXIS, axis_index_groups=near_groups)  42.8 us
    ppermute x6, waiting for transfers between devices, far(): return lax.ppermute(v, AXIS, far_pairs)  28 us
    pallas_call x18, Pallas kernels, call(): pl.pallas_call(kernel, out_shape=[jax.ShapeDtypeStruct(shape, dtype) for...  17 us
    ppermute x6, starting transfers between devices, far(): return lax.ppermute(v, AXIS, far_pairs)  14.1 us
    ppermute x1, starting transfers between devices, swap_near(): return lax.ppermute(v, AXIS, near_pairs)  7.4 us
  transfers between devices with their start and end apart: 7, of which 5 were waited for; matrix products, arithmetic and copies ran while one was open for 0% of the time, Pallas kernels for 7%

profile of v3, /device:TPU:1, one launch (start us, length us, event | category | flops | bytes accessed | tf_op | source)
XLA Modules:
  0.0 111.6 jit_solution(6413757025629920309)
XLA Ops:
  0.6 2.4 %shard_map.68 = (f32[512,128]{1,0:T(8,128)S(1)}, bf16[512,512]{1,0:T(8,128)(2,1)S(1)}, bf16[512,512]{1,0:T(8,128)(2,1)S(1)}) custom-call(f32[512,128]{1,0:T(8,128)} %bitcast.18, f32[512,512]{1,0:T(8,128)} %bitcast.20), custom_call_target="tpu_custom_call" | custom-call | flops 268435456 | bytes 1048576 | tf_op jit(solution)/shard_map/pallas_call | solution.py:178
  3.1 4.5 %collective-permute-start = (f32[512,128]{1,0:T(8,128)S(1)}, f32[512,128]{1,0:T(8,128)S(1)}, u32[]{:S(2)}, u32[]{:S(2)}) collective-permute-start(f32[512,128]{1,0:T(8,128)S(1)} %get-tuple-element.28._.w), channel_id=1, source_target_pairs={{0,511},{1,2},{2,1},{3,4},{4,3},{5,6},{6,5},{7,8},{8,7},{9,10},{10... | collective-permute-start | bytes 786440 | tf_op jit(solution)/shard_map/ppermute | solution.py:204
  7.6 14.3 %all-gather = f32[1024,128]{1,0:T(8,128)S(1)} all-gather(f32[512,128]{1,0:T(8,128)S(1)} %get-tuple-element.28._.w), channel_id=2, replica_groups={{0,1},{2,3},{4,5},{6,7},{8,9},{10,11},{12,13},{14,15},{16,17},{18,19},{..., dimensions={0}, use_global_device_ids=true | all-gather | bytes 786432 | tf_op jit(solution)/shard_map/all_gather | solution.py:198
  21.9 4.4 %shard_map.69 = (f32[4,512,128]{2,1,0:T(8,128)S(1)}, bf16[512,512]{1,0:T(8,128)(2,1)S(1)}, bf16[512,512]{1,0:T(8,128)(2,1)S(1)}, bf16[512,512]{1,0:T(8,128)(2,1)...) custom-call(s32[1]{0:T(128)} %bitcast.odd, ...), custom_call_target="tpu_custom_call" | custom-call | flops 2684354560 | bytes 1048576 | tf_op jit(solution)/shard_map/pallas_call | solution.py:178
  26.3 0.5 shard_map.70.part
  26.8 0.0 collective-permute-done.got
  26.8 0.5 shard_map.71.s
  27.3 1.9 %collective-permute-start.1 = (f32[512,128]{1,0:T(8,128)S(1)}, f32[512,128]{1,0:T(8,128)S(1)}, u32[]{:S(2)}, u32[]{:S(2)}) collective-permute-start(f32[512,128]{1,0:T(8,128)S(1)} %shard_map.71.s), channel_id=1, source_target_pairs={{0,511},{1,2},{2,1},{3,4},{4,3},{5,6},{6,5},{7,8},{8,7},{9,10},{10... | collective-permute-start | bytes 786440 | tf_op jit(solution)/shard_map/ppermute | solution.py:204
  29.2 6.3 %all-gather.1 = f32[1024,128]{1,0:T(8,128)S(1)} all-gather(f32[512,128]{1,0:T(8,128)S(1)} %shard_map.71.s), channel_id=3, replica_groups={{0,1},{2,3},{4,5},{6,7},{8,9},{10,11},{12,13},{14,15},{16,17},{18,19},{..., dimensions={0}, use_global_device_ids=true | all-gather | bytes 786432 | tf_op jit(solution)/shard_map/all_gather | solution.py:198
  35.5 0.4 shard_map.72
  35.9 1.9 %collective-permute-start.2 = (f32[4,512,128]{2,1,0:T(8,128)S(1)}, f32[4,512,128]{2,1,0:T(8,128)S(1)}, u32[]{:S(2)}, u32[]{:S(2)}) collective-permute-start(f32[4,512,128]{2,1,0:T(8,128)S(1)} %get-tuple-element.37), channel_id=1, source_target_pairs={{0,511},{1,2},{2,1},{3,4},{4,3},{5,6},{6,5},{7,8},{8,7},{9,10},{10... | collective-permute-start | bytes 3145736 | tf_op jit(solution)/shard_map/ppermute | solution.py:204
  37.9 0.0 collective-permute-done.1.v.s_far
  37.9 0.5 shard_map.73
  38.3 5.4 %all-gather.2 = f32[1024,128]{1,0:T(8,128)S(1)} all-gather(f32[512,128]{1,0:T(8,128)S(1)} %shard_map.73), channel_id=4, replica_groups={{0,1},{2,3},{4,5},{6,7},{8,9},{10,11},{12,13},{14,15},{16,17},{18,19},{..., dimensions={0}, use_global_device_ids=true | all-gather | bytes 786432 | tf_op jit(solution)/shard_map/all_gather | solution.py:198
  43.7 0.5 shard_map.74.sent
  44.2 1.9 %collective-permute-start.3 = (f32[2,512,128]{2,1,0:T(8,128)S(1)}, f32[2,512,128]{2,1,0:T(8,128)S(1)}, u32[]{:S(2)}, u32[]{:S(2)}) collective-permute-start(f32[2,512,128]{2,1,0:T(8,128)S(1)} %shard_map.74.sent), channel_id=1, source_target_pairs={{0,511},{1,2},{2,1},{3,4},{4,3},{5,6},{6,5},{7,8},{8,7},{9,10},{10... | collective-permute-start | bytes 1572872 | tf_op jit(solution)/shard_map/ppermute | solution.py:204
  46.1 6.2 %collective-permute-done.2.k_in = f32[4,512,128]{2,1,0:T(8,128)S(1)} collective-permute-done((f32[4,512,128]{2,1,0:T(8,128)S(1)}, f32[4,512,128]{2,1,0:T(8,128)S(1)}, u32[]{:S(2)}, u32[]{:S(2)}) %collective-permute-start.2) | collective-permute-done | bytes 1048608 | tf_op jit(solution)/shard_map/ppermute | solution.py:204
  52.3 0.2 shard_map.75
  52.6 0.0 copy-start
  52.6 0.4 shard_map.76.effect
  53.0 4.9 %collective-permute-done.3.got = f32[2,512,128]{2,1,0:T(8,128)S(1)} collective-permute-done((f32[2,512,128]{2,1,0:T(8,128)S(1)}, f32[2,512,128]{2,1,0:T(8,128)S(1)}, u32[]{:S(2)}, u32[]{:S(2)}) %collective-permute-start.3) | collective-permute-done | bytes 524320 | tf_op jit(solution)/shard_map/ppermute | solution.py:204
  58.0 0.0 copy-done
  58.0 1.2 %shard_map.77 = (f32[512,128]{1,0:T(8,128)S(1)}, f32[512,128]{1,0:T(8,128)S(1)}) custom-call(f32[512,128]{1,0:T(8,128)S(1)} %shard_map.71.s, f32[512,128]{1,0:T(8,128)S(1)} %collective-permute-done.1.v.s_far, f32[512,128]{1,0:T(8,128)S(1)} %shard_map.76.effect, f32[2,512,128]{2,1,0:T(8,128)S(1)} %shard_map.74.sent, ...), custom_call_target="tpu_custom_call" | custom-call | flops 268435456 | bytes 1048576 | tf_op jit(solution)/shard_map/pallas_call | solution.py:178
  59.1 7.3 %all-gather.3 = f32[1024,128]{1,0:T(8,128)S(1)} all-gather(f32[512,128]{1,0:T(8,128)S(1)} %get-tuple-element.44.first), channel_id=5, replica_groups={{0,1},{2,3},{4,5},{6,7},{8,9},{10,11},{12,13},{14,15},{16,17},{18,19},{..., dimensions={0}, use_global_device_ids=true | all-gather | bytes 786432 | tf_op jit(solution)/shard_map/all_gather | solution.py:198
  66.4 0.9 shard_map.78
  67.3 2.2 %all-gather.4 = f32[1024,128]{1,0:T(8,128)S(1)} all-gather(f32[512,128]{1,0:T(8,128)S(1)} %get-tuple-element.48.w), channel_id=6, replica_groups={{0,1},{2,3},{4,5},{6,7},{8,9},{10,11},{12,13},{14,15},{16,17},{18,19},{..., dimensions={0}, use_global_device_ids=true | all-gather | bytes 786432 | tf_op jit(solution)/shard_map/all_gather | solution.py:198
  69.5 0.5 shard_map.79.sent
  70.0 1.9 %collective-permute-start.4 = (f32[2,512,128]{2,1,0:T(8,128)S(1)}, f32[2,512,128]{2,1,0:T(8,128)S(1)}, u32[]{:S(2)}, u32[]{:S(2)}) collective-permute-start(f32[2,512,128]{2,1,0:T(8,128)S(1)} %shard_map.79.sent), channel_id=1, source_target_pairs={{0,511},{1,2},{2,1},{3,4},{4,3},{5,6},{6,5},{7,8},{8,7},{9,10},{10... | collective-permute-start | bytes 1572872 | tf_op jit(solution)/shard_map/ppermute | solution.py:204
  71.9 0.4 shard_map.80.effect
  72.4 8.4 %collective-permute-done.4.got = f32[2,512,128]{2,1,0:T(8,128)S(1)} collective-permute-done((f32[2,512,128]{2,1,0:T(8,128)S(1)}, f32[2,512,128]{2,1,0:T(8,128)S(1)}, u32[]{:S(2)}, u32[]{:S(2)}) %collective-permute-start.4) | collective-permute-done | bytes 524320 | tf_op jit(solution)/shard_map/ppermute | solution.py:204
  80.8 0.7 shard_map.81
  81.5 7.4 %collective-permute-start.5 = (f32[2,512,128]{2,1,0:T(8,128)S(1)}, f32[2,512,128]{2,1,0:T(8,128)S(1)}, u32[]{:S(2)}, u32[]{:S(2)}) collective-permute-start(f32[2,512,128]{2,1,0:T(8,128)S(1)} %get-tuple-element.49.pair), channel_id=1, source_target_pairs={{0,1},{1,0},{2,3},{3,2},{4,5},{5,4},{6,7},{7,6},{8,9},{9,8},{10,11... | collective-permute-start | bytes 1572872 | tf_op jit(solution)/shard_map/ppermute | solution.py:201
  88.9 1.5 %collective-permute-done.5.near = f32[2,512,128]{2,1,0:T(8,128)S(1)} collective-permute-done((f32[2,512,128]{2,1,0:T(8,128)S(1)}, f32[2,512,128]{2,1,0:T(8,128)S(1)}, u32[]{:S(2)}, u32[]{:S(2)}) %collective-permute-start.5) | collective-permute-done | bytes 524320 | tf_op jit(solution)/shard_map/ppermute | solution.py:201
  90.4 0.7 shard_map.82.sent
  91.2 1.9 %collective-permute-start.6 = (f32[2,512,128]{2,1,0:T(8,128)S(1)}, f32[2,512,128]{2,1,0:T(8,128)S(1)}, u32[]{:S(2)}, u32[]{:S(2)}) collective-permute-start(f32[2,512,128]{2,1,0:T(8,128)S(1)} %shard_map.82.sent), channel_id=1, source_target_pairs={{0,511},{1,2},{2,1},{3,4},{4,3},{5,6},{6,5},{7,8},{8,7},{9,10},{10... | collective-permute-start | bytes 1572872 | tf_op jit(solution)/shard_map/ppermute | solution.py:204
  93.1 0.4 shard_map.83.effect
  93.6 8.4 %collective-permute-done.6.got = f32[2,512,128]{2,1,0:T(8,128)S(1)} collective-permute-done((f32[2,512,128]{2,1,0:T(8,128)S(1)}, f32[2,512,128]{2,1,0:T(8,128)S(1)}, u32[]{:S(2)}, u32[]{:S(2)}) %collective-permute-start.6) | collective-permute-done | bytes 524320 | tf_op jit(solution)/shard_map/ppermute | solution.py:204
  102.0 1.2 %shard_map.84 = (f32[512,128]{1,0:T(8,128)S(1)}, f32[512,128]{1,0:T(8,128)S(1)}) custom-call(f32[2,512,128]{2,1,0:T(8,128)S(1)} %get-tuple-element.49.pair, f32[512,128]{1,0:T(8,128)S(1)} %get-tuple-element.50.s_far, f32[512,128]{1,0:T(8,128)S(1)} %shard_map.83.effect, f32[2,512,128]{2,1,0:T(8,128)S(1)} %shard_map.82.sent, ...), custom_call_target="tpu_custom_call" | custom-call | flops 268435456 | bytes 1048576 | tf_op jit(solution)/shard_map/pallas_call | solution.py:178
  103.1 7.3 %all-gather.5 = f32[1024,128]{1,0:T(8,128)S(1)} all-gather(f32[512,128]{1,0:T(8,128)S(1)} %get-tuple-element.52.d), channel_id=7, replica_groups={{0,1},{2,3},{4,5},{6,7},{8,9},{10,11},{12,13},{14,15},{16,17},{18,19},{..., dimensions={0}, use_global_device_ids=true | all-gather | bytes 786432 | tf_op jit(solution)/shard_map/all_gather | solution.py:198
  110.5 1.2 %shard_map.85 = (f32[1,512,128]{2,1,0:T(8,128)}, f32[1,512,128]{2,1,0:T(8,128)}) custom-call(s32[1]{0:T(128)} %bitcast.odd, f32[2,512,128]{2,1,0:T(8,128)S(1)} %bitcast.13, f32[512,128]{1,0:T(8,128)S(1)} %get-tuple-element.53.rest, bf16[512,512]{1,0:T(8,128)(2,1)S(1)} %get-tuple-element.46.n0, bf16[512,512]{1,0:T(8,128)(2,1)S(1)} %get-tuple-element.47.n1, ...), custom_call_target="tpu_custom_call" | custom-call | flops 268435456 | bytes 1048576 | tf_op jit(solution)/shard_map/pallas_call | solution.py:178
Async XLA Ops:
  3.1 23.7 %collective-permute-start = (f32[512,128]{1,0:T(8,128)S(1)}, f32[512,128]{1,0:T(8,128)S(1)}, u32[]{:S(2)}, u32[]{:S(2)}) collective-permute-start(f32[512,128]{1,0:T(8,128)S(1)} %get-tuple-element.28._.w), channel_id=1, source_target_pairs={{0,511},{1,2},{2,1},{3,4},{4,3},{5,6},{6,5},{7,8},{8,7},{9,10},{10... | collective-permute-start | bytes 786440 | tf_op jit(solution)/shard_map/ppermute | solution.py:204
  27.3 10.6 %collective-permute-start.1 = (f32[512,128]{1,0:T(8,128)S(1)}, f32[512,128]{1,0:T(8,128)S(1)}, u32[]{:S(2)}, u32[]{:S(2)}) collective-permute-start(f32[512,128]{1,0:T(8,128)S(1)} %shard_map.71.s), channel_id=1, source_target_pairs={{0,511},{1,2},{2,1},{3,4},{4,3},{5,6},{6,5},{7,8},{8,7},{9,10},{10... | collective-permute-start | bytes 786440 | tf_op jit(solution)/shard_map/ppermute | solution.py:204
  35.9 16.4 %collective-permute-start.2 = (f32[4,512,128]{2,1,0:T(8,128)S(1)}, f32[4,512,128]{2,1,0:T(8,128)S(1)}, u32[]{:S(2)}, u32[]{:S(2)}) collective-permute-start(f32[4,512,128]{2,1,0:T(8,128)S(1)} %get-tuple-element.37), channel_id=1, source_target_pairs={{0,511},{1,2},{2,1},{3,4},{4,3},{5,6},{6,5},{7,8},{8,7},{9,10},{10... | collective-permute-start | bytes 3145736 | tf_op jit(solution)/shard_map/ppermute | solution.py:204
  44.2 13.8 %collective-permute-start.3 = (f32[2,512,128]{2,1,0:T(8,128)S(1)}, f32[2,512,128]{2,1,0:T(8,128)S(1)}, u32[]{:S(2)}, u32[]{:S(2)}) collective-permute-start(f32[2,512,128]{2,1,0:T(8,128)S(1)} %shard_map.74.sent), channel_id=1, source_target_pairs={{0,511},{1,2},{2,1},{3,4},{4,3},{5,6},{6,5},{7,8},{8,7},{9,10},{10... | collective-permute-start | bytes 1572872 | tf_op jit(solution)/shard_map/ppermute | solution.py:204
  52.6 5.4 %copy-start = (f32[1,512,128]{2,1,0:T(8,128)S(1)}, f32[1,512,128]{2,1,0:T(8,128)}, u32[]{:S(2)}) copy-start(f32[1,512,128]{2,1,0:T(8,128)} %param.5) | copy-start | bytes 786436
  70.0 10.8 %collective-permute-start.4 = (f32[2,512,128]{2,1,0:T(8,128)S(1)}, f32[2,512,128]{2,1,0:T(8,128)S(1)}, u32[]{:S(2)}, u32[]{:S(2)}) collective-permute-start(f32[2,512,128]{2,1,0:T(8,128)S(1)} %shard_map.79.sent), channel_id=1, source_target_pairs={{0,511},{1,2},{2,1},{3,4},{4,3},{5,6},{6,5},{7,8},{8,7},{9,10},{10... | collective-permute-start | bytes 1572872 | tf_op jit(solution)/shard_map/ppermute | solution.py:204
  81.5 8.9 %collective-permute-start.5 = (f32[2,512,128]{2,1,0:T(8,128)S(1)}, f32[2,512,128]{2,1,0:T(8,128)S(1)}, u32[]{:S(2)}, u32[]{:S(2)}) collective-permute-start(f32[2,512,128]{2,1,0:T(8,128)S(1)} %get-tuple-element.49.pair), channel_id=1, source_target_pairs={{0,1},{1,0},{2,3},{3,2},{4,5},{5,4},{6,7},{7,6},{8,9},{9,8},{10,11... | collective-permute-start | bytes 1572872 | tf_op jit(solution)/shard_map/ppermute | solution.py:201
  91.2 10.8 %collective-permute-start.6 = (f32[2,512,128]{2,1,0:T(8,128)S(1)}, f32[2,512,128]{2,1,0:T(8,128)S(1)}, u32[]{:S(2)}, u32[]{:S(2)}) collective-permute-start(f32[2,512,128]{2,1,0:T(8,128)S(1)} %shard_map.82.sent), channel_id=1, source_target_pairs={{0,511},{1,2},{2,1},{3,4},{4,3},{5,6},{6,5},{7,8},{8,7},{9,10},{10... | collective-permute-start | bytes 1572872 | tf_op jit(solution)/shard_map/ppermute | solution.py:204

commit v4 on v3

--- a/solution.py
+++ b/solution.py
@@ -112,22 +112,36 @@
     s[...] = part[...] - times((h0, h1), got[...])
 
 
-def part_kernel(odd, near, j0, j1, h, out, h_out):
-    out[...] = times((j0, j1), near[1 - odd[0]])
-
-
-def product_kernel(v, h0, h1, out):
-    out[...] = times((h0, h1), v[...])
-
-
-def parts_kernel(odd, m, near, j0, j1, out):
-    out[0] = m[...]
+def part_kernel(odd, s, near, j0, j1, out):
+    out[0] = s[...]
     out[1] = times((j0, j1), near[1 - odd[0]])
 
 
-def pair_kernel(odd, w, near, j0, j1, out):
-    out[0] = w[...]
-    out[1] = w[...] - times((j0, j1), near[1 - odd[0]])
+def part_and_block_kernel(odd, s, near, j0, j1, h, out, h_out):
+    part_kernel(odd, s, near, j0, j1, out)
+
+
+def front_kernel(sent, got, h0, h1, f, g):
+    n = f.shape[1]
+    both = times((h0, h1), jnp.concatenate([got[0], got[1]], axis=1))
+    f[...] = both[:, :n]
+    g[...] = sent[0] + both[:, n:]
+
+
+def step_kernel(odd, g, near, j0, j1, d):
+    d[...] = g[...] + times((j0, j1), near[1 - odd[0]])
+
+
+def step_rest_kernel(odd, g, near, r, j0, j1, d0, d1, d, rest):
+    step_kernel(odd, g, near, j0, j1, d)
+    rest[...] = r[...] - times((d0, d1), d[...])
+
+
+def again_kernel(odd, near, rest, d, n0, n1, e0, e1, out, rest_out):
+    value = rest[...] - times((n0, n1), near[1 - odd[0]])
+    rest_out[...] = value
+    out[0] = d[...]
+    out[1] = times((e0, e1), value)
 
 
 def split_kernel(k_in, k0, k1):
@@ -140,38 +154,29 @@
     out[...] = times((k0, k1), sent[0])
 
 
-def seconds_kernel(sent, got, effect, h0, h1, pair, s_far):
-    value = got[1] - effect[...]
-    s_far[...] = value
-    pair[0] = sent[1] - times((h0, h1), got[0])
-    pair[1] = times((h0, h1), value)
-
-
-def both_parts_kernel(near, j0, j1, out):
-    out[0] = times((j0, j1), near[0])
-    out[1] = times((j0, j1), near[1])
-
-
-def step_kernel(s, s_far, effect, sent, got, r, h0, h1, d0, d1, f0, f1, d, rest):
-    change = s[...] + sent[1] + times((h0, h1), got[0])
-    far = s_far[...] + got[1] + effect[...]
-    d[...] = change
-    rest[...] = r[...] - times((d0, d1), change) - times((f0, f1), far)
-
-
-def pair_step_kernel(pair, s_far, effect, sent, got, r, h0, h1, d0, d1, f0, f1, d, rest):
-    step_kernel(pair.at[0], s_far, effect, sent, got, r, h0, h1, d0, d1, f0, f1, d, rest)
-
-
-def residual_kernel(odd, near, rest, n0, n1, e0, e1, r, w):
-    value = rest[...] - times((n0, n1), near[1 - odd[0]])
-    r[...] = value
-    w[...] = times((e0, e1), value)
-
-
-def last_kernel(odd, near, rest, n0, n1, first, d, x, r):
-    r[0] = rest[...] - times((n0, n1), near[1 - odd[0]])
+def both_w_kernel(sent, got, effect, h0, h1, w, base):
+    n = w.shape[1]
+    both = times((h0, h1), jnp.concatenate([got[0], got[1] - effect[...]], axis=1))
+    value = sent[1] - both[:, :n]
+    w[...] = value
+    base[...] = value - both[:, n:]
+
+
+def base_kernel(odd, base, near, j0, j1, s):
+    s[...] = base[...] - times((j0, j1), near[1 - odd[0]])
+
+
+def residual_kernel(_, rest, got, f0, f1, r):
+    r[...] = rest[...] - times((f0, f1), got[0])
+
+
+def sum_kernel(odd, near, r, d, first, n0, n1, d0, d1, rest, x):
+    rest[...] = r[...] - times((d0, d1), d[...]) - times((n0, n1), near[1 - odd[0]])
     x[0] = first[...] + d[...]
+
+
+def last_kernel(rest, got, f0, f1, r):
+    r[0] = rest[...] - times((f0, f1), got[...])
 
 
 def call(kernel, outs, *args, specs=None, scratch=(), limit=16, products=1, aliases={}, outs_at=None):
@@ -229,30 +234,30 @@
     H, J, N, F, D = (mats[i:i + 2] for i in range(0, 10, 2))
     (part,) = call(near_part_kernel, [vec], odd, w, near(w), *J)
     (s,) = call(second_kernel, [vec], part, w_far, *H)
-    s_far = far(s)
-    m, h = call(
-        part_kernel, [vec, blocks], odd, near(s), *J, h,
-        specs=[SMEM] + [VMEM] * 3 + [ANY], outs_at=[VMEM, ANY], aliases={4: 1},
+    sent, h = call(
+        part_and_block_kernel, [two, blocks], odd, s, near(s), *J, h,
+        specs=[SMEM] + [VMEM] * 4 + [ANY], outs_at=[VMEM, ANY], aliases={5: 1},
     )
+    got = far(sent)
     k_in = far(h)
-    (f,) = call(product_kernel, [vec], s_far, *H, products=20)
-    (parts,) = call(parts_kernel, [two], odd, m, near(f), *J)
-    got = far(parts)
+    f, g = call(front_kernel, [vec, vec], sent, got, *H, products=20)
+    first, rest = call(step_rest_kernel, [vec, vec], odd, g, near(f), b, *J, *D)
+    sent, rest = call(again_kernel, [two, vec], odd, near(first), rest, first, *N, *E)
+    got = far(sent)
     K = call(split_kernel, half, k_in)
-    (effect,) = call(sent_kernel, [vec], parts, *K)
-    d1, rest = call(step_kernel, [vec, vec], s, s_far, effect, parts, got, b, *H, *D, *F)
-
-    r, w = call(residual_kernel, [vec, vec], odd, near(d1), rest, *N, *E)
-    (sent,) = call(pair_kernel, [two], odd, w, near(w), *J)
-    got = far(sent)
     (effect,) = call(sent_kernel, [vec], sent, *K)
-    pair, s_far = call(seconds_kernel, [two, vec], sent, got, effect, *H)
-    (parts,) = call(both_parts_kernel, [two], swap_near(pair), *J)
-    got = far(parts)
-    (effect,) = call(sent_kernel, [vec], parts, *K)
-    d2, rest = call(pair_step_kernel, [vec, vec], pair, s_far, effect, parts, got, r, *H, *D, *F)
+    w, base = call(both_w_kernel, [vec, vec], sent, got, effect, *H)
+
+    (s,) = call(base_kernel, [vec], odd, base, near(w), *J)
+    (sent,) = call(part_kernel, [two], odd, s, near(s), *J)
+    (r,) = call(residual_kernel, [vec], sent, rest, got, *F, specs=[ANY] + [VMEM] * 4)
+    f, g = call(front_kernel, [vec, vec], sent, far(sent), *H)
+    (d,) = call(step_kernel, [vec], odd, g, near(f), *J)
+    got = far(d)
     one = ((1, size, cols), F32)
-    return tuple(call(last_kernel, [one, one], odd, near(d2), rest, *N, d1, d2))
+    rest, x = call(sum_kernel, [vec, one], odd, near(d), r, d, first, *N, *D)
+    (r,) = call(last_kernel, [one], rest, got, *F)
+    return x, r
 
 
 def solution(mesh):

time: 112 us -> 106 us (0.946)
  waiting for transfers between devices: 29.5 us -> 22.3 us
  blocking collectives: 42.8 us -> 49.2 us
  starting transfers between devices: 21.5 us -> 15.8 us
    ppermute x1 -> x0, starting transfers between devices: 7.4 us -> none  [swap_near(): return lax.ppermute(v, AXIS, near_pairs)]
    all_gather x6 -> x8, blocking collectives: 42.8 us -> 49.2 us  [near(): return lax.all_gather(v, AXIS, axis_index_groups=near_groups)]
    ppermute x6, waiting for transfers between devices: 28 us -> 22.3 us  [far(): return lax.ppermute(v, AXIS, far_pairs)]
    ppermute x6, starting transfers between devices: 14.1 us -> 15.8 us  [far(): return lax.ppermute(v, AXIS, far_pairs)]
    ppermute x1 -> x0, waiting for transfers between devices: 1.51 us -> none  [swap_near(): return lax.ppermute(v, AXIS, near_pairs)]
  transfers between devices with their start and end apart: 7 -> 6, of which waited for: 5 -> 3; matrix products, arithmetic and copies ran while one was open for 0% -> 0% of each run, Pallas kernels for 7% -> 9%
where the time goes in v4:
time: 106 us; the launch traced here: 105 us
  blocking collectives  49.2 us (46%)
  waiting for transfers between devices  22.3 us (21%)
  Pallas kernels  17.1 us (16%)
  starting transfers between devices  15.8 us (15%)
    all_gather x8, blocking collectives, near(): return lax.all_gather(v, AXIS, axis_index_groups=near_groups)  49.2 us
    ppermute x6, waiting for transfers between devices, far(): return lax.ppermute(v, AXIS, far_pairs)  22.3 us
    pallas_call x18, Pallas kernels, call(): pl.pallas_call(kernel, out_shape=[jax.ShapeDtypeStruct(shape, dtype) for...  17.1 us
    ppermute x6, starting transfers between devices, far(): return lax.ppermute(v, AXIS, far_pairs)  15.8 us
  transfers between devices with their start and end apart: 6, of which 3 were waited for; matrix products, arithmetic and copies ran while one was open for 0% of the time, Pallas kernels for 9%

profile of v4, /device:TPU:1, one launch (start us, length us, event | category | flops | bytes accessed | tf_op | source)
XLA Modules:
  0.0 105.2 jit_solution(659575989685043189)
XLA Ops:
  0.6 2.4 %shard_map.68 = (f32[512,128]{1,0:T(8,128)S(1)}, bf16[512,512]{1,0:T(8,128)(2,1)S(1)}, bf16[512,512]{1,0:T(8,128)(2,1)S(1)}) custom-call(f32[512,128]{1,0:T(8,128)} %bitcast.22, f32[512,512]{1,0:T(8,128)} %bitcast.24), custom_call_target="tpu_custom_call" | custom-call | flops 268435456 | bytes 1048576 | tf_op jit(solution)/shard_map/pallas_call | solution.py:183
  3.1 4.5 %collective-permute-start = (f32[512,128]{1,0:T(8,128)S(1)}, f32[512,128]{1,0:T(8,128)S(1)}, u32[]{:S(2)}, u32[]{:S(2)}) collective-permute-start(f32[512,128]{1,0:T(8,128)S(1)} %get-tuple-element.32._.w), channel_id=1, source_target_pairs={{0,511},{1,2},{2,1},{3,4},{4,3},{5,6},{6,5},{7,8},{8,7},{9,10},{10... | collective-permute-start | bytes 786440 | tf_op jit(solution)/shard_map/ppermute | solution.py:209
  7.6 14.3 %all-gather = f32[1024,128]{1,0:T(8,128)S(1)} all-gather(f32[512,128]{1,0:T(8,128)S(1)} %get-tuple-element.32._.w), channel_id=2, replica_groups={{0,1},{2,3},{4,5},{6,7},{8,9},{10,11},{12,13},{14,15},{16,17},{18,19},{..., dimensions={0}, use_global_device_ids=true | all-gather | bytes 786432 | tf_op jit(solution)/shard_map/all_gather | solution.py:203
  21.9 4.4 %shard_map.69 = (f32[4,512,128]{2,1,0:T(8,128)S(1)}, bf16[512,512]{1,0:T(8,128)(2,1)S(1)}, bf16[512,512]{1,0:T(8,128)(2,1)S(1)}, bf16[512,512]{1,0:T(8,128)(2,1)...) custom-call(s32[1]{0:T(128)} %bitcast.odd, ...), custom_call_target="tpu_custom_call" | custom-call | flops 2684354560 | bytes 1048576 | tf_op jit(solution)/shard_map/pallas_call | solution.py:183
  26.3 0.5 shard_map.70.part
  26.8 0.0 collective-permute-done.got
  26.8 0.5 shard_map.71.s
  27.3 2.4 %all-gather.1 = f32[1024,128]{1,0:T(8,128)S(1)} all-gather(f32[512,128]{1,0:T(8,128)S(1)} %shard_map.71.s), channel_id=3, replica_groups={{0,1},{2,3},{4,5},{6,7},{8,9},{10,11},{12,13},{14,15},{16,17},{18,19},{..., dimensions={0}, use_global_device_ids=true | all-gather | bytes 786432 | tf_op jit(solution)/shard_map/all_gather | solution.py:203
  29.6 0.5 shard_map.72
  30.1 1.9 %collective-permute-start.1 = (f32[2,512,128]{2,1,0:T(8,128)S(1)}, f32[2,512,128]{2,1,0:T(8,128)S(1)}, u32[]{:S(2)}, u32[]{:S(2)}) collective-permute-start(f32[2,512,128]{2,1,0:T(8,128)S(1)} %get-tuple-element.40.sent), channel_id=1, source_target_pairs={{0,511},{1,2},{2,1},{3,4},{4,3},{5,6},{6,5},{7,8},{8,7},{9,10},{10... | collective-permute-start | bytes 1572872 | tf_op jit(solution)/shard_map/ppermute | solution.py:209
  32.0 3.6 %collective-permute-start.3 = (f32[4,512,128]{2,1,0:T(8,128)S(1)}, f32[4,512,128]{2,1,0:T(8,128)S(1)}, u32[]{:S(2)}, u32[]{:S(2)}) collective-permute-start(f32[4,512,128]{2,1,0:T(8,128)S(1)} %get-tuple-element.50), channel_id=1, source_target_pairs={{0,511},{1,2},{2,1},{3,4},{4,3},{5,6},{6,5},{7,8},{8,7},{9,10},{10... | collective-permute-start | bytes 3145736 | tf_op jit(solution)/shard_map/ppermute | solution.py:209
  35.7 5.2 %collective-permute-done.1.got = f32[2,512,128]{2,1,0:T(8,128)S(1)} collective-permute-done((f32[2,512,128]{2,1,0:T(8,128)S(1)}, f32[2,512,128]{2,1,0:T(8,128)S(1)}, u32[]{:S(2)}, u32[]{:S(2)}) %collective-permute-start.1) | collective-permute-done | bytes 524320 | tf_op jit(solution)/shard_map/ppermute | solution.py:209
  40.9 0.7 shard_map.73
  41.6 0.0 copy-start
  41.6 7.5 %all-gather.2 = f32[1024,128]{1,0:T(8,128)S(1)} all-gather(f32[512,128]{1,0:T(8,128)S(1)} %get-tuple-element.42), channel_id=4, replica_groups={{0,1},{2,3},{4,5},{6,7},{8,9},{10,11},{12,13},{14,15},{16,17},{18,19},{..., dimensions={0}, use_global_device_ids=true | all-gather | bytes 786432 | tf_op jit(solution)/shard_map/all_gather | solution.py:203
  49.1 0.0 copy-done
  49.1 0.9 shard_map.74
  49.9 2.2 %all-gather.3 = f32[1024,128]{1,0:T(8,128)S(1)} all-gather(f32[512,128]{1,0:T(8,128)S(1)} %get-tuple-element.45.d.first), channel_id=5, replica_groups={{0,1},{2,3},{4,5},{6,7},{8,9},{10,11},{12,13},{14,15},{16,17},{18,19},{..., dimensions={0}, use_global_device_ids=true | all-gather | bytes 786432 | tf_op jit(solution)/shard_map/all_gather | solution.py:203
  52.1 0.9 shard_map.75
  53.0 1.9 %collective-permute-start.2 = (f32[2,512,128]{2,1,0:T(8,128)S(1)}, f32[2,512,128]{2,1,0:T(8,128)S(1)}, u32[]{:S(2)}, u32[]{:S(2)}) collective-permute-start(f32[2,512,128]{2,1,0:T(8,128)S(1)} %get-tuple-element.49.sent), channel_id=1, source_target_pairs={{0,511},{1,2},{2,1},{3,4},{4,3},{5,6},{6,5},{7,8},{8,7},{9,10},{10... | collective-permute-start | bytes 1572872 | tf_op jit(solution)/shard_map/ppermute | solution.py:209
  55.0 0.0 collective-permute-done.3.k_in
  55.0 0.2 shard_map.76
  55.2 0.4 shard_map.77.effect
  55.6 8.2 %collective-permute-done.2.got = f32[2,512,128]{2,1,0:T(8,128)S(1)} collective-permute-done((f32[2,512,128]{2,1,0:T(8,128)S(1)}, f32[2,512,128]{2,1,0:T(8,128)S(1)}, u32[]{:S(2)}, u32[]{:S(2)}) %collective-permute-start.2) | collective-permute-done | bytes 524320 | tf_op jit(solution)/shard_map/ppermute | solution.py:209
  63.8 0.7 shard_map.78
  64.6 7.3 %all-gather.4 = f32[1024,128]{1,0:T(8,128)S(1)} all-gather(f32[512,128]{1,0:T(8,128)S(1)} %get-tuple-element.54), channel_id=6, replica_groups={{0,1},{2,3},{4,5},{6,7},{8,9},{10,11},{12,13},{14,15},{16,17},{18,19},{..., dimensions={0}, use_global_device_ids=true | all-gather | bytes 786432 | tf_op jit(solution)/shard_map/all_gather | solution.py:203
  71.9 0.5 shard_map.79.s
  72.3 2.2 %all-gather.5 = f32[1024,128]{1,0:T(8,128)S(1)} all-gather(f32[512,128]{1,0:T(8,128)S(1)} %shard_map.79.s), channel_id=7, replica_groups={{0,1},{2,3},{4,5},{6,7},{8,9},{10,11},{12,13},{14,15},{16,17},{18,19},{..., dimensions={0}, use_global_device_ids=true | all-gather | bytes 786432 | tf_op jit(solution)/shard_map/all_gather | solution.py:203
  74.5 0.5 shard_map.80.sent._
  75.0 1.9 %collective-permute-start.4 = (f32[2,512,128]{2,1,0:T(8,128)S(1)}, f32[2,512,128]{2,1,0:T(8,128)S(1)}, u32[]{:S(2)}, u32[]{:S(2)}) collective-permute-start(f32[2,512,128]{2,1,0:T(8,128)S(1)} %shard_map.80.sent._), channel_id=1, source_target_pairs={{0,511},{1,2},{2,1},{3,4},{4,3},{5,6},{6,5},{7,8},{8,7},{9,10},{10... | collective-permute-start | bytes 1572872 | tf_op jit(solution)/shard_map/ppermute | solution.py:209
  76.9 8.9 %collective-permute-done.4.got = f32[2,512,128]{2,1,0:T(8,128)S(1)} collective-permute-done((f32[2,512,128]{2,1,0:T(8,128)S(1)}, f32[2,512,128]{2,1,0:T(8,128)S(1)}, u32[]{:S(2)}, u32[]{:S(2)}) %collective-permute-start.4) | collective-permute-done | bytes 524320 | tf_op jit(solution)/shard_map/ppermute | solution.py:209
  85.8 0.7 shard_map.81
  86.5 7.3 %all-gather.6 = f32[1024,128]{1,0:T(8,128)S(1)} all-gather(f32[512,128]{1,0:T(8,128)S(1)} %get-tuple-element.56), channel_id=8, replica_groups={{0,1},{2,3},{4,5},{6,7},{8,9},{10,11},{12,13},{14,15},{16,17},{18,19},{..., dimensions={0}, use_global_device_ids=true | all-gather | bytes 786432 | tf_op jit(solution)/shard_map/all_gather | solution.py:203
  93.8 0.5 shard_map.82.d
  94.3 1.9 %collective-permute-start.5 = (f32[512,128]{1,0:T(8,128)S(1)}, f32[512,128]{1,0:T(8,128)S(1)}, u32[]{:S(2)}, u32[]{:S(2)}) collective-permute-start(f32[512,128]{1,0:T(8,128)S(1)} %shard_map.82.d), channel_id=1, source_target_pairs={{0,511},{1,2},{2,1},{3,4},{4,3},{5,6},{6,5},{7,8},{8,7},{9,10},{10... | collective-permute-start | bytes 786440 | tf_op jit(solution)/shard_map/ppermute | solution.py:209
  96.2 0.5 shard_map.83.r
  96.7 6.1 %all-gather.7 = f32[1024,128]{1,0:T(8,128)S(1)} all-gather(f32[512,128]{1,0:T(8,128)S(1)} %shard_map.82.d), channel_id=9, replica_groups={{0,1},{2,3},{4,5},{6,7},{8,9},{10,11},{12,13},{14,15},{16,17},{18,19},{..., dimensions={0}, use_global_device_ids=true | all-gather | bytes 786432 | tf_op jit(solution)/shard_map/all_gather | solution.py:203
  102.8 1.3 %shard_map.84 = (f32[512,128]{1,0:T(8,128)S(1)}, f32[1,512,128]{2,1,0:T(8,128)}) custom-call(s32[1]{0:T(128)} %bitcast.odd, f32[2,512,128]{2,1,0:T(8,128)S(1)} %bitcast.18, f32[512,128]{1,0:T(8,128)S(1)} %shard_map.83.r, f32[512,128]{1,0:T(8,128)S(1)} %shard_map.82.d, f32[512,128]{1,0:T(8,128)S(1)} %get-tuple-element.45.d.first, ...), custom_call_target="tpu_custom_call" | custom-call | flops 268435456 | bytes 1048576 | tf_op jit(solution)/shard_map/pallas_call | solution.py:183
  104.1 0.0 collective-permute-done.5.got
  104.1 1.2 %shard_map.85 = f32[1,512,128]{2,1,0:T(8,128)} custom-call(f32[512,128]{1,0:T(8,128)S(1)} %get-tuple-element.61.rest, f32[512,128]{1,0:T(8,128)S(1)} %collective-permute-done.5.got, bf16[512,512]{1,0:T(8,128)(2,1)S(1)} %get-tuple-element.58.f0, bf16[512,512]{1,0:T(8,128)(2,1)S(1)} %get-tuple-element.59.f1), custom_call_target="tpu_custom_call" | custom-call | flops 268435456 | bytes 1048576 | tf_op jit(solution)/shard_map/pallas_call | solution.py:183
Async XLA Ops:
  3.1 23.7 %collective-permute-start = (f32[512,128]{1,0:T(8,128)S(1)}, f32[512,128]{1,0:T(8,128)S(1)}, u32[]{:S(2)}, u32[]{:S(2)}) collective-permute-start(f32[512,128]{1,0:T(8,128)S(1)} %get-tuple-element.32._.w), channel_id=1, source_target_pairs={{0,511},{1,2},{2,1},{3,4},{4,3},{5,6},{6,5},{7,8},{8,7},{9,10},{10... | collective-permute-start | bytes 786440 | tf_op jit(solution)/shard_map/ppermute | solution.py:209
  30.1 10.8 %collective-permute-start.1 = (f32[2,512,128]{2,1,0:T(8,128)S(1)}, f32[2,512,128]{2,1,0:T(8,128)S(1)}, u32[]{:S(2)}, u32[]{:S(2)}) collective-permute-start(f32[2,512,128]{2,1,0:T(8,128)S(1)} %get-tuple-element.40.sent), channel_id=1, source_target_pairs={{0,511},{1,2},{2,1},{3,4},{4,3},{5,6},{6,5},{7,8},{8,7},{9,10},{10... | collective-permute-start | bytes 1572872 | tf_op jit(solution)/shard_map/ppermute | solution.py:209
  32.0 22.9 %collective-permute-start.3 = (f32[4,512,128]{2,1,0:T(8,128)S(1)}, f32[4,512,128]{2,1,0:T(8,128)S(1)}, u32[]{:S(2)}, u32[]{:S(2)}) collective-permute-start(f32[4,512,128]{2,1,0:T(8,128)S(1)} %get-tuple-element.50), channel_id=1, source_target_pairs={{0,511},{1,2},{2,1},{3,4},{4,3},{5,6},{6,5},{7,8},{8,7},{9,10},{10... | collective-permute-start | bytes 3145736 | tf_op jit(solution)/shard_map/ppermute | solution.py:209
  41.6 7.5 %copy-start = (f32[1,512,128]{2,1,0:T(8,128)S(1)}, f32[1,512,128]{2,1,0:T(8,128)}, u32[]{:S(2)}) copy-start(f32[1,512,128]{2,1,0:T(8,128)} %param.5) | copy-start | bytes 786436
  53.0 10.8 %collective-permute-start.2 = (f32[2,512,128]{2,1,0:T(8,128)S(1)}, f32[2,512,128]{2,1,0:T(8,128)S(1)}, u32[]{:S(2)}, u32[]{:S(2)}) collective-permute-start(f32[2,512,128]{2,1,0:T(8,128)S(1)} %get-tuple-element.49.sent), channel_id=1, source_target_pairs={{0,511},{1,2},{2,1},{3,4},{4,3},{5,6},{6,5},{7,8},{8,7},{9,10},{10... | collective-permute-start | bytes 1572872 | tf_op jit(solution)/shard_map/ppermute | solution.py:209
  75.0 10.8 %collective-permute-start.4 = (f32[2,512,128]{2,1,0:T(8,128)S(1)}, f32[2,512,128]{2,1,0:T(8,128)S(1)}, u32[]{:S(2)}, u32[]{:S(2)}) collective-permute-start(f32[2,512,128]{2,1,0:T(8,128)S(1)} %shard_map.80.sent._), channel_id=1, source_target_pairs={{0,511},{1,2},{2,1},{3,4},{4,3},{5,6},{6,5},{7,8},{8,7},{9,10},{10... | collective-permute-start | bytes 1572872 | tf_op jit(solution)/shard_map/ppermute | solution.py:209
  94.3 9.8 %collective-permute-start.5 = (f32[512,128]{1,0:T(8,128)S(1)}, f32[512,128]{1,0:T(8,128)S(1)}, u32[]{:S(2)}, u32[]{:S(2)}) collective-permute-start(f32[512,128]{1,0:T(8,128)S(1)} %shard_map.82.d), channel_id=1, source_target_pairs={{0,511},{1,2},{2,1},{3,4},{4,3},{5,6},{6,5},{7,8},{8,7},{9,10},{10... | collective-permute-start | bytes 786440 | tf_op jit(solution)/shard_map/ppermute | solution.py:209

commit v5 on v4

--- a/solution.py
+++ b/solution.py
@@ -66,19 +66,20 @@
     return copies
 
 
-def first_kernel(rhs, inverse, w, e0, e1, b_in, e_in, b_sem, e_sem):
-    b_copies = fetch(rhs, b_in, b_sem)
-    e_copies = fetch(inverse, e_in, e_sem)
-    for copy in b_copies:
-        copy.wait()
+def first_kernel(rhs, inverse, w, b_in, e0, e1, e_in, b_sem, e_sem):
+    b_copy = pltpu.make_async_copy(rhs, b_in, b_sem)
+    e_copy = pltpu.make_async_copy(inverse, e_in, e_sem)
+    b_copy.start()
+    e_copy.start()
+    b_copy.wait()
     both = stack(b_in[...])
-    for copy, rows in zip(e_copies, blocks_of(inverse.shape[0])):
-        copy.wait()
-        put_split((e0, e1), e_in[rows], rows)
+    e_copy.wait()
+    put_split((e0, e1), e_in[...])
+    for rows in blocks_of(inverse.shape[0]):
         w[rows] = rows_times((e0, e1), rows, both)
 
 
-def blocks_kernel(odd, _, lower, upper, diag, e0, e1, h, h0, h1, j0, j1, n0, n1, f0, f1, d0, d1, n_in, f_in, d_in, n_sem, f_sem, d_sem):
+def blocks_kernel(odd, _, lower, upper, diag, e0, e1, h, j, h0, h1, j0, j1, n0, n1, f0, f1, d0, d1, n_in, f_in, d_in, n_sem, f_sem, d_sem):
     is_odd = odd[0] == 1
     n_copies = fetch_either(is_odd, lower, upper, n_in, n_sem)
     f_copies = fetch_either(is_odd, upper, lower, f_in, f_sem)
@@ -86,21 +87,21 @@
     cuts = blocks_of(diag.shape[0])
     cols = h.shape[2]
 
-    def product(parts, to, whole=None):
-        for k in range(h.shape[0]):
-            at = pl.ds(k * cols, cols)
+    def product(parts, to, whole):
+        for k in range(0, h.shape[0], 2):
+            at = pl.ds(k * cols, 2 * cols)
             both = jnp.concatenate([parts[0][:, at], parts[1][:, at]], axis=1)
             for rows in cuts:
                 value = rows_times((e0, e1), rows, both)
                 put_split(to, value, rows, at)
-                if whole is not None:
-                    whole[k, rows] = value
+                whole[k, rows] = value[:, :cols]
+                whole[k + 1, rows] = value[:, cols:]
 
     for copies, source, to in ((n_copies, n_in, (n0, n1)), (f_copies, f_in, (f0, f1)), (d_copies, d_in, (d0, d1))):
         for copy, rows in zip(copies, cuts):
             copy.wait()
             put_split(to, source[rows], rows)
-    product((n0, n1), (j0, j1))
+    product((n0, n1), (j0, j1), j)
     product((f0, f1), (h0, h1), h)
 
 
@@ -117,31 +118,51 @@
     out[1] = times((j0, j1), near[1 - odd[0]])
 
 
-def part_and_block_kernel(odd, s, near, j0, j1, h, out, h_out):
+def part_and_blocks_kernel(odd, s, near, j0, j1, h, j, out, h_out, j_out):
     part_kernel(odd, s, near, j0, j1, out)
 
 
-def front_kernel(sent, got, h0, h1, f, g):
-    n = f.shape[1]
-    both = times((h0, h1), jnp.concatenate([got[0], got[1]], axis=1))
-    f[...] = both[:, :n]
-    g[...] = sent[0] + both[:, n:]
-
-
-def step_kernel(odd, g, near, j0, j1, d):
-    d[...] = g[...] + times((j0, j1), near[1 - odd[0]])
-
-
-def step_rest_kernel(odd, g, near, r, j0, j1, d0, d1, d, rest):
-    step_kernel(odd, g, near, j0, j1, d)
-    rest[...] = r[...] - times((d0, d1), d[...])
-
-
-def again_kernel(odd, near, rest, d, n0, n1, e0, e1, out, rest_out):
-    value = rest[...] - times((n0, n1), near[1 - odd[0]])
-    rest_out[...] = value
-    out[0] = d[...]
-    out[1] = times((e0, e1), value)
+def twice_kernel(near_j, j0, j1, q0, q1):
+    cols = near_j.shape[2]
+    for k in range(0, near_j.shape[0], 2):
+        both = stack(jnp.concatenate([near_j[k], near_j[k + 1]], axis=1))
+        for rows in blocks_of(q0.shape[0]):
+            put_split((q0, q1), rows_times((j0, j1), rows, both), rows, pl.ds(k * cols, 2 * cols))
+
+
+def two_times(matrix, pair):
+    n = pair.shape[2]
+    both = times(matrix, jnp.concatenate([pair[0], pair[1]], axis=1))
+    return both[:, :n], both[:, n:]
+
+
+def front_kernel(sent, got, h0, h1, pair):
+    f, change = two_times((h0, h1), got)
+    pair[0] = f
+    pair[1] = sent[0] + change
+
+
+def last_front_kernel(_, sent, got, h0, h1, f, g):
+    value, change = two_times((h0, h1), got)
+    f[...] = value
+    g[...] = sent[0] + change
+
+
+def sent_kernel(sent, k0, k1, out):
+    out[...] = times((k0, k1), sent[0])
+
+
+def again_kernel(pair, near, effect, r, j0, j1, d0, d1, e0, e1, out, rest):
+    own, other = two_times((j0, j1), near)
+    change = pair[1] + own
+    value = r[...] - times((d0, d1), change)
+    rest[...] = value
+    out[0] = change
+    out[1] = times((e0, e1), value) - other - effect[...]
+
+
+def near_rest_kernel(odd, near, before, n0, n1, rest):
+    rest[...] = before[...] - times((n0, n1), near[1 - odd[0]])
 
 
 def split_kernel(k_in, k0, k1):
@@ -150,29 +171,35 @@
         put_split((k0, k1), k_in[i], slice(None), pl.ds(i * cols, cols))
 
 
-def sent_kernel(sent, k0, k1, out):
-    out[...] = times((k0, k1), sent[0])
-
-
-def both_w_kernel(sent, got, effect, h0, h1, w, base):
-    n = w.shape[1]
+def both_w_kernel(sent, got, effect, h0, h1, pair):
+    n = pair.shape[2]
     both = times((h0, h1), jnp.concatenate([got[0], got[1] - effect[...]], axis=1))
-    value = sent[1] - both[:, :n]
-    w[...] = value
-    base[...] = value - both[:, n:]
-
-
-def base_kernel(odd, base, near, j0, j1, s):
-    s[...] = base[...] - times((j0, j1), near[1 - odd[0]])
+    w = sent[1] - both[:, :n]
+    pair[0] = w
+    pair[1] = w - both[:, n:]
+
+
+def both_s_kernel(pair, near, effect, j0, j1, out):
+    own, other = two_times((j0, j1), near)
+    out[0] = pair[1] - own
+    out[1] = other - effect[...]
+
+
+def step_kernel(odd, g, near, j0, j1, d):
+    d[...] = g[...] + times((j0, j1), near[1 - odd[0]])
 
 
 def residual_kernel(_, rest, got, f0, f1, r):
     r[...] = rest[...] - times((f0, f1), got[0])
 
 
-def sum_kernel(odd, near, r, d, first, n0, n1, d0, d1, rest, x):
-    rest[...] = r[...] - times((d0, d1), d[...]) - times((n0, n1), near[1 - odd[0]])
-    x[0] = first[...] + d[...]
+def sum_kernel(r, d, first, d0, d1, rest, x):
+    rest[...] = r[...] - times((d0, d1), d[...])
+    x[0] = first[0] + d[...]
+
+
+def swapped_rest_kernel(near, before, n0, n1, rest):
+    rest[...] = before[...] - times((n0, n1), near[...])
 
 
 def last_kernel(rest, got, f0, f1, r):
@@ -222,40 +249,47 @@
     def in_hbm(*arrays):
         return [pltpu.with_memory_space_constraint(a, pltpu.HBM) for a in arrays]
 
-    w, *E = call(
-        first_kernel, [vec] + half, *in_hbm(b, inverse), specs=[HBM] * 2,
-        scratch=[pltpu.VMEM((size, cols), F32), square, dmas, dmas],
+    w, b, *E = call(
+        first_kernel, [vec, vec] + half, *in_hbm(b, inverse), specs=[HBM] * 2,
+        scratch=[square] + [pltpu.SemaphoreType.DMA(())] * 2,
     )
     w_far = far(w)
-    h, *mats = call(
-        blocks_kernel, [blocks] + half * 5, odd, w, *in_hbm(lower, upper, diag), *E,
+    h, j, *mats = call(
+        blocks_kernel, [blocks] * 2 + half * 5, odd, w, *in_hbm(lower, upper, diag), *E,
         specs=[SMEM, ANY] + [HBM] * 3 + [VMEM] * 2, scratch=[square] * 3 + [dmas] * 3, products=10,
     )
     H, J, N, F, D = (mats[i:i + 2] for i in range(0, 10, 2))
     (part,) = call(near_part_kernel, [vec], odd, w, near(w), *J)
     (s,) = call(second_kernel, [vec], part, w_far, *H)
-    sent, h = call(
-        part_and_block_kernel, [two, blocks], odd, s, near(s), *J, h,
-        specs=[SMEM] + [VMEM] * 4 + [ANY], outs_at=[VMEM, ANY], aliases={5: 1},
+    sent, h, j = call(
+        part_and_blocks_kernel, [two, blocks, blocks], odd, s, near(s), *J, h, j,
+        specs=[SMEM] + [VMEM] * 4 + [ANY] * 2, outs_at=[VMEM, ANY, ANY], aliases={5: 1, 6: 2},
     )
     got = far(sent)
     k_in = far(h)
-    f, g = call(front_kernel, [vec, vec], sent, got, *H, products=20)
-    first, rest = call(step_rest_kernel, [vec, vec], odd, g, near(f), b, *J, *D)
-    sent, rest = call(again_kernel, [two, vec], odd, near(first), rest, first, *N, *E)
+    Q = call(twice_kernel, half, swap_near(j), *J)
+    (pair,) = call(front_kernel, [two], sent, got, *H, products=20)
+    other = swap_near(pair)
+    (effect,) = call(sent_kernel, [vec], pair, *Q, products=1)
+    sent, rest = call(again_kernel, [two, vec], pair, other, effect, b, *J, *D, *E)
     got = far(sent)
     K = call(split_kernel, half, k_in)
     (effect,) = call(sent_kernel, [vec], sent, *K)
-    w, base = call(both_w_kernel, [vec, vec], sent, got, effect, *H)
-
-    (s,) = call(base_kernel, [vec], odd, base, near(w), *J)
-    (sent,) = call(part_kernel, [two], odd, s, near(s), *J)
+    (rest,) = call(near_rest_kernel, [vec], odd, near(sent[0]), rest, *N)
+    first = sent
+    (pair,) = call(both_w_kernel, [two], sent, got, effect, *H)
+
+    other = swap_near(pair)
+    (effect,) = call(sent_kernel, [vec], pair, *Q)
+    (sent,) = call(both_s_kernel, [two], pair, other, effect, *J)
     (r,) = call(residual_kernel, [vec], sent, rest, got, *F, specs=[ANY] + [VMEM] * 4)
-    f, g = call(front_kernel, [vec, vec], sent, far(sent), *H)
+    f, g = call(last_front_kernel, [vec, vec], r, sent, far(sent), *H, specs=[ANY] + [VMEM] * 4)
     (d,) = call(step_kernel, [vec], odd, g, near(f), *J)
     got = far(d)
     one = ((1, size, cols), F32)
-    rest, x = call(sum_kernel, [vec, one], odd, near(d), r, d, first, *N, *D)
+    other = swap_near(d)
+    rest, x = call(sum_kernel, [vec, one], r, d, first, *D, products=20)
+    (rest,) = call(swapped_rest_kernel, [vec], other, rest, *N)
     (r,) = call(last_kernel, [one], rest, got, *F)
     return x, r
 

time: 106 us -> 103 us (0.972)
  starting transfers between devices: 15.8 us -> 41.1 us
  blocking collectives: 49.2 us -> 30.1 us
  waiting for transfers between devices: 22.3 us -> 11.9 us
  Pallas kernels: 17.1 us -> 18.9 us
    ppermute x0 -> x4, starting transfers between devices: none -> 27 us  [swap_near(): return lax.ppermute(v, AXIS, near_pairs)]
    all_gather x8 -> x4, blocking collectives: 49.2 us -> 30.1 us  [near(): return lax.all_gather(v, AXIS, axis_index_groups=near_groups)]
    ppermute x6, waiting for transfers between devices: 22.3 us -> 10.7 us  [far(): return lax.ppermute(v, AXIS, far_pairs)]
    pallas_call x18 -> x21, Pallas kernels: 17.1 us -> 18.9 us  [call(): pl.pallas_call(kernel, out_shape=[jax.ShapeDtypeStruct(shape, dtype) for...]
    ppermute x6, starting transfers between devices: 15.8 us -> 14.1 us  [far(): return lax.ppermute(v, AXIS, far_pairs)]
    ppermute x0 -> x4, waiting for transfers between devices: none -> 1.16 us  [swap_near(): return lax.ppermute(v, AXIS, near_pairs)]
  transfers between devices with their start and end apart: 6 -> 10, of which waited for: 3 -> 6; matrix products, arithmetic and copies ran while one was open for 0% -> 0% of each run, Pallas kernels for 9% -> 12%
where the time goes in v5:
time: 103 us
  starting transfers between devices  41.1 us (40%)
  blocking collectives  30.1 us (29%)
  Pallas kernels  18.9 us (18%)
  waiting for transfers between devices  11.9 us (12%)
    all_gather x4, blocking collectives, near(): return lax.all_gather(v, AXIS, axis_index_groups=near_groups)  30.1 us
    ppermute x4, starting transfers between devices, swap_near(): return lax.ppermute(v, AXIS, near_pairs)  27 us
    pallas_call x21, Pallas kernels, call(): pl.pallas_call(kernel, out_shape=[jax.ShapeDtypeStruct(shape, dtype) for...  18.9 us
    ppermute x6, starting transfers between devices, far(): return lax.ppermute(v, AXIS, far_pairs)  14.1 us
    ppermute x6, waiting for transfers between devices, far(): return lax.ppermute(v, AXIS, far_pairs)  10.7 us
  transfers between devices with their start and end apart: 10, of which 6 were waited for; matrix products, arithmetic and copies ran while one was open for 0% of the time, Pallas kernels for 12%

profile of v5, /device:TPU:1, one launch (start us, length us, event | category | flops | bytes accessed | tf_op | source)
XLA Modules:
  0.0 102.9 jit_solution(2887365769123311299)
XLA Ops:
  0.6 1.8 %shard_map.68 = (f32[512,128]{1,0:T(8,128)S(1)}, f32[512,128]{1,0:T(8,128)S(1)}, bf16[512,512]{1,0:T(8,128)(2,1)S(1)}, bf16[512,512]{1,0:T(8,128)(2,1)S(1)}) custom-call(f32[512,128]{1,0:T(8,128)} %bitcast.13, f32[512,512]{1,0:T(8,128)} %bitcast.12), custom_call_target="tpu_custom_call" | custom-call | flops 268435456 | bytes 1048576 | tf_op jit(solution)/shard_map/pallas_call | solution.py:210
  2.4 4.5 %collective-permute-start = (f32[512,128]{1,0:T(8,128)S(1)}, f32[512,128]{1,0:T(8,128)S(1)}, u32[]{:S(2)}, u32[]{:S(2)}) collective-permute-start(f32[512,128]{1,0:T(8,128)S(1)} %get-tuple-element.31._.w), channel_id=1, source_target_pairs={{0,511},{1,2},{2,1},{3,4},{4,3},{5,6},{6,5},{7,8},{8,7},{9,10},{10... | collective-permute-start | bytes 786440 | tf_op jit(solution)/shard_map/ppermute | solution.py:236
  7.0 14.3 %all-gather = f32[1024,128]{1,0:T(8,128)S(1)} all-gather(f32[512,128]{1,0:T(8,128)S(1)} %get-tuple-element.31._.w), channel_id=2, replica_groups={{0,1},{2,3},{4,5},{6,7},{8,9},{10,11},{12,13},{14,15},{16,17},{18,19},{..., dimensions={0}, use_global_device_ids=true | all-gather | bytes 786432 | tf_op jit(solution)/shard_map/all_gather | solution.py:230
  21.3 4.4 %shard_map.69 = (f32[4,512,128]{2,1,0:T(8,128)S(1)}, f32[4,512,128]{2,1,0:T(8,128)S(1)}, bf16[512,512]{1,0:T(8,128)(2,1)S(1)}, bf16[512,512]{1,0:T(8,128)(2,1)S(...) custom-call(s32[1]{0:T(128)} %bitcast.odd, ...), custom_call_target="tpu_custom_call" | custom-call | flops 2684354560 | bytes 1048576 | tf_op jit(solution)/shard_map/pallas_call | solution.py:210
  25.6 0.5 shard_map.70.part
  26.1 0.0 collective-permute-done.got
  26.1 0.5 shard_map.71.s
  26.6 2.4 %all-gather.1 = f32[1024,128]{1,0:T(8,128)S(1)} all-gather(f32[512,128]{1,0:T(8,128)S(1)} %shard_map.71.s), channel_id=3, replica_groups={{0,1},{2,3},{4,5},{6,7},{8,9},{10,11},{12,13},{14,15},{16,17},{18,19},{..., dimensions={0}, use_global_device_ids=true | all-gather | bytes 786432 | tf_op jit(solution)/shard_map/all_gather | solution.py:230
  28.9 0.5 shard_map.72
  29.4 1.9 %collective-permute-start.1 = (f32[2,512,128]{2,1,0:T(8,128)S(1)}, f32[2,512,128]{2,1,0:T(8,128)S(1)}, u32[]{:S(2)}, u32[]{:S(2)}) collective-permute-start(f32[2,512,128]{2,1,0:T(8,128)S(1)} %get-tuple-element.40.sent), channel_id=1, source_target_pairs={{0,511},{1,2},{2,1},{3,4},{4,3},{5,6},{6,5},{7,8},{8,7},{9,10},{10... | collective-permute-start | bytes 1572872 | tf_op jit(solution)/shard_map/ppermute | solution.py:236
  31.3 6.2 %collective-permute-start.3 = (f32[4,512,128]{2,1,0:T(8,128)S(1)}, f32[4,512,128]{2,1,0:T(8,128)S(1)}, u32[]{:S(2)}, u32[]{:S(2)}) collective-permute-start(f32[4,512,128]{2,1,0:T(8,128)S(1)} %get-tuple-element.41), channel_id=1, source_target_pairs={{0,1},{1,0},{2,3},{3,2},{4,5},{5,4},{6,7},{7,6},{8,9},{9,8},{10,11... | collective-permute-start | bytes 3145736 | tf_op jit(solution)/shard_map/ppermute | solution.py:233
  37.6 1.9 %collective-permute-start.5 = (f32[4,512,128]{2,1,0:T(8,128)S(1)}, f32[4,512,128]{2,1,0:T(8,128)S(1)}, u32[]{:S(2)}, u32[]{:S(2)}) collective-permute-start(f32[4,512,128]{2,1,0:T(8,128)S(1)} %get-tuple-element.48), channel_id=1, source_target_pairs={{0,511},{1,2},{2,1},{3,4},{4,3},{5,6},{6,5},{7,8},{8,7},{9,10},{10... | collective-permute-start | bytes 3145736 | tf_op jit(solution)/shard_map/ppermute | solution.py:236
  39.5 0.7 collective-permute-done.1.got
  40.2 0.7 shard_map.73.sent.pair
  40.9 7.4 %collective-permute-start.2 = (f32[2,512,128]{2,1,0:T(8,128)S(1)}, f32[2,512,128]{2,1,0:T(8,128)S(1)}, u32[]{:S(2)}, u32[]{:S(2)}) collective-permute-start(f32[2,512,128]{2,1,0:T(8,128)S(1)} %shard_map.73.sent.pair), channel_id=1, source_target_pairs={{0,1},{1,0},{2,3},{3,2},{4,5},{5,4},{6,7},{7,6},{8,9},{9,8},{10,11... | collective-permute-start | bytes 1572872 | tf_op jit(solution)/shard_map/ppermute | solution.py:233
  48.4 0.0 collective-permute-done.3.near_j
  48.4 1.3 %shard_map.74 = (bf16[512,512]{1,0:T(8,128)(2,1)S(1)}, bf16[512,512]{1,0:T(8,128)(2,1)S(1)}) custom-call(f32[4,512,128]{2,1,0:T(8,128)S(1)} %collective-permute-done.3.near_j, bf16[512,512]{1,0:T(8,128)(2,1)S(1)} %get-tuple-element.34.j0, bf16[512,512]{1,0:T(8,128)(2,1)S(1)} %get-tuple-element.35.j1), custom_call_target="tpu_custom_call" | custom-call | flops 268435456 | bytes 1048576 | tf_op jit(solution)/shard_map/pallas_call | solution.py:210
  49.7 0.4 shard_map.75.effect
  50.2 0.0 collective-permute-done.2.near
  50.2 1.5 %shard_map.76 = (f32[2,512,128]{2,1,0:T(8,128)S(1)}, f32[512,128]{1,0:T(8,128)S(1)}) custom-call(f32[2,512,128]{2,1,0:T(8,128)S(1)} %shard_map.73.sent.pair, f32[2,512,128]{2,1,0:T(8,128)S(1)} %collective-permute-done.2.near, f32[512,128]{1,0:T(8,128)S(1)} %shard_map.75.effect, f32[512,128]{1,0:T(8,128)S(1)} %get-tuple-element.44.r, ...), custom_call_target="tpu_custom_call" | custom-call | flops 268435456 | bytes 1048576 | tf_op jit(solution)/shard_map/pallas_call | solution.py:210
  51.7 1.9 %collective-permute-start.4 = (f32[2,512,128]{2,1,0:T(8,128)S(1)}, f32[2,512,128]{2,1,0:T(8,128)S(1)}, u32[]{:S(2)}, u32[]{:S(2)}) collective-permute-start(f32[2,512,128]{2,1,0:T(8,128)S(1)} %get-tuple-element.47.sent.first), channel_id=1, source_target_pairs={{0,511},{1,2},{2,1},{3,4},{4,3},{5,6},{6,5},{7,8},{8,7},{9,10},{10... | collective-permute-start | bytes 1572872 | tf_op jit(solution)/shard_map/ppermute | solution.py:236
  53.7 0.4 collective-permute-done.5.k_in
  54.0 0.2 shard_map.77
  54.2 0.4 shard_map.78.effect
  54.7 7.8 %collective-permute-done.4.got = f32[2,512,128]{2,1,0:T(8,128)S(1)} collective-permute-done((f32[2,512,128]{2,1,0:T(8,128)S(1)}, f32[2,512,128]{2,1,0:T(8,128)S(1)}, u32[]{:S(2)}, u32[]{:S(2)}) %collective-permute-start.4) | collective-permute-done | bytes 524320 | tf_op jit(solution)/shard_map/ppermute | solution.py:236
  62.5 0.7 shard_map.79.sent.pair
  63.3 7.1 %collective-permute-start.6 = (f32[2,512,128]{2,1,0:T(8,128)S(1)}, f32[2,512,128]{2,1,0:T(8,128)S(1)}, u32[]{:S(2)}, u32[]{:S(2)}) collective-permute-start(f32[2,512,128]{2,1,0:T(8,128)S(1)} %shard_map.79.sent.pair), channel_id=1, source_target_pairs={{0,1},{1,0},{2,3},{3,2},{4,5},{5,4},{6,7},{7,6},{8,9},{9,8},{10,11... | collective-permute-start | bytes 1572872 | tf_op jit(solution)/shard_map/ppermute | solution.py:233
  70.4 0.4 shard_map.80.effect
  70.9 1.1 %collective-permute-done.6.near = f32[2,512,128]{2,1,0:T(8,128)S(1)} collective-permute-done((f32[2,512,128]{2,1,0:T(8,128)S(1)}, f32[2,512,128]{2,1,0:T(8,128)S(1)}, u32[]{:S(2)}, u32[]{:S(2)}) %collective-permute-start.6) | collective-permute-done | bytes 524320 | tf_op jit(solution)/shard_map/ppermute | solution.py:233
  71.9 0.7 shard_map.81._.sent
  72.7 1.9 %collective-permute-start.7 = (f32[2,512,128]{2,1,0:T(8,128)S(1)}, f32[2,512,128]{2,1,0:T(8,128)S(1)}, u32[]{:S(2)}, u32[]{:S(2)}) collective-permute-start(f32[2,512,128]{2,1,0:T(8,128)S(1)} %shard_map.81._.sent), channel_id=1, source_target_pairs={{0,511},{1,2},{2,1},{3,4},{4,3},{5,6},{6,5},{7,8},{8,7},{9,10},{10... | collective-permute-start | bytes 1572872 | tf_op jit(solution)/shard_map/ppermute | solution.py:236
  74.6 6.1 %all_gather.25.near = f32[2,512,128]{2,1,0:T(8,128)S(1)} all-gather(f32[1,512,128]{2,1,0:T(8,128)S(1)} %slice.3), channel_id=1, replica_groups={{0,1},{2,3},{4,5},{6,7},{8,9},{10,11},{12,13},{14,15},{16,17},{18,19},{..., dimensions={0}, use_global_device_ids=true | all-gather | bytes 786432 | tf_op jit(solution)/shard_map/all_gather | solution.py:230
  80.7 0.5 shard_map.82.rest
  81.2 0.5 shard_map.83._.r
  81.6 1.8 %collective-permute-done.7.got = f32[2,512,128]{2,1,0:T(8,128)S(1)} collective-permute-done((f32[2,512,128]{2,1,0:T(8,128)S(1)}, f32[2,512,128]{2,1,0:T(8,128)S(1)}, u32[]{:S(2)}, u32[]{:S(2)}) %collective-permute-start.7) | collective-permute-done | bytes 524320 | tf_op jit(solution)/shard_map/ppermute | solution.py:236
  83.4 0.7 shard_map.84
  84.2 7.3 %all-gather.2 = f32[1024,128]{1,0:T(8,128)S(1)} all-gather(f32[512,128]{1,0:T(8,128)S(1)} %get-tuple-element.57), channel_id=4, replica_groups={{0,1},{2,3},{4,5},{6,7},{8,9},{10,11},{12,13},{14,15},{16,17},{18,19},{..., dimensions={0}, use_global_device_ids=true | all-gather | bytes 786432 | tf_op jit(solution)/shard_map/all_gather | solution.py:230
  91.5 0.5 shard_map.85.d
  92.0 1.9 %collective-permute-start.9 = (f32[512,128]{1,0:T(8,128)S(1)}, f32[512,128]{1,0:T(8,128)S(1)}, u32[]{:S(2)}, u32[]{:S(2)}) collective-permute-start(f32[512,128]{1,0:T(8,128)S(1)} %shard_map.85.d), channel_id=1, source_target_pairs={{0,511},{1,2},{2,1},{3,4},{4,3},{5,6},{6,5},{7,8},{8,7},{9,10},{10... | collective-permute-start | bytes 786440 | tf_op jit(solution)/shard_map/ppermute | solution.py:236
  93.9 6.2 %collective-permute-start.8 = (f32[512,128]{1,0:T(8,128)S(1)}, f32[512,128]{1,0:T(8,128)S(1)}, u32[]{:S(2)}, u32[]{:S(2)}) collective-permute-start(f32[512,128]{1,0:T(8,128)S(1)} %shard_map.85.d), channel_id=1, source_target_pairs={{0,1},{1,0},{2,3},{3,2},{4,5},{5,4},{6,7},{7,6},{8,9},{9,8},{10,11... | collective-permute-start | bytes 786440 | tf_op jit(solution)/shard_map/ppermute | solution.py:233
  100.1 1.1 %shard_map.86 = (f32[512,128]{1,0:T(8,128)S(1)}, f32[1,512,128]{2,1,0:T(8,128)}) custom-call(f32[512,128]{1,0:T(8,128)S(1)} %shard_map.83._.r, f32[512,128]{1,0:T(8,128)S(1)} %shard_map.85.d, f32[2,512,128]{2,1,0:T(8,128)S(1)} %get-tuple-element.47.sent.first, bf16[512,512]{1,0:T(8,128)(2,1)S(1)} %get-tuple-element.45.d0, ...), custom_call_target="tpu_custom_call" | custom-call | flops 5368709120 | bytes 1048576 | tf_op jit(solution)/shard_map/pallas_call | solution.py:210
  101.2 0.1 collective-permute-done.8.near
  101.2 0.4 shard_map.87.rest
  101.7 0.0 collective-permute-done.9.got
  101.7 1.2 %shard_map.88 = f32[1,512,128]{2,1,0:T(8,128)} custom-call(f32[512,128]{1,0:T(8,128)S(1)} %shard_map.87.rest, f32[512,128]{1,0:T(8,128)S(1)} %collective-permute-done.9.got, bf16[512,512]{1,0:T(8,128)(2,1)S(1)} %get-tuple-element.54.f0, bf16[512,512]{1,0:T(8,128)(2,1)S(1)} %get-tuple-element.55.f1), custom_call_target="tpu_custom_call" | custom-call | flops 268435456 | bytes 1048576 | tf_op jit(solution)/shard_map/pallas_call | solution.py:210
  (1 shorter events, 0.0 us)
Async XLA Ops:
  2.4 23.7 %collective-permute-start = (f32[512,128]{1,0:T(8,128)S(1)}, f32[512,128]{1,0:T(8,128)S(1)}, u32[]{:S(2)}, u32[]{:S(2)}) collective-permute-start(f32[512,128]{1,0:T(8,128)S(1)} %get-tuple-element.31._.w), channel_id=1, source_target_pairs={{0,511},{1,2},{2,1},{3,4},{4,3},{5,6},{6,5},{7,8},{8,7},{9,10},{10... | collective-permute-start | bytes 786440 | tf_op jit(solution)/shard_map/ppermute | solution.py:236
  29.4 10.8 %collective-permute-start.1 = (f32[2,512,128]{2,1,0:T(8,128)S(1)}, f32[2,512,128]{2,1,0:T(8,128)S(1)}, u32[]{:S(2)}, u32[]{:S(2)}) collective-permute-start(f32[2,512,128]{2,1,0:T(8,128)S(1)} %get-tuple-element.40.sent), channel_id=1, source_target_pairs={{0,511},{1,2},{2,1},{3,4},{4,3},{5,6},{6,5},{7,8},{8,7},{9,10},{10... | collective-permute-start | bytes 1572872 | tf_op jit(solution)/shard_map/ppermute | solution.py:236
  31.3 17.0 %collective-permute-start.3 = (f32[4,512,128]{2,1,0:T(8,128)S(1)}, f32[4,512,128]{2,1,0:T(8,128)S(1)}, u32[]{:S(2)}, u32[]{:S(2)}) collective-permute-start(f32[4,512,128]{2,1,0:T(8,128)S(1)} %get-tuple-element.41), channel_id=1, source_target_pairs={{0,1},{1,0},{2,3},{3,2},{4,5},{5,4},{6,7},{7,6},{8,9},{9,8},{10,11... | collective-permute-start | bytes 3145736 | tf_op jit(solution)/shard_map/ppermute | solution.py:233
  37.6 16.4 %collective-permute-start.5 = (f32[4,512,128]{2,1,0:T(8,128)S(1)}, f32[4,512,128]{2,1,0:T(8,128)S(1)}, u32[]{:S(2)}, u32[]{:S(2)}) collective-permute-start(f32[4,512,128]{2,1,0:T(8,128)S(1)} %get-tuple-element.48), channel_id=1, source_target_pairs={{0,511},{1,2},{2,1},{3,4},{4,3},{5,6},{6,5},{7,8},{8,7},{9,10},{10... | collective-permute-start | bytes 3145736 | tf_op jit(solution)/shard_map/ppermute | solution.py:236
  40.9 9.2 %collective-permute-start.2 = (f32[2,512,128]{2,1,0:T(8,128)S(1)}, f32[2,512,128]{2,1,0:T(8,128)S(1)}, u32[]{:S(2)}, u32[]{:S(2)}) collective-permute-start(f32[2,512,128]{2,1,0:T(8,128)S(1)} %shard_map.73.sent.pair), channel_id=1, source_target_pairs={{0,1},{1,0},{2,3},{3,2},{4,5},{5,4},{6,7},{7,6},{8,9},{9,8},{10,11... | collective-permute-start | bytes 1572872 | tf_op jit(solution)/shard_map/ppermute | solution.py:233
  51.7 10.8 %collective-permute-start.4 = (f32[2,512,128]{2,1,0:T(8,128)S(1)}, f32[2,512,128]{2,1,0:T(8,128)S(1)}, u32[]{:S(2)}, u32[]{:S(2)}) collective-permute-start(f32[2,512,128]{2,1,0:T(8,128)S(1)} %get-tuple-element.47.sent.first), channel_id=1, source_target_pairs={{0,511},{1,2},{2,1},{3,4},{4,3},{5,6},{6,5},{7,8},{8,7},{9,10},{10... | collective-permute-start | bytes 1572872 | tf_op jit(solution)/shard_map/ppermute | solution.py:236
  63.3 8.7 %collective-permute-start.6 = (f32[2,512,128]{2,1,0:T(8,128)S(1)}, f32[2,512,128]{2,1,0:T(8,128)S(1)}, u32[]{:S(2)}, u32[]{:S(2)}) collective-permute-start(f32[2,512,128]{2,1,0:T(8,128)S(1)} %shard_map.79.sent.pair), channel_id=1, source_target_pairs={{0,1},{1,0},{2,3},{3,2},{4,5},{5,4},{6,7},{7,6},{8,9},{9,8},{10,11... | collective-permute-start | bytes 1572872 | tf_op jit(solution)/shard_map/ppermute | solution.py:233
  72.7 10.8 %collective-permute-start.7 = (f32[2,512,128]{2,1,0:T(8,128)S(1)}, f32[2,512,128]{2,1,0:T(8,128)S(1)}, u32[]{:S(2)}, u32[]{:S(2)}) collective-permute-start(f32[2,512,128]{2,1,0:T(8,128)S(1)} %shard_map.81._.sent), channel_id=1, source_target_pairs={{0,511},{1,2},{2,1},{3,4},{4,3},{5,6},{6,5},{7,8},{8,7},{9,10},{10... | collective-permute-start | bytes 1572872 | tf_op jit(solution)/shard_map/ppermute | solution.py:236
  92.0 9.7 %collective-permute-start.9 = (f32[512,128]{1,0:T(8,128)S(1)}, f32[512,128]{1,0:T(8,128)S(1)}, u32[]{:S(2)}, u32[]{:S(2)}) collective-permute-start(f32[512,128]{1,0:T(8,128)S(1)} %shard_map.85.d), channel_id=1, source_target_pairs={{0,511},{1,2},{2,1},{3,4},{4,3},{5,6},{6,5},{7,8},{8,7},{9,10},{10... | collective-permute-start | bytes 786440 | tf_op jit(solution)/shard_map/ppermute | solution.py:236
  93.9 7.4 %collective-permute-start.8 = (f32[512,128]{1,0:T(8,128)S(1)}, f32[512,128]{1,0:T(8,128)S(1)}, u32[]{:S(2)}, u32[]{:S(2)}) collective-permute-start(f32[512,128]{1,0:T(8,128)S(1)} %shard_map.85.d), channel_id=1, source_target_pairs={{0,1},{1,0},{2,3},{3,2},{4,5},{5,4},{6,7},{7,6},{8,9},{9,8},{10,11... | collective-permute-start | bytes 786440 | tf_op jit(solution)/shard_map/ppermute | solution.py:233

commit v6 on v5

--- a/solution.py
+++ b/solution.py
@@ -26,8 +26,9 @@
 
 
 def rows_times(matrix, rows, both):
-    out = jnp.dot(matrix[0][rows, :], both, preferred_element_type=F32)
-    out += jnp.dot(matrix[1][rows, :], both, preferred_element_type=F32)
+    parts = jnp.concatenate([matrix[0][rows, :], matrix[1][rows, :]], axis=0)
+    out = jnp.dot(parts, both, preferred_element_type=F32)
+    out = out[:ROWS] + out[ROWS:]
     n = both.shape[1] // 2
     return out[:, :n] + out[:, n:]
 
@@ -193,17 +194,11 @@
     r[...] = rest[...] - times((f0, f1), got[0])
 
 
-def sum_kernel(r, d, first, d0, d1, rest, x):
-    rest[...] = r[...] - times((d0, d1), d[...])
-    x[0] = first[0] + d[...]
-
-
-def swapped_rest_kernel(near, before, n0, n1, rest):
-    rest[...] = before[...] - times((n0, n1), near[...])
-
-
-def last_kernel(rest, got, f0, f1, r):
-    r[0] = rest[...] - times((f0, f1), got[...])
+def last_kernel(odd, near, r_before, got, first, d, d0, d1, n0, n1, f0, f1, x, r):
+    change = d[...]
+    x[0] = first[0] + change
+    rest = r_before[...] - times((d0, d1), change) - times((f0, f1), got[...])
+    r[0] = rest - times((n0, n1), near[1 - odd[0]])
 
 
 def call(kernel, outs, *args, specs=None, scratch=(), limit=16, products=1, aliases={}, outs_at=None):
@@ -287,11 +282,7 @@
     (d,) = call(step_kernel, [vec], odd, g, near(f), *J)
     got = far(d)
     one = ((1, size, cols), F32)
-    other = swap_near(d)
-    rest, x = call(sum_kernel, [vec, one], r, d, first, *D, products=20)
-    (rest,) = call(swapped_rest_kernel, [vec], other, rest, *N)
-    (r,) = call(last_kernel, [one], rest, got, *F)
-    return x, r
+    return tuple(call(last_kernel, [one, one], odd, near(d), r, got, first, d, *D, *N, *F))
 
 
 def solution(mesh):

time: 103 us -> 102 us (level)
  blocking collectives: 30.1 us -> 36.4 us
  starting transfers between devices: 41.1 us -> 35 us
  Pallas kernels: 18.9 us -> 17.6 us
    all_gather x4 -> x5, blocking collectives: 30.1 us -> 36.4 us  [near(): return lax.all_gather(v, AXIS, axis_index_groups=near_groups)]
    ppermute x4 -> x3, starting transfers between devices: 27 us -> 20.9 us  [swap_near(): return lax.ppermute(v, AXIS, near_pairs)]
    pallas_call x21 -> x19, Pallas kernels: 18.9 us -> 17.6 us  [call(): pl.pallas_call(kernel, out_shape=[jax.ShapeDtypeStruct(shape, dtype) for...]
  transfers between devices with their start and end apart: 10 -> 9, of which waited for: 6 -> 5; matrix products, arithmetic and copies ran while one was open for 0% -> 0% of each run, Pallas kernels for 12% -> 10%
where the time goes in v6:
time: 102 us
  blocking collectives  36.4 us (36%)
  starting transfers between devices  35 us (34%)
  Pallas kernels  17.6 us (17%)
  waiting for transfers between devices  11.6 us (11%)
    all_gather x5, blocking collectives, near(): return lax.all_gather(v, AXIS, axis_index_groups=near_groups)  36.4 us
    ppermute x3, starting transfers between devices, swap_near(): return lax.ppermute(v, AXIS, near_pairs)  20.9 us
    pallas_call x19, Pallas kernels, call(): pl.pallas_call(kernel, out_shape=[jax.ShapeDtypeStruct(shape, dtype) for...  17.6 us
    ppermute x6, starting transfers between devices, far(): return lax.ppermute(v, AXIS, far_pairs)  14.1 us
    ppermute x6, waiting for transfers between devices, far(): return lax.ppermute(v, AXIS, far_pairs)  10.5 us
  transfers between devices with their start and end apart: 9, of which 5 were waited for; matrix products, arithmetic and copies ran while one was open for 0% of the time, Pallas kernels for 10%

profile of v6, /device:TPU:1, one launch (start us, length us, event | category | flops | bytes accessed | tf_op | source)
XLA Modules:
  0.0 101.5 jit_solution(11954342790956797240)
XLA Ops:
  0.6 1.8 %shard_map.68 = (f32[512,128]{1,0:T(8,128)S(1)}, f32[512,128]{1,0:T(8,128)S(1)}, bf16[512,512]{1,0:T(8,128)(2,1)S(1)}, bf16[512,512]{1,0:T(8,128)(2,1)S(1)}) custom-call(f32[512,128]{1,0:T(8,128)} %bitcast.15, f32[512,512]{1,0:T(8,128)} %bitcast.14), custom_call_target="tpu_custom_call" | custom-call | flops 268435456 | bytes 1048576 | tf_op jit(solution)/shard_map/pallas_call | solution.py:205
  2.4 4.5 %collective-permute-start = (f32[512,128]{1,0:T(8,128)S(1)}, f32[512,128]{1,0:T(8,128)S(1)}, u32[]{:S(2)}, u32[]{:S(2)}) collective-permute-start(f32[512,128]{1,0:T(8,128)S(1)} %get-tuple-element.29._.w), channel_id=1, source_target_pairs={{0,511},{1,2},{2,1},{3,4},{4,3},{5,6},{6,5},{7,8},{8,7},{9,10},{10... | collective-permute-start | bytes 786440 | tf_op jit(solution)/shard_map/ppermute | solution.py:231
  7.0 14.3 %all-gather = f32[1024,128]{1,0:T(8,128)S(1)} all-gather(f32[512,128]{1,0:T(8,128)S(1)} %get-tuple-element.29._.w), channel_id=2, replica_groups={{0,1},{2,3},{4,5},{6,7},{8,9},{10,11},{12,13},{14,15},{16,17},{18,19},{..., dimensions={0}, use_global_device_ids=true | all-gather | bytes 786432 | tf_op jit(solution)/shard_map/all_gather | solution.py:225
  21.2 4.3 %shard_map.69 = (f32[4,512,128]{2,1,0:T(8,128)S(1)}, f32[4,512,128]{2,1,0:T(8,128)S(1)}, bf16[512,512]{1,0:T(8,128)(2,1)S(1)}, bf16[512,512]{1,0:T(8,128)(2,1)S(...) custom-call(s32[1]{0:T(128)} %bitcast.odd, ...), custom_call_target="tpu_custom_call" | custom-call | flops 2684354560 | bytes 1048576 | tf_op jit(solution)/shard_map/pallas_call | solution.py:205
  25.6 0.4 shard_map.70.part
  26.0 0.0 collective-permute-done.got
  26.0 0.4 shard_map.71.s
  26.5 2.4 %all-gather.1 = f32[1024,128]{1,0:T(8,128)S(1)} all-gather(f32[512,128]{1,0:T(8,128)S(1)} %shard_map.71.s), channel_id=3, replica_groups={{0,1},{2,3},{4,5},{6,7},{8,9},{10,11},{12,13},{14,15},{16,17},{18,19},{..., dimensions={0}, use_global_device_ids=true | all-gather | bytes 786432 | tf_op jit(solution)/shard_map/all_gather | solution.py:225
  28.8 0.4 shard_map.72
  29.3 1.9 %collective-permute-start.1 = (f32[2,512,128]{2,1,0:T(8,128)S(1)}, f32[2,512,128]{2,1,0:T(8,128)S(1)}, u32[]{:S(2)}, u32[]{:S(2)}) collective-permute-start(f32[2,512,128]{2,1,0:T(8,128)S(1)} %get-tuple-element.38.sent), channel_id=1, source_target_pairs={{0,511},{1,2},{2,1},{3,4},{4,3},{5,6},{6,5},{7,8},{8,7},{9,10},{10... | collective-permute-start | bytes 1572872 | tf_op jit(solution)/shard_map/ppermute | solution.py:231
  31.2 6.3 %collective-permute-start.3 = (f32[4,512,128]{2,1,0:T(8,128)S(1)}, f32[4,512,128]{2,1,0:T(8,128)S(1)}, u32[]{:S(2)}, u32[]{:S(2)}) collective-permute-start(f32[4,512,128]{2,1,0:T(8,128)S(1)} %get-tuple-element.39), channel_id=1, source_target_pairs={{0,1},{1,0},{2,3},{3,2},{4,5},{5,4},{6,7},{7,6},{8,9},{9,8},{10,11... | collective-permute-start | bytes 3145736 | tf_op jit(solution)/shard_map/ppermute | solution.py:228
  37.6 1.9 %collective-permute-start.5 = (f32[4,512,128]{2,1,0:T(8,128)S(1)}, f32[4,512,128]{2,1,0:T(8,128)S(1)}, u32[]{:S(2)}, u32[]{:S(2)}) collective-permute-start(f32[4,512,128]{2,1,0:T(8,128)S(1)} %get-tuple-element.46), channel_id=1, source_target_pairs={{0,511},{1,2},{2,1},{3,4},{4,3},{5,6},{6,5},{7,8},{8,7},{9,10},{10... | collective-permute-start | bytes 3145736 | tf_op jit(solution)/shard_map/ppermute | solution.py:231
  39.5 0.6 collective-permute-done.1.got
  40.1 0.7 shard_map.73.sent.pair
  40.8 7.4 %collective-permute-start.2 = (f32[2,512,128]{2,1,0:T(8,128)S(1)}, f32[2,512,128]{2,1,0:T(8,128)S(1)}, u32[]{:S(2)}, u32[]{:S(2)}) collective-permute-start(f32[2,512,128]{2,1,0:T(8,128)S(1)} %shard_map.73.sent.pair), channel_id=1, source_target_pairs={{0,1},{1,0},{2,3},{3,2},{4,5},{5,4},{6,7},{7,6},{8,9},{9,8},{10,11... | collective-permute-start | bytes 1572872 | tf_op jit(solution)/shard_map/ppermute | solution.py:228
  48.2 0.0 collective-permute-done.3.near_j
  48.2 1.3 %shard_map.74 = (bf16[512,512]{1,0:T(8,128)(2,1)S(1)}, bf16[512,512]{1,0:T(8,128)(2,1)S(1)}) custom-call(f32[4,512,128]{2,1,0:T(8,128)S(1)} %collective-permute-done.3.near_j, bf16[512,512]{1,0:T(8,128)(2,1)S(1)} %get-tuple-element.32.j0, bf16[512,512]{1,0:T(8,128)(2,1)S(1)} %get-tuple-element.33.j1), custom_call_target="tpu_custom_call" | custom-call | flops 268435456 | bytes 1048576 | tf_op jit(solution)/shard_map/pallas_call | solution.py:205
  49.6 0.4 shard_map.75.effect
  50.0 0.0 collective-permute-done.2.near
  50.0 1.4 %shard_map.76 = (f32[2,512,128]{2,1,0:T(8,128)S(1)}, f32[512,128]{1,0:T(8,128)S(1)}) custom-call(f32[2,512,128]{2,1,0:T(8,128)S(1)} %shard_map.73.sent.pair, f32[2,512,128]{2,1,0:T(8,128)S(1)} %collective-permute-done.2.near, f32[512,128]{1,0:T(8,128)S(1)} %shard_map.75.effect, f32[512,128]{1,0:T(8,128)S(1)} %get-tuple-element.42.r, ...), custom_call_target="tpu_custom_call" | custom-call | flops 268435456 | bytes 1048576 | tf_op jit(solution)/shard_map/pallas_call | solution.py:205
  51.5 1.9 %collective-permute-start.4 = (f32[2,512,128]{2,1,0:T(8,128)S(1)}, f32[2,512,128]{2,1,0:T(8,128)S(1)}, u32[]{:S(2)}, u32[]{:S(2)}) collective-permute-start(f32[2,512,128]{2,1,0:T(8,128)S(1)} %get-tuple-element.45.sent.first), channel_id=1, source_target_pairs={{0,511},{1,2},{2,1},{3,4},{4,3},{5,6},{6,5},{7,8},{8,7},{9,10},{10... | collective-permute-start | bytes 1572872 | tf_op jit(solution)/shard_map/ppermute | solution.py:231
  53.4 0.6 collective-permute-done.5.k_in
  54.0 0.2 shard_map.77
  54.2 0.4 shard_map.78.effect
  54.6 7.6 %collective-permute-done.4.got = f32[2,512,128]{2,1,0:T(8,128)S(1)} collective-permute-done((f32[2,512,128]{2,1,0:T(8,128)S(1)}, f32[2,512,128]{2,1,0:T(8,128)S(1)}, u32[]{:S(2)}, u32[]{:S(2)}) %collective-permute-start.4) | collective-permute-done | bytes 524320 | tf_op jit(solution)/shard_map/ppermute | solution.py:231
  62.3 0.7 shard_map.79.sent.pair
  63.0 7.2 %collective-permute-start.6 = (f32[2,512,128]{2,1,0:T(8,128)S(1)}, f32[2,512,128]{2,1,0:T(8,128)S(1)}, u32[]{:S(2)}, u32[]{:S(2)}) collective-permute-start(f32[2,512,128]{2,1,0:T(8,128)S(1)} %shard_map.79.sent.pair), channel_id=1, source_target_pairs={{0,1},{1,0},{2,3},{3,2},{4,5},{5,4},{6,7},{7,6},{8,9},{9,8},{10,11... | collective-permute-start | bytes 1572872 | tf_op jit(solution)/shard_map/ppermute | solution.py:228
  70.1 0.4 shard_map.80.effect
  70.6 1.1 %collective-permute-done.6.near = f32[2,512,128]{2,1,0:T(8,128)S(1)} collective-permute-done((f32[2,512,128]{2,1,0:T(8,128)S(1)}, f32[2,512,128]{2,1,0:T(8,128)S(1)}, u32[]{:S(2)}, u32[]{:S(2)}) %collective-permute-start.6) | collective-permute-done | bytes 524320 | tf_op jit(solution)/shard_map/ppermute | solution.py:228
  71.7 0.7 shard_map.81._.sent
  72.4 1.9 %collective-permute-start.7 = (f32[2,512,128]{2,1,0:T(8,128)S(1)}, f32[2,512,128]{2,1,0:T(8,128)S(1)}, u32[]{:S(2)}, u32[]{:S(2)}) collective-permute-start(f32[2,512,128]{2,1,0:T(8,128)S(1)} %shard_map.81._.sent), channel_id=1, source_target_pairs={{0,511},{1,2},{2,1},{3,4},{4,3},{5,6},{6,5},{7,8},{8,7},{9,10},{10... | collective-permute-start | bytes 1572872 | tf_op jit(solution)/shard_map/ppermute | solution.py:231
  74.3 6.2 %all_gather.31.near = f32[2,512,128]{2,1,0:T(8,128)S(1)} all-gather(f32[1,512,128]{2,1,0:T(8,128)S(1)} %slice.3), channel_id=1, replica_groups={{0,1},{2,3},{4,5},{6,7},{8,9},{10,11},{12,13},{14,15},{16,17},{18,19},{..., dimensions={0}, use_global_device_ids=true | all-gather | bytes 786432 | tf_op jit(solution)/shard_map/all_gather | solution.py:225
  80.6 0.4 shard_map.82.rest
  81.0 0.4 shard_map.83._.r_before
  81.5 1.7 %collective-permute-done.7.got = f32[2,512,128]{2,1,0:T(8,128)S(1)} collective-permute-done((f32[2,512,128]{2,1,0:T(8,128)S(1)}, f32[2,512,128]{2,1,0:T(8,128)S(1)}, u32[]{:S(2)}, u32[]{:S(2)}) %collective-permute-start.7) | collective-permute-done | bytes 524320 | tf_op jit(solution)/shard_map/ppermute | solution.py:231
  83.2 0.7 shard_map.84
  83.9 7.3 %all-gather.2 = f32[1024,128]{1,0:T(8,128)S(1)} all-gather(f32[512,128]{1,0:T(8,128)S(1)} %get-tuple-element.55), channel_id=4, replica_groups={{0,1},{2,3},{4,5},{6,7},{8,9},{10,11},{12,13},{14,15},{16,17},{18,19},{..., dimensions={0}, use_global_device_ids=true | all-gather | bytes 786432 | tf_op jit(solution)/shard_map/all_gather | solution.py:225
  91.2 0.4 shard_map.85.d
  91.7 1.9 %collective-permute-start.8 = (f32[512,128]{1,0:T(8,128)S(1)}, f32[512,128]{1,0:T(8,128)S(1)}, u32[]{:S(2)}, u32[]{:S(2)}) collective-permute-start(f32[512,128]{1,0:T(8,128)S(1)} %shard_map.85.d), channel_id=1, source_target_pairs={{0,511},{1,2},{2,1},{3,4},{4,3},{5,6},{6,5},{7,8},{8,7},{9,10},{10... | collective-permute-start | bytes 786440 | tf_op jit(solution)/shard_map/ppermute | solution.py:231
  93.6 6.2 %all-gather.3 = f32[1024,128]{1,0:T(8,128)S(1)} all-gather(f32[512,128]{1,0:T(8,128)S(1)} %shard_map.85.d), channel_id=5, replica_groups={{0,1},{2,3},{4,5},{6,7},{8,9},{10,11},{12,13},{14,15},{16,17},{18,19},{..., dimensions={0}, use_global_device_ids=true | all-gather | bytes 786432 | tf_op jit(solution)/shard_map/all_gather | solution.py:225
  99.8 0.0 collective-permute-done.8.got
  99.8 1.7 %shard_map.86 = (f32[1,512,128]{2,1,0:T(8,128)}, f32[1,512,128]{2,1,0:T(8,128)}) custom-call(s32[1]{0:T(128)} %bitcast.odd, f32[2,512,128]{2,1,0:T(8,128)S(1)} %bitcast.11, f32[512,128]{1,0:T(8,128)S(1)} %shard_map.83._.r_before, f32[512,128]{1,0:T(8,128)S(1)} %collective-permute-done.8.got, f32[2,512,128]{2,1,0:T(8,128)S(1)} %get-tuple-element.45.sent.first, ...), custom_call_target="tpu_custom_call" | custom-call | flops 268435456 | bytes 1048576 | tf_op jit(solution)/shard_map/pallas_call | solution.py:205
  (1 shorter events, 0.0 us)
Async XLA Ops:
  2.4 23.6 %collective-permute-start = (f32[512,128]{1,0:T(8,128)S(1)}, f32[512,128]{1,0:T(8,128)S(1)}, u32[]{:S(2)}, u32[]{:S(2)}) collective-permute-start(f32[512,128]{1,0:T(8,128)S(1)} %get-tuple-element.29._.w), channel_id=1, source_target_pairs={{0,511},{1,2},{2,1},{3,4},{4,3},{5,6},{6,5},{7,8},{8,7},{9,10},{10... | collective-permute-start | bytes 786440 | tf_op jit(solution)/shard_map/ppermute | solution.py:231
  29.3 10.8 %collective-permute-start.1 = (f32[2,512,128]{2,1,0:T(8,128)S(1)}, f32[2,512,128]{2,1,0:T(8,128)S(1)}, u32[]{:S(2)}, u32[]{:S(2)}) collective-permute-start(f32[2,512,128]{2,1,0:T(8,128)S(1)} %get-tuple-element.38.sent), channel_id=1, source_target_pairs={{0,511},{1,2},{2,1},{3,4},{4,3},{5,6},{6,5},{7,8},{8,7},{9,10},{10... | collective-permute-start | bytes 1572872 | tf_op jit(solution)/shard_map/ppermute | solution.py:231
  31.2 17.0 %collective-permute-start.3 = (f32[4,512,128]{2,1,0:T(8,128)S(1)}, f32[4,512,128]{2,1,0:T(8,128)S(1)}, u32[]{:S(2)}, u32[]{:S(2)}) collective-permute-start(f32[4,512,128]{2,1,0:T(8,128)S(1)} %get-tuple-element.39), channel_id=1, source_target_pairs={{0,1},{1,0},{2,3},{3,2},{4,5},{5,4},{6,7},{7,6},{8,9},{9,8},{10,11... | collective-permute-start | bytes 3145736 | tf_op jit(solution)/shard_map/ppermute | solution.py:228
  37.6 16.4 %collective-permute-start.5 = (f32[4,512,128]{2,1,0:T(8,128)S(1)}, f32[4,512,128]{2,1,0:T(8,128)S(1)}, u32[]{:S(2)}, u32[]{:S(2)}) collective-permute-start(f32[4,512,128]{2,1,0:T(8,128)S(1)} %get-tuple-element.46), channel_id=1, source_target_pairs={{0,511},{1,2},{2,1},{3,4},{4,3},{5,6},{6,5},{7,8},{8,7},{9,10},{10... | collective-permute-start | bytes 3145736 | tf_op jit(solution)/shard_map/ppermute | solution.py:231
  40.8 9.2 %collective-permute-start.2 = (f32[2,512,128]{2,1,0:T(8,128)S(1)}, f32[2,512,128]{2,1,0:T(8,128)S(1)}, u32[]{:S(2)}, u32[]{:S(2)}) collective-permute-start(f32[2,512,128]{2,1,0:T(8,128)S(1)} %shard_map.73.sent.pair), channel_id=1, source_target_pairs={{0,1},{1,0},{2,3},{3,2},{4,5},{5,4},{6,7},{7,6},{8,9},{9,8},{10,11... | collective-permute-start | bytes 1572872 | tf_op jit(solution)/shard_map/ppermute | solution.py:228
  51.5 10.8 %collective-permute-start.4 = (f32[2,512,128]{2,1,0:T(8,128)S(1)}, f32[2,512,128]{2,1,0:T(8,128)S(1)}, u32[]{:S(2)}, u32[]{:S(2)}) collective-permute-start(f32[2,512,128]{2,1,0:T(8,128)S(1)} %get-tuple-element.45.sent.first), channel_id=1, source_target_pairs={{0,511},{1,2},{2,1},{3,4},{4,3},{5,6},{6,5},{7,8},{8,7},{9,10},{10... | collective-permute-start | bytes 1572872 | tf_op jit(solution)/shard_map/ppermute | solution.py:231
  63.0 8.7 %collective-permute-start.6 = (f32[2,512,128]{2,1,0:T(8,128)S(1)}, f32[2,512,128]{2,1,0:T(8,128)S(1)}, u32[]{:S(2)}, u32[]{:S(2)}) collective-permute-start(f32[2,512,128]{2,1,0:T(8,128)S(1)} %shard_map.79.sent.pair), channel_id=1, source_target_pairs={{0,1},{1,0},{2,3},{3,2},{4,5},{5,4},{6,7},{7,6},{8,9},{9,8},{10,11... | collective-permute-start | bytes 1572872 | tf_op jit(solution)/shard_map/ppermute | solution.py:228
  72.4 10.8 %collective-permute-start.7 = (f32[2,512,128]{2,1,0:T(8,128)S(1)}, f32[2,512,128]{2,1,0:T(8,128)S(1)}, u32[]{:S(2)}, u32[]{:S(2)}) collective-permute-start(f32[2,512,128]{2,1,0:T(8,128)S(1)} %shard_map.81._.sent), channel_id=1, source_target_pairs={{0,511},{1,2},{2,1},{3,4},{4,3},{5,6},{6,5},{7,8},{8,7},{9,10},{10... | collective-permute-start | bytes 1572872 | tf_op jit(solution)/shard_map/ppermute | solution.py:231
  91.7 8.1 %collective-permute-start.8 = (f32[512,128]{1,0:T(8,128)S(1)}, f32[512,128]{1,0:T(8,128)S(1)}, u32[]{:S(2)}, u32[]{:S(2)}) collective-permute-start(f32[512,128]{1,0:T(8,128)S(1)} %shard_map.85.d), channel_id=1, source_target_pairs={{0,511},{1,2},{2,1},{3,4},{4,3},{5,6},{6,5},{7,8},{8,7},{9,10},{10... | collective-permute-start | bytes 786440 | tf_op jit(solution)/shard_map/ppermute | solution.py:231
